TPU v7x, 32 devices: a whole 2x2x4 slice. The times are simulated.
32 devices in a mesh: groups: 2 (over x), row: 16 (over z, y, core).
Axes of the slice: x: 2, y: 2, z: 4, core: 2. Of those that a mesh axis runs over, the one named last changes fastest.
Arguments:
- walkers: bfloat16 [512, 256, 64], P(('groups', 'row')), parts along dimension 0, may hold values from -6 to 6
- inv_intersection: bfloat16 [512, 64, 64], P(('groups', 'row')), parts along dimension 0, may hold values from -0.75 to 0.75
- copies: int32 [512], P(('groups', 'row')), parts along dimension 0, may hold values from 0 to 3, as said below
- deal: int32 [32], P('groups'), parts along dimension 0, may hold values from 0 to 15, each once
- trial: bfloat16 [512, 64], P('groups'), parts along dimension 0, may hold values from -6 to 6
- chol: bfloat16 [8192, 256, 256], P('groups', 'row'), parts along dimension 0, may hold values from -0.15625 to 0.15625
- noise: float32 [512, 4096], P(('groups', 'row')), parts along dimension 0, may hold values from -6 to 6
Outputs:
- propagated: bfloat16 [512, 256, 64], P(('groups', 'row')), parts along dimension 0
- force_bias: float32 [512, 4096], P(('groups', 'row')), parts along dimension 0
There are 2 independent parts, one for each index of `groups`. A program takes and returns all parts, laid end to end along the dimension named above; each array names one. Nothing has to cross between parts.
Inputs may be any that keep to these rules, and one draw needn't show every extreme that they name: The copy counts sum to 256; the walkers of one device have at most 32 copies together, and some device reaches that.
All inputs are finite; a program needn't handle non-finite values.
Results may differ from a plain program's by a relative error of at most 0.023.
Values may be sent and summed in bfloat16 or wider, within the bound.
No kernel may reach another device: no remote copies, remote signals or barrier semaphores. Data moves between devices by JAX's collectives and lax.ppermute only.
A program may use at most 128 MiB of HBM per device.

v0:
```python
import jax
import jax.numpy as jnp
from jax import lax
from jax.sharding import PartitionSpec as P

root_step = 0.1


def local(walkers, inv_intersection, copies, deal, trial, chol, noise):
    devices = lax.axis_size("row")
    own_index = lax.axis_index("row")
    per_device = walkers.shape[0]
    everyone = lax.all_gather(copies, "row", axis=0, tiled=True)
    copy_ends = jnp.cumsum(everyone)
    copy_starts = copy_ends - everyone
    residue = jnp.argsort(deal)
    slot_ids = jnp.arange(per_device, dtype=jnp.int32)
    wanted = slot_ids * devices + residue[own_index]
    parent = jnp.searchsorted(copy_ends, wanted, side="right")
    capacity = (2 * per_device + devices - 1) // devices
    own_first = copy_starts[own_index * per_device]
    own_count = jnp.sum(copies)
    own_ends = jnp.cumsum(copies)
    picks = jnp.arange(capacity, dtype=jnp.int32)[None, :]
    first_hit = own_first + jnp.mod(residue[:, None] - own_first, devices)
    positions = (first_hit + picks * devices).reshape(-1)
    usable = positions < own_first + own_count
    local_walker = jnp.searchsorted(own_ends, positions - own_first, side="right")
    local_walker = jnp.minimum(local_walker, per_device - 1)
    keep_mask = usable[:, None, None]
    send_orbital = jnp.where(keep_mask, walkers[local_walker], jnp.zeros((), walkers.dtype))
    send_inverse = jnp.where(
        keep_mask, inv_intersection[local_walker], jnp.zeros((), inv_intersection.dtype)
    )
    got_orbital, got_inverse = (
        lax.all_to_all(send_orbital, "row", split_axis=0, concat_axis=0, tiled=True),
        lax.all_to_all(send_inverse, "row", split_axis=0, concat_axis=0, tiled=True),
    )
    source = parent // per_device
    source_first = copy_starts[source * per_device]
    source_hit = source_first + jnp.mod(residue[own_index] - source_first, devices)
    received_index = source * capacity + (wanted - source_hit) // devices
    orbitals = got_orbital[received_index]
    inverse = got_inverse[received_index]
    half_rotated = jnp.einsum(
        "wmk,wkn->wmn", orbitals, inverse, preferred_element_type=jnp.float32
    ).astype(jnp.bfloat16)
    whole_density = jnp.einsum(
        "win,kn->wik", half_rotated, trial, preferred_element_type=jnp.float32
    ).astype(jnp.bfloat16)
    density = lax.all_to_all(whole_density, "row", split_axis=1, concat_axis=0, tiled=True)
    all_walkers = density.shape[0]
    own_rows = chol.shape[1]
    width = chol.shape[2]
    chol_flat = chol.reshape(chol.shape[0], own_rows * width)
    density_flat = density.reshape(all_walkers, own_rows * width)
    bias_raw = lax.psum_scatter(
        lax.dot_general(
            density_flat, chol_flat, (((1,), (1,)), ((), ())), preferred_element_type=jnp.float32
        ).astype(jnp.bfloat16),
        "row",
        scatter_dimension=0,
        tiled=True,
    ).astype(jnp.float32)
    force_bias = root_step * bias_raw
    fields = (noise + jnp.clip(force_bias, -1.0, 1.0)).astype(jnp.bfloat16)
    propagator_part = jnp.dot(
        lax.all_gather(fields, "row", axis=0, tiled=True),
        chol_flat,
        preferred_element_type=jnp.float32,
    ).astype(jnp.bfloat16)
    propagator_part = propagator_part.reshape(all_walkers, own_rows, width)
    propagator = lax.all_to_all(propagator_part, "row", split_axis=0, concat_axis=1, tiled=True)
    current = orbitals
    summed = orbitals.astype(jnp.float32)
    for degree in range(1, 5):
        product = jnp.einsum(
            "wik,wkn->win", propagator, current, preferred_element_type=jnp.float32
        )
        current = (root_step / degree * product).astype(jnp.bfloat16)
        summed = summed + current.astype(jnp.float32)
    return (summed.astype(jnp.bfloat16), force_bias)


def solution(mesh):
    in_specs = (
        P(("groups", "row"), None, None),
        P(("groups", "row"), None, None),
        P(("groups", "row")),
        P("groups"),
        P("groups", None),
        P("groups", "row", None),
        P(("groups", "row"), None),
    )
    out_specs = (P(("groups", "row"), None, None), P(("groups", "row"), None))
    return jax.shard_map(local, mesh=mesh, in_specs=in_specs, out_specs=out_specs, check_vma=False)
```

profile of v0, /device:TPU:15, one launch (start us, length us, event | category | flops | bytes accessed | tf_op | source)
XLA Modules:
  0.0 339.5 jit_solution(5975468247891966408)
XLA Ops:
  7.2 1.5 reduce_sum.9
  8.7 1.2 dynamic-slice
  10.6 0.9 dynamic-update-slice
  11.4 7.9 %all-reduce = s32[256]{0:T(256)S(1)} all-reduce(s32[256]{0:T(256)S(1)} %dynamic-update-slice), channel_id=1, replica_groups=mesh['groups'=2,'row'=16] {'row'}, use_global_device_ids=true, to_apply=%add | all-reduce | flops 256 | bytes 2048
  20.0 1.9 sort.17
  23.8 0.7 fusion.16
  24.6 0.7 copy.14
  25.5 7.9 %while.48 = (s32[]{:T(128)}, u32[32]{0:T(128)S(1)}, u32[32]{0:T(128)S(1)}, s32[16]{0:T(128)S(1)}, s32[2]{0:T(128)S(1)}, /*index=5*/s32[16]{0:T(128)S(1)}, s32[]{:T(128)}, s32[]{:T(128)}, s32[]{:T(128)}, s32[]{}) while((s32[]{:T(128)}, u32[32]{0:T(128)S(1)}, u32[32]{0:T(128)S(1)}, s32[16]{0:T(128)S(1)}, s32[2]{0:T(128)S(1)}, ...), condition=%wide.region_6.7_spmd.clone, body=%wide.region_5.6_spmd.clone.sunk | while | flops 1508 | bytes 6344 | solution.py:28
  25.5 0.7 gather_fusion
  26.2 0.7 add_subtract_fusion.2
  27.1 0.7 gather_fusion
  27.8 0.7 add_subtract_fusion.2
  28.7 0.7 gather_fusion
  29.4 0.7 add_subtract_fusion.2
  30.3 0.7 gather_fusion
  31.0 0.7 add_subtract_fusion.2
  31.8 0.7 gather_fusion
  32.5 0.7 add_subtract_fusion.2
  33.4 0.6 gather_fusion.5
  34.2 1.1 reshape.170
  35.3 8.5 %all-to-all-start.1 = ((bf16[16,2,4096]{2,1,0:T(2,128)(2,1)}), bf16[16,2,4096]{2,1,0:T(2,128)(2,1)S(1)}, u32[]{:S(2)}, u32[]{:S(2)}) async-start(bf16[16,2,4096]{2,1,0:T(2,128)(2,1)} %reshape.170), calls=%async_computation.1 | async-start | bytes 524288 | tf_op jit(solution)/shard_map/all_to_all | solution.py:37
  43.8 0.7 dynamic_slice.8
  45.1 1.1 broadcast_select_fusion.4
  46.2 5.5 %all-to-all-done.1 = bf16[16,2,4096]{2,1,0:T(2,128)(2,1)S(1)} async-done(((bf16[16,2,4096]{2,1,0:T(2,128)(2,1)}), bf16[16,2,4096]{2,1,0:T(2,128)(2,1)S(1)}, u32[]{:S(2)}, u32[]{:S(2)}) %all-to-all-start.1) | async-done | bytes 262176 | tf_op jit(solution)/shard_map/all_to_all | solution.py:37
  51.7 5.7 %all-to-all-start = ((bf16[32,256,64]{1,2,0:T(8,128)(2,1)}), bf16[32,256,64]{1,2,0:T(8,128)(2,1)S(1)}, u32[]{:S(2)}, u32[]{:S(2)}) async-start(bf16[32,256,64]{1,2,0:T(8,128)(2,1)} %broadcast_select_fusion.4), calls=%async_computation | async-start | bytes 2097152 | tf_op jit(solution)/shard_map/all_to_all | solution.py:36
  57.4 12.8 %while.49 = (s32[]{:T(128)}, u32[16]{0:T(128)S(1)}, u32[16]{0:T(128)S(1)}, s32[256]{0:T(256)S(1)}, s32[]{:T(128)}, /*index=5*/s32[]{:T(128)}, s32[]{:T(128)}, s32[]{}) while((s32[]{:T(128)}, u32[16]{0:T(128)S(1)}, u32[16]{0:T(128)S(1)}, s32[256]{0:T(256)S(1)}, s32[]{:T(128)}, /*index=5*/s32[]{:T(128)}, s32[]{:T(128)}, s32[]{}) %tuple.71), condition=%wide.region_8.9_spmd.clone, body=%wide.region_7.8_spmd.clone.sunk | while | flops 1268 | bytes 4976 | solution.py:19
  57.5 0.7 gather_fusion.1
  58.1 0.7 fusion.35
  58.9 0.7 gather_fusion.1
  59.5 0.7 fusion.35
  60.3 0.7 gather_fusion.1
  61.0 0.7 fusion.35
  61.7 0.7 gather_fusion.1
  62.4 0.7 fusion.35
  63.1 0.7 gather_fusion.1
  63.8 0.7 fusion.35
  64.5 0.7 gather_fusion.1
  65.2 0.7 fusion.35
  66.0 0.7 gather_fusion.1
  66.6 0.7 fusion.35
  67.4 0.7 gather_fusion.1
  68.0 0.7 fusion.35
  68.8 0.7 gather_fusion.1
  69.5 0.7 fusion.35
  70.2 0.7 gather_fusion.3
  70.9 0.7 compare_select_fusion.2
  72.6 9.7 %all-to-all-done = bf16[32,256,64]{1,2,0:T(8,128)(2,1)S(1)} async-done(((bf16[32,256,64]{1,2,0:T(8,128)(2,1)}), bf16[32,256,64]{1,2,0:T(8,128)(2,1)S(1)}, u32[]{:S(2)}, u32[]{:S(2)}) %all-to-all-start) | async-done | bytes 1048608 | tf_op jit(solution)/shard_map/all_to_all | solution.py:36
  82.9 1.0 convolution_convert_fusion.2
  83.9 2.5 copy.16
  86.4 4.9 %all-to-all-start.2 = ((bf16[16,256,256]{2,0,1:T(8,128)(2,1)}), bf16[16,256,256]{2,0,1:T(8,128)(2,1)S(1)}, u32[]{:S(2)}, u32[]{:S(2)}) async-start(bf16[16,256,256]{2,0,1:T(8,128)(2,1)} %copy.16), calls=%async_computation.2 | async-start | bytes 4194304 | tf_op jit(solution)/shard_map/all_to_all | solution.py:51
  91.4 22.6 %copy.21 = bf16[512,8,16,256]{3,1,2,0:T(8,128)(2,1)} copy(bf16[512,8,16,256]{3,2,1,0:T(8,128)(2,1)} %bitcast.42) | data formatting | bytes 67108864
  114.0 24.8 %all-to-all-done.2 = bf16[16,256,256]{2,0,1:T(8,128)(2,1)S(1)} async-done(((bf16[16,256,256]{2,0,1:T(8,128)(2,1)}), bf16[16,256,256]{2,0,1:T(8,128)(2,1)S(1)}, u32[]{:S(2)}, u32[]{:S(2)}) %all-to-all-start.2) | async-done | bytes 2097184 | tf_op jit(solution)/shard_map/all_to_all | solution.py:51
  138.7 0.9 copy.17
  139.7 1.0 copy.20
  140.6 15.7 %convolution_convert_fusion.1 = bf16[256,4096]{1,0:T(8,128)(2,1)} fusion(bf16[256,4096]{1,0:T(8,128)(2,1)S(1)} %bitcast.50, bf16[4096,4096]{1,0:T(8,128)(2,1)} %bitcast.43), kind=kOutput, calls=%fused_computation.24 | convolution fusion | flops 8590983168 | bytes 37748736 | tf_op jit(solution)/shard_map/dot_general | solution.py:58
  156.6 58.9 %reduce-scatter.2.cloned.1.call-done = bf16[16,4096]{1,0:T(8,128)(2,1)} async-done(((bf16[256,4096]{1,0:T(8,128)(2,1)}), bf16[16,4096]{1,0:T(8,128)(2,1)}) %reduce-scatter.2.cloned.1.call-update) | async-done | bytes 131088 | tf_op jit(solution)/shard_map/reduce_scatter | solution.py:57
  215.6 1.7 add_convert_fusion
  217.3 42.2 %all-gather.2.cloned.1.call-done = bf16[256,4096]{1,0:T(8,128)(2,1)} async-done(((bf16[16,4096]{1,0:T(8,128)(2,1)}), bf16[256,4096]{1,0:T(8,128)(2,1)}) %all-gather.2.cloned.1.call-update) | async-done | bytes 2097168 | tf_op jit(solution)/shard_map/all_gather | solution.py:68
  259.5 15.6 %convolution_convert_fusion = bf16[256,4096]{1,0:T(8,128)(2,1)S(1)} fusion(bf16[256,4096]{1,0:T(8,128)(2,1)} %all-gather.2.cloned.1.call-done, bf16[4096,4096]{1,0:T(8,128)(2,1)} %bitcast.44), kind=kOutput, calls=%fused_computation.23 | convolution fusion | flops 8590983168 | bytes 37748736 | tf_op jit(solution)/shard_map/dot_general | solution.py:67
  275.8 52.8 %all_to_all.43 = bf16[256,16,256]{2,1,0:T(8,128)(2,1)S(1)} all-to-all(bf16[256,16,256]{2,1,0:T(8,128)(2,1)S(1)} %bitcast.47), channel_id=1, replica_groups=mesh['groups'=2,'row'=16] {'row'}, dimensions={0} | all-to-all | bytes 4194304 | tf_op jit(solution)/shard_map/all_to_all | solution.py:73
  328.8 0.8 fusion.6
  329.6 0.8 fusion.7
  330.4 0.8 fusion.8
  331.1 1.6 fusion.12
  (81 shorter events, 5.7 us)
Async XLA Ops:
  7.2 37.3 %copy-start = (bf16[16,256,64]{1,2,0:T(8,128)(2,1)S(1)}, bf16[16,256,64]{1,2,0:T(8,128)(2,1)}, u32[]{:S(2)}) copy-start(bf16[16,256,64]{1,2,0:T(8,128)(2,1)} %param.11) | copy-start | bytes 1572868
  7.2 26.2 %copy-start.2 = (bf16[16,64,64]{2,1,0:T(8,128)(2,1)S(1)}, bf16[16,64,64]{2,1,0:T(8,128)(2,1)}, u32[]{:S(2)}) copy-start(bf16[16,64,64]{2,1,0:T(8,128)(2,1)} %param.12) | copy-start | bytes 393220
  35.3 16.4 %all-to-all-start.1 = ((bf16[16,2,4096]{2,1,0:T(2,128)(2,1)}), bf16[16,2,4096]{2,1,0:T(2,128)(2,1)S(1)}, u32[]{:S(2)}, u32[]{:S(2)}) async-start(bf16[16,2,4096]{2,1,0:T(2,128)(2,1)} %reshape.170), calls=%async_computation.1 | async-start | bytes 524288 | tf_op jit(solution)/shard_map/all_to_all | solution.py:37
  51.7 30.6 %all-to-all-start = ((bf16[32,256,64]{1,2,0:T(8,128)(2,1)}), bf16[32,256,64]{1,2,0:T(8,128)(2,1)S(1)}, u32[]{:S(2)}, u32[]{:S(2)}) async-start(bf16[32,256,64]{1,2,0:T(8,128)(2,1)} %broadcast_select_fusion.4), calls=%async_computation | async-start | bytes 2097152 | tf_op jit(solution)/shard_map/all_to_all | solution.py:36
  70.2 12.7 %copy-start.4 = (bf16[256,64]{0,1:T(8,128)(2,1)S(1)}, bf16[256,64]{0,1:T(8,128)(2,1)}, u32[]{:S(2)}) copy-start(bf16[256,64]{0,1:T(8,128)(2,1)} %param.15) | copy-start | bytes 98308
  86.4 52.3 %all-to-all-start.2 = ((bf16[16,256,256]{2,0,1:T(8,128)(2,1)}), bf16[16,256,256]{2,0,1:T(8,128)(2,1)S(1)}, u32[]{:S(2)}, u32[]{:S(2)}) async-start(bf16[16,256,256]{2,0,1:T(8,128)(2,1)} %copy.16), calls=%async_computation.2 | async-start | bytes 4194304 | tf_op jit(solution)/shard_map/all_to_all | solution.py:51
  91.3 124.2 %reduce-scatter.2.cloned.1.call-start = ((), (), s32[]{:S(2)}) async-start(), calls=%async_computation.5 | async-start | bytes 2228224 | tf_op jit(solution)/shard_map/reduce_scatter | solution.py:57
  156.4 59.2 %copy-start.3 = (f32[16,4096]{1,0:T(8,128)S(1)}, f32[16,4096]{1,0:T(8,128)}, u32[]{:S(2)}) copy-start(f32[16,4096]{1,0:T(8,128)} %param.17) | copy-start | bytes 786436
  156.4 103.1 %all-gather.2.cloned.1.call-start = ((), (), s32[]{:S(2)}) async-start(), calls=%async_computation.6 | async-start | bytes 2228224 | tf_op jit(solution)/shard_map/all_gather | solution.py:68
  330.3 2.3 copy-start.1
Sparse Core Ops, SparseCore 0:
  156.5 58.9 reduce-scatter.1
  218.5 40.9 all-gather.1
where the time goes:
time: 341 us; the launch traced here: 340 us
  waiting for transfers between devices  141 us (41%)
  blocking collectives  60.7 us (18%)
  local copies, waits for them, and re-layouts  46.7 us (14%)
  matrix products  36.2 us (11%)
  starting transfers between devices  19.3 us (6%)
  other arithmetic  18.6 us (5%)
  between operations  16.3 us (5%)
    reduce_scatter x1, waiting for transfers between devices, local(): lax.psum_scatter(lax.dot_general(density_flat, chol_flat, (((1,), (1,)),...  58.9 us
    all_to_all x1, blocking collectives, local(): lax.all_to_all(propagator_part, 'row', split_axis=0, concat_axis=1, tiled...  52.8 us
    all_gather x1, waiting for transfers between devices, local(): lax.all_gather(fields, 'row', axis=0, tiled=True)  42.2 us
    unnamed x18, local copies, waits for them, and re-layouts  27.8 us
    all_to_all x1, waiting for transfers between devices, local(): lax.all_to_all(whole_density, 'row', split_axis=1, concat_axis=0, tiled=T...  24.8 us
    dot_general x1, matrix products, local(): lax.dot_general(density_flat, chol_flat, (((1,), (1,)), ((), ())), prefer...  15.7 us
    dot_general x1, matrix products, local(): jnp.dot(lax.all_gather(fields, 'row', axis=0, tiled=True), chol_flat, pre...  15.6 us
    all_to_all x1, waiting for transfers between devices, local(): lax.all_to_all(send_orbital, 'row', split_axis=0, concat_axis=0, tiled=True)  9.74 us
  transfers between devices with their start and end apart: 5, of which 5 were waited for; matrix products, arithmetic and copies ran while one was open for 12% of the time, Pallas kernels for 0%

commit v1 on v0

v1 whole, which is shorter than its diff:
```python
import jax
import jax.numpy as jnp
from jax import lax
from jax.sharding import PartitionSpec as P

root_step = 0.1
f32 = jnp.float32
bf16 = jnp.bfloat16


def chip_ring(devices):
    chips = devices // 2
    return [m for m in range(chips) if m % 2 == 0] + [m for m in reversed(range(chips)) if m % 2]


def ring_move(devices, flip, steps):
    ring = chip_ring(devices)
    chips = len(ring)
    return [
        (2 * ring[p] + b, 2 * ring[(p + steps) % chips] + (b ^ flip))
        for p in range(chips)
        for b in (0, 1)
    ]


def local(walkers, inv_intersection, copies, deal, trial, chol, noise):
    devices = lax.axis_size("row")
    me = lax.axis_index("row")
    per_device, orbitals_n, electrons = walkers.shape
    chol_n, own_rows, width = chol.shape
    everyone = devices * per_device
    chips = devices // 2
    ring = chip_ring(devices)
    place = [ring.index(m) for m in range(chips)]

    theta = jnp.einsum(
        "wmk,wkn->wmn", walkers, inv_intersection, preferred_element_type=f32
    ).astype(bf16)

    def by_owner(a):
        a = a.reshape(per_device, devices, own_rows * electrons)
        return jnp.transpose(a, (1, 0, 2))

    counts = jnp.broadcast_to(copies.astype(bf16)[None, :, None], (devices, per_device, 128))
    first = lax.all_to_all(
        jnp.concatenate([by_owner(theta), counts], axis=2), "row", 0, 0, tiled=True
    ).reshape(everyone, own_rows * electrons + 128)
    theta_rows = first[:, : own_rows * electrons]
    count_column = first[:, own_rows * electrons :][:, :1].astype(f32)
    walker_rows = lax.all_to_all(by_owner(walkers), "row", 0, 0, tiled=True).reshape(
        everyone, own_rows * electrons
    )

    ids = jnp.arange(everyone, dtype=jnp.int32)
    before = (ids[:, None] <= ids[None, :]).astype(f32)
    ends = jnp.sum(before * count_column, axis=0)
    before_own = (ids[:, None] < ids[None, :]).astype(f32)
    starts = jnp.sum(before_own * count_column, axis=0)
    residues = jnp.arange(devices, dtype=jnp.int32)

    def parents_of(owner, slot):
        residue = jnp.sum(
            jnp.where(deal[None, :] == owner[:, None], residues[None, :], 0), axis=1
        )
        position = (slot * devices + residue).astype(f32)[:, None]
        return ((position >= starts[None, :]) & (position < ends[None, :])).astype(bf16)

    chip, core = me // 2, me % 2
    ring_ids = jnp.array(ring, jnp.int32)
    own_place = jnp.sum(jnp.where(residues[:chips] == chip, jnp.array(place, jnp.int32), 0))
    slot = ids % per_device
    step = (ids // per_device) % chips
    flip = ids // (per_device * chips)
    spot = (own_place + step) % chips
    to_chip = jnp.sum(
        jnp.where(spot[:, None] == residues[None, :chips], ring_ids[None, :], 0), axis=1
    )
    owner = 2 * to_chip + (core ^ flip)
    picked = jnp.dot(parents_of(owner, slot), theta_rows, preferred_element_type=f32).astype(bf16)
    density = jnp.einsum(
        "win,jn->wij",
        picked.reshape(everyone, own_rows, electrons),
        trial,
        preferred_element_type=f32,
    ).astype(bf16)

    new_rows = jnp.dot(
        parents_of(ids // per_device, slot), walker_rows, preferred_element_type=f32
    ).astype(bf16)
    got_rows = lax.all_to_all(
        new_rows.reshape(devices, per_device, own_rows * electrons), "row", 0, 0, tiled=True
    )
    orbitals = jnp.transpose(
        got_rows.reshape(devices, per_device, own_rows, electrons), (1, 0, 2, 3)
    ).reshape(per_device, orbitals_n, electrons)

    chol_flat = chol.reshape(chol_n, own_rows * width)
    part = lax.dot_general(
        density.reshape(everyone, own_rows * width),
        chol_flat,
        (((1,), (1,)), ((), ())),
        preferred_element_type=f32,
    ).astype(bf16)
    part = part.reshape(2, chips, per_device, chol_n)

    swap = ring_move(devices, 1, 0)
    right = ring_move(devices, 0, 1)
    left = ring_move(devices, 0, -1)
    swapped = lax.ppermute(part[1], "row", swap)

    def own_term(k):
        return part[0, k % chips].astype(f32) + swapped[k % chips].astype(f32)

    to_right, to_left = chips // 2, chips - 1 - chips // 2
    moving_right = own_term(to_right).astype(bf16)
    moving_left = own_term(-to_left).astype(bf16)
    for t in range(to_right):
        moving_right = lax.ppermute(moving_right, "row", right)
        if t < to_left:
            moving_left = lax.ppermute(moving_left, "row", left)
        if t < to_right - 1:
            moving_right = (moving_right.astype(f32) + own_term(to_right - 1 - t)).astype(bf16)
        if t < to_left - 1:
            moving_left = (moving_left.astype(f32) + own_term(-(to_left - 1 - t))).astype(bf16)
    bias_raw = own_term(0) + moving_right.astype(f32)
    if to_left:
        bias_raw = bias_raw + moving_left.astype(f32)
    force_bias = root_step * bias_raw
    fields = (noise + jnp.clip(force_bias, -1.0, 1.0)).astype(bf16)

    pieces, offsets = [fields], [0]
    going_right = going_left = fields
    for t in range(to_right):
        going_right = lax.ppermute(going_right, "row", right)
        pieces.append(going_right)
        offsets.append(-(t + 1))
        if t < to_left:
            going_left = lax.ppermute(going_left, "row", left)
            pieces.append(going_left)
            offsets.append(t + 1)
    own_core = jnp.stack(pieces)
    other_core = lax.ppermute(own_core, "row", swap)
    all_fields = jnp.zeros((devices, per_device, chol_n), bf16)
    for held, side in ((own_core, core), (other_core, 1 - core)):
        for n, offset in enumerate(offsets):
            spot = (own_place + offset) % chips
            to = 2 * jnp.sum(jnp.where(residues[:chips] == spot, ring_ids, 0)) + side
            all_fields = lax.dynamic_update_index_in_dim(all_fields, held[n], to, 0)
    propagator_part = jnp.dot(
        all_fields.reshape(everyone, chol_n), chol_flat, preferred_element_type=f32
    ).astype(bf16)
    propagator = lax.all_to_all(
        propagator_part.reshape(everyone, own_rows, width),
        "row",
        split_axis=0,
        concat_axis=1,
        tiled=True,
    )
    current = orbitals
    summed = orbitals.astype(f32)
    for degree in range(1, 5):
        product = jnp.einsum("wik,wkn->win", propagator, current, preferred_element_type=f32)
        current = (root_step / degree * product).astype(bf16)
        summed = summed + current.astype(f32)
    return (summed.astype(bf16), force_bias)


def solution(mesh):
    in_specs = (
        P(("groups", "row"), None, None),
        P(("groups", "row"), None, None),
        P(("groups", "row")),
        P("groups"),
        P("groups", None),
        P("groups", "row", None),
        P(("groups", "row"), None),
    )
    out_specs = (P(("groups", "row"), None, None), P(("groups", "row"), None))
    return jax.shard_map(local, mesh=mesh, in_specs=in_specs, out_specs=out_specs, check_vma=False)
```

time: 341 us -> 246 us (0.72)
  waiting for transfers between devices: 141 us -> 77.6 us
  blocking collectives: 60.7 us -> 0 us
  matrix products: 36.2 us -> 60.4 us
  starting transfers between devices: 19.3 us -> 42.4 us
  other arithmetic: 18.6 us -> 4.66 us
  between operations: 16.3 us -> 12.6 us
    reduce_scatter x1 -> x0, waiting for transfers between devices: 58.9 us -> none  [local(): lax.psum_scatter(lax.dot_general(density_flat, chol_flat, (((1,), (1,)),...]
    all_to_all x1 -> x0, blocking collectives: 52.8 us -> none  [local(): lax.all_to_all(propagator_part, 'row', split_axis=0, concat_axis=1, tiled...]
    all_gather x1 -> x0, waiting for transfers between devices: 42.2 us -> none  [local(): lax.all_gather(fields, 'row', axis=0, tiled=True)]
    dot_general x7 -> x9, matrix products: 36.2 us -> 60.4 us  [the longest x1 38.3 us: local(): lax.dot_general(density.reshape(everyone, own_rows * width), chol_flat, (...]
    ppermute x0 -> x16, waiting for transfers between devices: none -> 20.6 us  [the longest x4 9.42 us: local(): moving_right = lax.ppermute(moving_right, 'row', right)]
    all_to_all x3 -> x4, waiting for transfers between devices: 40.1 us -> 57 us  [the longest x1 43.4 us: local(): lax.all_to_all(propagator_part.reshape(everyone, own_rows, width), 'row',...]
    ppermute x0 -> x16, starting transfers between devices: none -> 14.5 us  [the longest x1 4.64 us: local(): other_core = lax.ppermute(own_core, 'row', swap)]
    gather x19 -> x0, local copies, waits for them, and re-layouts: 12.6 us -> none  [the longest x9 5.98 us: local(): parent = jnp.searchsorted(copy_ends, wanted, side='right')]
  transfers between devices with their start and end apart: 5 -> 20, of which waited for: 5 -> 13; matrix products, arithmetic and copies ran while one was open for 12% -> 26% of each run, Pallas kernels for 0% -> 0%
where the time goes in v1:
time: 246 us; the launch traced here: 245 us
  waiting for transfers between devices  77.6 us (32%)
  matrix products  60.4 us (25%)
  local copies, waits for them, and re-layouts  47 us (19%)
  starting transfers between devices  42.4 us (17%)
  between operations  12.6 us (5%)
  other arithmetic  4.66 us (2%)
    all_to_all x1, waiting for transfers between devices, local(): lax.all_to_all(propagator_part.reshape(everyone, own_rows, width), 'row',...  43.4 us
    dot_general x1, matrix products, local(): lax.dot_general(density.reshape(everyone, own_rows * width), chol_flat, (...  38.3 us
    unnamed x33, local copies, waits for them, and re-layouts  30.3 us
    dot_general x1, matrix products, local(): jnp.dot(all_fields.reshape(everyone, chol_n), chol_flat, preferred_elemen...  15.3 us
    all_to_all x1, waiting for transfers between devices, local(): lax.all_to_all(jnp.concatenate([by_owner(theta), counts], axis=2), 'row',...  13.5 us
    all_to_all x1, starting transfers between devices, local(): lax.all_to_all(by_owner(walkers), 'row', 0, 0, tiled=True)  9.56 us
    ppermute x4, waiting for transfers between devices, local(): moving_right = lax.ppermute(moving_right, 'row', right)  9.42 us
    dynamic_update_slice x9, local copies, waits for them, and re-layouts, local(): all_fields = lax.dynamic_update_index_in_dim(all_fields, held[n], to, 0)  7.38 us
  transfers between devices with their start and end apart: 20, of which 13 were waited for; matrix products, arithmetic and copies ran while one was open for 26% of the time, Pallas kernels for 0%

profile of v1, /device:TPU:15, one launch (start us, length us, event | category | flops | bytes accessed | tf_op | source)
XLA Modules:
  0.0 244.7 jit_solution(11815817821980627699)
XLA Ops:
  0.7 0.9 copy-done
  1.6 1.4 convolution_convert_fusion.1
  3.0 0.5 copy.38
  3.5 0.7 reshape.155
  4.4 0.9 copy.39
  5.3 6.6 %all-to-all-start = ((bf16[16,16,1152]{2,1,0:T(8,128)(2,1)}), bf16[16,16,1152]{2,1,0:T(8,128)(2,1)S(1)}, u32[]{:S(2)}, u32[]{:S(2)}) async-start(bf16[16,16,1152]{2,1,0:T(8,128)(2,1)} %copy.39), calls=%async_computation | async-start | bytes 1179648 | tf_op jit(solution)/shard_map/all_to_all | solution.py:45
  11.9 0.6 fusion.66
  12.5 0.7 and_select_fusion.1
  13.4 13.5 %all-to-all-done = bf16[16,16,1152]{2,1,0:T(8,128)(2,1)S(1)} async-done(((bf16[16,16,1152]{2,1,0:T(8,128)(2,1)}), bf16[16,16,1152]{2,1,0:T(8,128)(2,1)S(1)}, u32[]{:S(2)}, u32[]{:S(2)}) %all-to-all-start) | async-done | bytes 589856 | tf_op jit(solution)/shard_map/all_to_all | solution.py:45
  27.1 0.3 convolution_convert_fusion.2
  27.7 38.3 %fusion.5 = bf16[256,4096]{1,0:T(8,128)(2,1)S(1)} fusion(bf16[4096,16,256]{2,1,0:T(8,128)(2,1)} %param.14, bf16[256,16,64]{0,2,1:T(8,128)(2,1)S(1)} %bitcast.172, bf16[256,64]{0,1:T(8,128)(2,1)S(1)} %copy-done.10), kind=kOutput, calls=%fused_computation.4 | convolution fusion | flops 8726249472 | bytes 36208640 | tf_op jit(solution)/shard_map/dot_general | solution.py:98
  66.4 2.4 %collective-permute-done = bf16[8,16,4096]{2,1,0:T(8,128)(2,1)S(1)} collective-permute-done((bf16[8,16,4096]{2,1,0:T(8,128)(2,1)S(1)}, bf16[8,16,4096]{2,1,0:T(8,128)(2,1)S(1)}, u32[]{:S(2)}, u32[]{:S(2)}) %collective-permute-start) | collective-permute-done | bytes 1048608 | tf_op jit(solution)/shard_map/ppermute | solution.py:109
  69.0 4.8 %collective-permute-done.1 = bf16[16,4096]{1,0:T(8,128)(2,1)S(1)} collective-permute-done((bf16[16,4096]{1,0:T(8,128)(2,1)S(1)}, bf16[16,4096]{1,0:T(8,128)(2,1)S(1)}, u32[]{:S(2)}, u32[]{:S(2)}) %collective-permute-start.1) | collective-permute-done | bytes 131104 | tf_op jit(solution)/shard_map/ppermute | solution.py:118
  74.1 1.3 collective-permute-start.5
  75.5 2.4 collective-permute-done.2
  77.8 0.4 collective-permute-done.5
  78.4 0.7 collective-permute-start.3
  79.1 0.9 collective-permute-start.6
  80.0 2.2 collective-permute-done.3
  82.2 0.7 collective-permute-done.6
  83.0 1.6 collective-permute-start.4
  84.7 0.5 copy.40
  85.2 0.7 reshape.157
  85.9 1.1 copy.41
  87.0 9.6 %all-to-all-start.1 = ((bf16[16,16,1024]{2,1,0:T(8,128)(2,1)}), bf16[16,16,1024]{2,1,0:T(8,128)(2,1)S(1)}, u32[]{:S(2)}, u32[]{:S(2)}) async-start(bf16[16,16,1024]{2,1,0:T(8,128)(2,1)} %copy.41), calls=%async_computation.1 | async-start | bytes 1048576 | tf_op jit(solution)/shard_map/all_to_all | solution.py:50
  103.1 0.8 fusion.64
  108.9 1.8 bitcast_dynamic-update-slice_fusion.14
  110.9 1.2 collective-permute-start.9
  112.4 3.0 %collective-permute-done.8 = bf16[16,4096]{1,0:T(8,128)(2,1)S(1)} collective-permute-done((bf16[16,4096]{1,0:T(8,128)(2,1)S(1)}, bf16[16,4096]{1,0:T(8,128)(2,1)S(1)}, u32[]{:S(2)}, u32[]{:S(2)}) %collective-permute-start.8) | collective-permute-done | bytes 131104 | tf_op jit(solution)/shard_map/ppermute | solution.py:134
  115.7 1.2 collective-permute-start.11
  116.9 0.7 bitcast_dynamic-update-slice_fusion.12
  117.5 0.7 bitcast_dynamic-update-slice_fusion.10
  118.2 1.0 collective-permute-done.10
  119.8 1.2 collective-permute-start.13
  121.0 0.7 bitcast_dynamic-update-slice_fusion.8
  121.6 0.7 bitcast_dynamic-update-slice_fusion.6
  122.3 0.7 collective-permute-done.12
  123.3 0.7 bitcast_dynamic-update-slice_fusion.4
  124.0 0.7 bitcast_dynamic-update-slice_fusion.2
  124.6 2.6 %collective-permute-done.14 = bf16[16,4096]{1,0:T(8,128)(2,1)S(1)} collective-permute-done((bf16[16,4096]{1,0:T(8,128)(2,1)S(1)}, bf16[16,4096]{1,0:T(8,128)(2,1)S(1)}, u32[]{:S(2)}, u32[]{:S(2)}) %collective-permute-start.14) | collective-permute-done | bytes 131104 | tf_op jit(solution)/shard_map/ppermute | solution.py:134
  127.3 0.7 bitcast_dynamic-update-slice_fusion
  127.9 4.6 %collective-permute-start.15 = (bf16[8,16,4096]{2,1,0:T(8,128)(2,1)}, bf16[8,16,4096]{2,1,0:T(8,128)(2,1)}, u32[]{:S(2)}, u32[]{:S(2)}) collective-permute-start(bf16[8,16,4096]{2,1,0:T(8,128)(2,1)} %get-tuple-element.23), channel_id=1, source_target_pairs={{0,1},{1,0},{4,5},{5,4},{8,9},{9,8},{12,13},{13,12},{14,15},{15,14... | collective-permute-start | bytes 3145736 | tf_op jit(solution)/shard_map/ppermute | solution.py:142
  132.6 22.6 %copy.50 = bf16[512,8,16,256]{3,1,2,0:T(8,128)(2,1)} copy(bf16[512,8,16,256]{3,2,1,0:T(8,128)(2,1)} %bitcast.154) | data formatting | bytes 67108864
  155.2 1.1 convolution_convert_fusion.3
  156.3 5.8 %all-to-all-start.2 = ((bf16[16,16,1024]{2,1,0:T(8,128)(2,1)}), bf16[16,16,1024]{2,1,0:T(8,128)(2,1)S(1)}, u32[]{:S(2)}, u32[]{:S(2)}) async-start(bf16[16,16,1024]{2,1,0:T(8,128)(2,1)} %bitcast.4), calls=%async_computation.2 | async-start | bytes 1048576 | tf_op jit(solution)/shard_map/all_to_all | solution.py:90
  162.1 0.9 slice_dynamic-update-slice_fusion.7
  163.0 0.9 slice_dynamic-update-slice_fusion.6
  164.0 0.9 slice_dynamic-update-slice_fusion.5
  164.9 0.9 slice_dynamic-update-slice_fusion.4
  165.8 0.9 slice_dynamic-update-slice_fusion.3
  166.7 0.9 slice_dynamic-update-slice_fusion.2
  167.7 0.9 slice_dynamic-update-slice_fusion.1
  168.6 0.9 slice_dynamic-update-slice_fusion
  169.5 15.3 %convolution_convert_fusion = bf16[256,4096]{1,0:T(8,128)(2,1)S(1)} fusion(bf16[256,4096]{1,0:T(8,128)(2,1)S(1)} %bitcast.161, bf16[4096,4096]{1,0:T(8,128)(2,1)} %bitcast.155), kind=kOutput, calls=%fused_computation.3 | convolution fusion | flops 8590983168 | bytes 37748736 | tf_op jit(solution)/shard_map/dot_general | solution.py:149
  184.9 2.0 copy.51
  186.9 6.0 %all-to-all-start.3 = ((bf16[256,16,256]{2,1,0:T(8,128)(2,1)}), bf16[256,16,256]{2,1,0:T(8,128)(2,1)S(1)}, u32[]{:S(2)}, u32[]{:S(2)}) async-start(bf16[256,16,256]{2,1,0:T(8,128)(2,1)} %bitcast.62), calls=%async_computation.3 | async-start | bytes 4194304 | tf_op jit(solution)/shard_map/all_to_all | solution.py:152
  192.9 1.1 copy.42
  194.0 1.8 reshape.160
  195.7 1.1 copy.43
  196.9 43.4 %all-to-all-done.3 = bf16[256,16,256]{2,1,0:T(8,128)(2,1)S(1)} async-done(((bf16[256,16,256]{2,1,0:T(8,128)(2,1)}), bf16[256,16,256]{2,1,0:T(8,128)(2,1)S(1)}, u32[]{:S(2)}, u32[]{:S(2)}) %all-to-all-start.3) | async-done | bytes 2097184 | tf_op jit(solution)/shard_map/all_to_all | solution.py:152
  240.5 0.8 fusion.17
  241.3 0.8 fusion.11
  242.1 0.8 fusion.12
  243.1 1.6 fusion.16
  (59 shorter events, 3.9 us)
Async XLA Ops:
  0.6 1.0 copy-start
  0.6 3.5 %copy-start.11 = (s32[16]{0:T(128)S(1)}, s32[16]{0:T(128)}, u32[]{:S(2)}) copy-start(s32[16]{0:T(128)} %param.11) | copy-start | bytes 196
  4.2 7.7 %copy-start.9 = (s32[8]{0:T(128)S(1)}, s32[8]{0:T(128)}, u32[]{:S(2)}) copy-start(s32[8]{0:T(128)} %constant.207.clone) | copy-start | bytes 100
  4.2 9.0 %copy-start.7 = (s32[8]{0:T(128)S(1)}, s32[8]{0:T(128)}, u32[]{:S(2)}) copy-start(s32[8]{0:T(128)} %constant.206.clone) | copy-start | bytes 100
  4.2 9.1 %copy-start.8 = (s32[16]{0:T(128)S(1)}, s32[16]{0:T(128)}, u32[]{:S(2)}) copy-start(s32[16]{0:T(128)} %param.12) | copy-start | bytes 196
  4.4 23.3 %copy-start.10 = (bf16[256,64]{0,1:T(8,128)(2,1)S(1)}, bf16[256,64]{0,1:T(8,128)(2,1)}, u32[]{:S(2)}) copy-start(bf16[256,64]{0,1:T(8,128)(2,1)} %param.13) | copy-start | bytes 98308
  5.3 21.6 %all-to-all-start = ((bf16[16,16,1152]{2,1,0:T(8,128)(2,1)}), bf16[16,16,1152]{2,1,0:T(8,128)(2,1)S(1)}, u32[]{:S(2)}, u32[]{:S(2)}) async-start(bf16[16,16,1152]{2,1,0:T(8,128)(2,1)} %copy.39), calls=%async_computation | async-start | bytes 1179648 | tf_op jit(solution)/shard_map/all_to_all | solution.py:45
  66.0 18.6 %copy-start.4 = (bf16[256,4096]{1,0:T(8,128)(2,1)}, bf16[256,4096]{1,0:T(8,128)(2,1)S(1)}, u32[]{:S(2)}) copy-start(bf16[256,4096]{1,0:T(8,128)(2,1)S(1)} %fusion.5) | copy-start | bytes 6291460
  66.2 18.5 %copy-start.3 = (bf16[16,256,64]{1,2,0:T(8,128)(2,1)S(1)}, bf16[16,256,64]{1,2,0:T(8,128)(2,1)}, u32[]{:S(2)}) copy-start(bf16[16,256,64]{1,2,0:T(8,128)(2,1)} %param.9) | copy-start | bytes 1572868
  66.2 2.7 %collective-permute-start = (bf16[8,16,4096]{2,1,0:T(8,128)(2,1)S(1)}, bf16[8,16,4096]{2,1,0:T(8,128)(2,1)S(1)}, u32[]{:S(2)}, u32[]{:S(2)}) collective-permute-start(bf16[8,16,4096]{2,1,0:T(8,128)(2,1)S(1)} %bitcast.169), channel_id=1, source_target_pairs={{0,1},{1,0},{4,5},{5,4},{8,9},{9,8},{12,13},{13,12},{14,15},{15,14... | collective-permute-start | bytes 3145736 | tf_op jit(solution)/shard_map/ppermute | solution.py:109
  68.9 15.8 %copy-start.5 = (bf16[8,16,4096]{2,1,0:T(8,128)(2,1)}, bf16[8,16,4096]{2,1,0:T(8,128)(2,1)S(1)}, u32[]{:S(2)}) copy-start(bf16[8,16,4096]{2,1,0:T(8,128)(2,1)S(1)} %collective-permute-done) | copy-start | bytes 3145732
  68.9 4.9 %collective-permute-start.1 = (bf16[16,4096]{1,0:T(8,128)(2,1)S(1)}, bf16[16,4096]{1,0:T(8,128)(2,1)S(1)}, u32[]{:S(2)}, u32[]{:S(2)}) collective-permute-start(bf16[16,4096]{1,0:T(8,128)(2,1)S(1)} %fusion.30), channel_id=1, source_target_pairs={{0,4},{1,5},{4,8},{5,9},{8,12},{9,13},{12,14},{13,15},{14,10},{15,... | collective-permute-start | bytes 393224 | tf_op jit(solution)/shard_map/ppermute | solution.py:118
  74.0 3.9 %collective-permute-start.2 = (bf16[16,4096]{1,0:T(8,128)(2,1)S(1)}, bf16[16,4096]{1,0:T(8,128)(2,1)S(1)}, u32[]{:S(2)}, u32[]{:S(2)}) collective-permute-start(bf16[16,4096]{1,0:T(8,128)(2,1)S(1)} %get-tuple-element.21), channel_id=1, source_target_pairs={{0,4},{1,5},{4,8},{5,9},{8,12},{9,13},{12,14},{13,15},{14,10},{15,... | collective-permute-start | bytes 393224 | tf_op jit(solution)/shard_map/ppermute | solution.py:118
  74.1 4.1 %collective-permute-start.5 = (bf16[16,4096]{1,0:T(8,128)(2,1)S(1)}, bf16[16,4096]{1,0:T(8,128)(2,1)S(1)}, u32[]{:S(2)}, u32[]{:S(2)}) collective-permute-start(bf16[16,4096]{1,0:T(8,128)(2,1)S(1)} %get-tuple-element.22), channel_id=1, source_target_pairs={{0,2},{1,3},{4,0},{5,1},{8,4},{9,5},{12,8},{13,9},{14,12},{15,13},... | collective-permute-start | bytes 393224 | tf_op jit(solution)/shard_map/ppermute | solution.py:120
  78.4 3.9 %collective-permute-start.3 = (bf16[16,4096]{1,0:T(8,128)(2,1)S(1)}, bf16[16,4096]{1,0:T(8,128)(2,1)S(1)}, u32[]{:S(2)}, u32[]{:S(2)}) collective-permute-start(bf16[16,4096]{1,0:T(8,128)(2,1)S(1)} %get-tuple-element.19), channel_id=1, source_target_pairs={{0,4},{1,5},{4,8},{5,9},{8,12},{9,13},{12,14},{13,15},{14,10},{15,... | collective-permute-start | bytes 393224 | tf_op jit(solution)/shard_map/ppermute | solution.py:118
  79.1 3.8 %collective-permute-start.6 = (bf16[16,4096]{1,0:T(8,128)(2,1)S(1)}, bf16[16,4096]{1,0:T(8,128)(2,1)S(1)}, u32[]{:S(2)}, u32[]{:S(2)}) collective-permute-start(bf16[16,4096]{1,0:T(8,128)(2,1)S(1)} %get-tuple-element.20), channel_id=1, source_target_pairs={{0,2},{1,3},{4,0},{5,1},{8,4},{9,5},{12,8},{13,9},{14,12},{15,13},... | collective-permute-start | bytes 393224 | tf_op jit(solution)/shard_map/ppermute | solution.py:120
  83.0 25.8 %collective-permute-start.4 = (bf16[16,4096]{1,0:T(8,128)(2,1)S(1)}, bf16[16,4096]{1,0:T(8,128)(2,1)S(1)}, u32[]{:S(2)}, u32[]{:S(2)}) collective-permute-start(bf16[16,4096]{1,0:T(8,128)(2,1)S(1)} %get-tuple-element.17), channel_id=1, source_target_pairs={{0,4},{1,5},{4,8},{5,9},{8,12},{9,13},{12,14},{13,15},{14,10},{15,... | collective-permute-start | bytes 393224 | tf_op jit(solution)/shard_map/ppermute | solution.py:118
  84.7 24.2 %collective-permute-start.7 = (bf16[16,4096]{1,0:T(8,128)(2,1)S(1)}, bf16[16,4096]{1,0:T(8,128)(2,1)S(1)}, u32[]{:S(2)}, u32[]{:S(2)}) collective-permute-start(bf16[16,4096]{1,0:T(8,128)(2,1)S(1)} %get-tuple-element.18), channel_id=1, source_target_pairs={{0,2},{1,3},{4,0},{5,1},{8,4},{9,5},{12,8},{13,9},{14,12},{15,13},... | collective-permute-start | bytes 393224 | tf_op jit(solution)/shard_map/ppermute | solution.py:120
  85.2 23.7 %copy-start.6 = (f32[16,4096]{1,0:T(8,128)S(1)}, f32[16,4096]{1,0:T(8,128)}, u32[]{:S(2)}) copy-start(f32[16,4096]{1,0:T(8,128)} %param.15) | copy-start | bytes 786436
  87.0 68.2 %all-to-all-start.1 = ((bf16[16,16,1024]{2,1,0:T(8,128)(2,1)}), bf16[16,16,1024]{2,1,0:T(8,128)(2,1)S(1)}, u32[]{:S(2)}, u32[]{:S(2)}) async-start(bf16[16,16,1024]{2,1,0:T(8,128)(2,1)} %copy.41), calls=%async_computation.1 | async-start | bytes 1048576 | tf_op jit(solution)/shard_map/all_to_all | solution.py:50
  110.7 4.7 %collective-permute-start.8 = (bf16[16,4096]{1,0:T(8,128)(2,1)S(1)}, bf16[16,4096]{1,0:T(8,128)(2,1)S(1)}, u32[]{:S(2)}, u32[]{:S(2)}) collective-permute-start(bf16[16,4096]{1,0:T(8,128)(2,1)S(1)} %get-tuple-element.15), channel_id=1, source_target_pairs={{0,4},{1,5},{4,8},{5,9},{8,12},{9,13},{12,14},{13,15},{14,10},{15,... | collective-permute-start | bytes 393224 | tf_op jit(solution)/shard_map/ppermute | solution.py:134
  110.9 4.7 %collective-permute-start.9 = (bf16[16,4096]{1,0:T(8,128)(2,1)S(1)}, bf16[16,4096]{1,0:T(8,128)(2,1)S(1)}, u32[]{:S(2)}, u32[]{:S(2)}) collective-permute-start(bf16[16,4096]{1,0:T(8,128)(2,1)S(1)} %get-tuple-element.15), channel_id=1, source_target_pairs={{0,2},{1,3},{4,0},{5,1},{8,4},{9,5},{12,8},{13,9},{14,12},{15,13},... | collective-permute-start | bytes 393224 | tf_op jit(solution)/shard_map/ppermute | solution.py:138
  115.4 3.8 %collective-permute-start.10 = (bf16[16,4096]{1,0:T(8,128)(2,1)S(1)}, bf16[16,4096]{1,0:T(8,128)(2,1)S(1)}, u32[]{:S(2)}, u32[]{:S(2)}) collective-permute-start(bf16[16,4096]{1,0:T(8,128)(2,1)S(1)} %collective-permute-done.8), channel_id=1, source_target_pairs={{0,4},{1,5},{4,8},{5,9},{8,12},{9,13},{12,14},{13,15},{14,10},{15,... | collective-permute-start | bytes 393224 | tf_op jit(solution)/shard_map/ppermute | solution.py:134
  115.7 4.1 %collective-permute-start.11 = (bf16[16,4096]{1,0:T(8,128)(2,1)S(1)}, bf16[16,4096]{1,0:T(8,128)(2,1)S(1)}, u32[]{:S(2)}, u32[]{:S(2)}) collective-permute-start(bf16[16,4096]{1,0:T(8,128)(2,1)S(1)} %collective-permute-done.9), channel_id=1, source_target_pairs={{0,2},{1,3},{4,0},{5,1},{8,4},{9,5},{12,8},{13,9},{14,12},{15,13},... | collective-permute-start | bytes 393224 | tf_op jit(solution)/shard_map/ppermute | solution.py:138
  119.2 3.8 %collective-permute-start.12 = (bf16[16,4096]{1,0:T(8,128)(2,1)S(1)}, bf16[16,4096]{1,0:T(8,128)(2,1)S(1)}, u32[]{:S(2)}, u32[]{:S(2)}) collective-permute-start(bf16[16,4096]{1,0:T(8,128)(2,1)S(1)} %collective-permute-done.10), channel_id=1, source_target_pairs={{0,4},{1,5},{4,8},{5,9},{8,12},{9,13},{12,14},{13,15},{14,10},{15,... | collective-permute-start | bytes 393224 | tf_op jit(solution)/shard_map/ppermute | solution.py:134
  119.8 4.2 %collective-permute-start.13 = (bf16[16,4096]{1,0:T(8,128)(2,1)S(1)}, bf16[16,4096]{1,0:T(8,128)(2,1)S(1)}, u32[]{:S(2)}, u32[]{:S(2)}) collective-permute-start(bf16[16,4096]{1,0:T(8,128)(2,1)S(1)} %collective-permute-done.11), channel_id=1, source_target_pairs={{0,2},{1,3},{4,0},{5,1},{8,4},{9,5},{12,8},{13,9},{14,12},{15,13},... | collective-permute-start | bytes 393224 | tf_op jit(solution)/shard_map/ppermute | solution.py:138
  123.0 4.2 %collective-permute-start.14 = (bf16[16,4096]{1,0:T(8,128)(2,1)S(1)}, bf16[16,4096]{1,0:T(8,128)(2,1)S(1)}, u32[]{:S(2)}, u32[]{:S(2)}) collective-permute-start(bf16[16,4096]{1,0:T(8,128)(2,1)S(1)} %collective-permute-done.12), channel_id=1, source_target_pairs={{0,4},{1,5},{4,8},{5,9},{8,12},{9,13},{12,14},{13,15},{14,10},{15,... | collective-permute-start | bytes 393224 | tf_op jit(solution)/shard_map/ppermute | solution.py:134
  127.9 34.2 %collective-permute-start.15 = (bf16[8,16,4096]{2,1,0:T(8,128)(2,1)}, bf16[8,16,4096]{2,1,0:T(8,128)(2,1)}, u32[]{:S(2)}, u32[]{:S(2)}) collective-permute-start(bf16[8,16,4096]{2,1,0:T(8,128)(2,1)} %get-tuple-element.23), channel_id=1, source_target_pairs={{0,1},{1,0},{4,5},{5,4},{8,9},{9,8},{12,13},{13,12},{14,15},{15,14... | collective-permute-start | bytes 3145736 | tf_op jit(solution)/shard_map/ppermute | solution.py:142
  156.3 30.6 %all-to-all-start.2 = ((bf16[16,16,1024]{2,1,0:T(8,128)(2,1)}), bf16[16,16,1024]{2,1,0:T(8,128)(2,1)S(1)}, u32[]{:S(2)}, u32[]{:S(2)}) async-start(bf16[16,16,1024]{2,1,0:T(8,128)(2,1)} %bitcast.4), calls=%async_computation.2 | async-start | bytes 1048576 | tf_op jit(solution)/shard_map/all_to_all | solution.py:90
  186.9 53.4 %all-to-all-start.3 = ((bf16[256,16,256]{2,1,0:T(8,128)(2,1)}), bf16[256,16,256]{2,1,0:T(8,128)(2,1)S(1)}, u32[]{:S(2)}, u32[]{:S(2)}) async-start(bf16[256,16,256]{2,1,0:T(8,128)(2,1)} %bitcast.62), calls=%async_computation.3 | async-start | bytes 4194304 | tf_op jit(solution)/shard_map/all_to_all | solution.py:152
  242.0 1.0 copy-start.2
  242.1 2.6 %copy-start.1 = (bf16[16,64,64]{2,1,0:T(8,128)(2,1)S(1)}, bf16[16,64,64]{2,1,0:T(8,128)(2,1)}, u32[]{:S(2)}) copy-start(bf16[16,64,64]{2,1,0:T(8,128)(2,1)} %param.10) | copy-start | bytes 393220

commit v2 on v1

--- a/solution.py
+++ b/solution.py
@@ -1,6 +1,8 @@
 import jax
 import jax.numpy as jnp
 from jax import lax
+from jax.experimental import pallas as pl
+from jax.experimental.pallas import tpu as pltpu
 from jax.sharding import PartitionSpec as P
 
 root_step = 0.1
@@ -21,6 +23,177 @@
         for p in range(chips)
         for b in (0, 1)
     ]
+
+
+GROUP = 16
+SLOTS = 4
+SPAN = 256
+MIB = 1 << 20
+whole_vmem = pl.BlockSpec(memory_space=pltpu.VMEM)
+
+
+def divisor(n, most, unit):
+    fits = [d for d in range(unit, min(n, most) + 1, unit) if n % d == 0]
+    return fits[-1] if fits else n
+
+
+def by_row_kernel(chol, out):
+    depth, rows, width = chol.shape
+    size = GROUP * rows
+    to = lax.broadcasted_iota(jnp.int32, (size, size), 0)
+    source = lax.broadcasted_iota(jnp.int32, (size, size), 1)
+    regroup = (to == (source % rows) * GROUP + source // rows).astype(f32).astype(bf16)
+    for at in range(0, depth, GROUP):
+        mixed = chol[at : at + GROUP].reshape(size, width)
+        sorted_rows = jnp.dot(regroup, mixed, preferred_element_type=f32).astype(bf16)
+        out[:, at : at + GROUP, :] = sorted_rows.reshape(rows, GROUP, width)
+
+
+def chol_by_row(chol):
+    chol_n, rows, width = chol.shape
+    depth = divisor(chol_n, 8192 // rows, GROUP)
+    return pl.pallas_call(
+        by_row_kernel,
+        grid=(chol_n // depth,),
+        in_specs=[pl.BlockSpec((depth, rows, width), lambda t: (t, 0, 0))],
+        out_specs=pl.BlockSpec((rows, depth, width), lambda t: (0, t, 0)),
+        out_shape=jax.ShapeDtypeStruct((rows, chol_n, width), bf16),
+        compiler_params=pltpu.CompilerParams(vmem_limit_bytes=40 * MIB),
+        cost_estimate=pl.CostEstimate(
+            flops=2 * chol.size * GROUP * rows, bytes_accessed=4 * chol.size, transcendentals=0
+        ),
+    )(chol)
+
+
+def stream(blocks, fetch, work):
+    first = min(SLOTS - 1, blocks)
+    for block in range(first):
+        fetch(block, block).start()
+
+    def run():
+        def step(block, carry):
+            slot = lax.rem(block, SLOTS)
+
+            @pl.when(block + SLOTS - 1 < blocks)
+            def _():
+                fetch(block + SLOTS - 1, lax.rem(block + SLOTS - 1, SLOTS)).start()
+
+            fetch(block, slot).wait()
+            work(block, slot)
+            return carry
+
+        lax.fori_loop(0, blocks, step, 0)
+
+    return run
+
+
+def bias_kernel(pick, theta, trial, chol, out, density, held, arrived):
+    rows, chol_n, width = chol.shape
+    electrons = trial.shape[0]
+    span = held.shape[2]
+
+    def fetch(block, slot):
+        here = pl.ds(block * span, span)
+        return pltpu.make_async_copy(chol.at[:, here], held.at[slot], arrived.at[slot])
+
+    def work(block, slot):
+        total = jnp.zeros((pick.shape[0], span), f32)
+        for i in range(rows):
+            total += lax.dot_general(
+                density[i], held[slot, i], (((1,), (1,)), ((), ())), preferred_element_type=f32
+            )
+        out[:, pl.ds(pl.multiple_of(block * span, span), span)] = total.astype(bf16)
+
+    run = stream(chol_n // span, fetch, work)
+    picked = jnp.dot(
+        pick[...], theta[:, : rows * electrons], preferred_element_type=f32
+    ).astype(bf16)
+    for i in range(rows):
+        density[i] = jnp.dot(
+            picked[:, i * electrons : (i + 1) * electrons], trial[...], preferred_element_type=f32
+        ).astype(bf16)
+    run()
+
+
+def bias_parts(pick, theta, trial, by_row):
+    rows, chol_n, width = by_row.shape
+    everyone = pick.shape[0]
+    span = divisor(chol_n, SPAN, 128)
+    return pl.pallas_call(
+        bias_kernel,
+        in_specs=[whole_vmem] * 3 + [pl.BlockSpec(memory_space=pl.ANY)],
+        out_specs=whole_vmem,
+        out_shape=jax.ShapeDtypeStruct((everyone, chol_n), bf16),
+        scratch_shapes=[
+            pltpu.VMEM((rows, everyone, width), bf16),
+            pltpu.VMEM((SLOTS, rows, span, width), bf16),
+            pltpu.SemaphoreType.DMA((SLOTS,)),
+        ],
+        compiler_params=pltpu.CompilerParams(vmem_limit_bytes=40 * MIB),
+        cost_estimate=pl.CostEstimate(
+            flops=2 * everyone * by_row.size, bytes_accessed=2 * by_row.size, transcendentals=0
+        ),
+    )(pick, theta, trial, by_row)
+
+
+def propagator_kernel(
+    spots, own_core, other_core, chol, out, fields, built, sent, held, arrived
+):
+    rows, chol_n, width = chol.shape
+    pieces, per_device = own_core.shape[:2]
+    span = divisor(chol_n, 1024, 256)
+
+    def fetch(block, slot):
+        return pltpu.make_async_copy(chol.at[block], held.at[slot], arrived.at[slot])
+
+    def put(i):
+        return pltpu.make_async_copy(built.at[i], out.at[:, i], sent.at[i])
+
+    def work(i, slot):
+        total = jnp.zeros((fields.shape[0], width), f32)
+        for at in range(0, chol_n, span):
+            total += jnp.dot(
+                fields[:, at : at + span],
+                held[slot, at : at + span],
+                preferred_element_type=f32,
+            )
+        built[i] = total.astype(bf16).reshape(built.shape[1:])
+        put(i).start()
+
+    run = stream(rows, fetch, work)
+    for side, piece in enumerate((own_core, other_core)):
+        for n in range(pieces):
+            at = pl.multiple_of(spots[side * pieces + n] * per_device, per_device)
+            fields[pl.ds(at, per_device), :] = piece[n]
+    run()
+    for i in range(rows):
+        put(i).wait()
+
+
+def propagator_parts(spots, own_core, other_core, by_row):
+    rows, chol_n, width = by_row.shape
+    chips, per_device, _ = own_core.shape
+    devices = 2 * chips
+    in_hbm = pl.BlockSpec(memory_space=pl.ANY)
+    return pl.pallas_call(
+        propagator_kernel,
+        in_specs=[pl.BlockSpec(memory_space=pltpu.SMEM), whole_vmem, whole_vmem, in_hbm],
+        out_specs=in_hbm,
+        out_shape=jax.ShapeDtypeStruct((devices, rows, per_device, width), bf16),
+        scratch_shapes=[
+            pltpu.VMEM((devices * per_device, chol_n), bf16),
+            pltpu.VMEM((rows, devices, per_device, width), bf16),
+            pltpu.SemaphoreType.DMA((rows,)),
+            pltpu.VMEM((SLOTS, chol_n, width), bf16),
+            pltpu.SemaphoreType.DMA((SLOTS,)),
+        ],
+        compiler_params=pltpu.CompilerParams(vmem_limit_bytes=40 * MIB),
+        cost_estimate=pl.CostEstimate(
+            flops=2 * devices * per_device * by_row.size,
+            bytes_accessed=2 * by_row.size,
+            transcendentals=0,
+        ),
+    )(spots, own_core, other_core, by_row)
 
 
 def local(walkers, inv_intersection, copies, deal, trial, chol, noise):
@@ -33,6 +206,8 @@
     ring = chip_ring(devices)
     place = [ring.index(m) for m in range(chips)]
 
+    by_row = chol_by_row(chol)
+
     theta = jnp.einsum(
         "wmk,wkn->wmn", walkers, inv_intersection, preferred_element_type=f32
     ).astype(bf16)
@@ -42,14 +217,16 @@
         return jnp.transpose(a, (1, 0, 2))
 
     counts = jnp.broadcast_to(copies.astype(bf16)[None, :, None], (devices, per_device, 128))
+    wide = own_rows * electrons
     first = lax.all_to_all(
-        jnp.concatenate([by_owner(theta), counts], axis=2), "row", 0, 0, tiled=True
-    ).reshape(everyone, own_rows * electrons + 128)
-    theta_rows = first[:, : own_rows * electrons]
-    count_column = first[:, own_rows * electrons :][:, :1].astype(f32)
-    walker_rows = lax.all_to_all(by_owner(walkers), "row", 0, 0, tiled=True).reshape(
-        everyone, own_rows * electrons
-    )
+        jnp.concatenate([by_owner(theta), by_owner(walkers), counts], axis=2),
+        "row",
+        0,
+        0,
+        tiled=True,
+    ).reshape(everyone, 2 * wide + 128)
+    count_column = first[:, 2 * wide :][:, :1].astype(f32)
+    walker_rows = first[:, wide : 2 * wide]
 
     ids = jnp.arange(everyone, dtype=jnp.int32)
     before = (ids[:, None] <= ids[None, :]).astype(f32)
@@ -76,14 +253,6 @@
         jnp.where(spot[:, None] == residues[None, :chips], ring_ids[None, :], 0), axis=1
     )
     owner = 2 * to_chip + (core ^ flip)
-    picked = jnp.dot(parents_of(owner, slot), theta_rows, preferred_element_type=f32).astype(bf16)
-    density = jnp.einsum(
-        "win,jn->wij",
-        picked.reshape(everyone, own_rows, electrons),
-        trial,
-        preferred_element_type=f32,
-    ).astype(bf16)
-
     new_rows = jnp.dot(
         parents_of(ids // per_device, slot), walker_rows, preferred_element_type=f32
     ).astype(bf16)
@@ -94,13 +263,7 @@
         got_rows.reshape(devices, per_device, own_rows, electrons), (1, 0, 2, 3)
     ).reshape(per_device, orbitals_n, electrons)
 
-    chol_flat = chol.reshape(chol_n, own_rows * width)
-    part = lax.dot_general(
-        density.reshape(everyone, own_rows * width),
-        chol_flat,
-        (((1,), (1,)), ((), ())),
-        preferred_element_type=f32,
-    ).astype(bf16)
+    part = bias_parts(parents_of(owner, slot), first, trial.T, by_row)
     part = part.reshape(2, chips, per_device, chol_n)
 
     swap = ring_move(devices, 1, 0)
@@ -140,22 +303,14 @@
             offsets.append(t + 1)
     own_core = jnp.stack(pieces)
     other_core = lax.ppermute(own_core, "row", swap)
-    all_fields = jnp.zeros((devices, per_device, chol_n), bf16)
-    for held, side in ((own_core, core), (other_core, 1 - core)):
-        for n, offset in enumerate(offsets):
-            spot = (own_place + offset) % chips
-            to = 2 * jnp.sum(jnp.where(residues[:chips] == spot, ring_ids, 0)) + side
-            all_fields = lax.dynamic_update_index_in_dim(all_fields, held[n], to, 0)
-    propagator_part = jnp.dot(
-        all_fields.reshape(everyone, chol_n), chol_flat, preferred_element_type=f32
-    ).astype(bf16)
-    propagator = lax.all_to_all(
-        propagator_part.reshape(everyone, own_rows, width),
-        "row",
-        split_axis=0,
-        concat_axis=1,
-        tiled=True,
+    spots = (own_place + jnp.array(offsets, jnp.int32)) % chips
+    spots = 2 * jnp.sum(
+        jnp.where(spots[:, None] == residues[None, :chips], ring_ids[None, :], 0), axis=1
     )
+    spots = jnp.concatenate([spots + core, spots + 1 - core])
+    propagator_part = propagator_parts(spots, own_core, other_core, by_row)
+    got = lax.all_to_all(propagator_part, "row", 0, 0, tiled=True)
+    propagator = jnp.transpose(got, (2, 0, 1, 3)).reshape(per_device, orbitals_n, width)
     current = orbitals
     summed = orbitals.astype(f32)
     for degree in range(1, 5):

time: 246 us -> 192 us (0.78)
  Pallas kernels: 0 us -> 54.4 us
  matrix products: 60.4 us -> 12.2 us
  local copies, waits for them, and re-layouts: 47 us -> 6.19 us
  between operations: 12.6 us -> 0.94 us
  starting transfers between devices: 42.4 us -> 38.3 us
  waiting for transfers between devices: 77.6 us -> 74.8 us
    pallas_call x0 -> x3, Pallas kernels: none -> 54.4 us  [the longest x1 25.8 us: chol_by_row(): pl.pallas_call(by_row_kernel, grid=(chol_n // depth,), in_specs=[pl.Block...]
    dot_general x3 -> x0, matrix products: 54 us -> none  [the longest x1 38.3 us: local(): lax.dot_general(density.reshape(everyone, own_rows * width), chol_flat, (...]
    unnamed x33 -> x25, local copies, waits for them, and re-layouts: 30.3 us -> 1.63 us
    all_to_all x3 -> x2, waiting for transfers between devices: 57 us -> 46.2 us  [the longest x1 46.2 us: local(): got = lax.all_to_all(propagator_part, 'row', 0, 0, tiled=True)]
    all_to_all x3 -> x2, starting transfers between devices: 22.1 us -> 12.6 us  [the longest x1 6.55 us: local(): lax.all_to_all(jnp.concatenate([by_owner(theta), by_owner(walkers), count...]
    dynamic_update_slice x9 -> x0, local copies, waits for them, and re-layouts: 7.38 us -> none  [local(): all_fields = lax.dynamic_update_index_in_dim(all_fields, held[n], to, 0)]
    dot_general x4, matrix products: 3.85 us -> 10.7 us  [local(): jnp.einsum('wik,wkn->win', propagator, current, preferred_element_type=f32)]
    ppermute x1, starting transfers between devices: 4.64 us -> 10 us  [local(): other_core = lax.ppermute(own_core, 'row', swap)]
  transfers between devices with their start and end apart: 20 -> 19, of which waited for: 13 -> 15; matrix products, arithmetic and copies ran while one was open for 26% -> 3% of each run, Pallas kernels for 0% -> 21%
where the time goes in v2:
time: 192 us; the launch traced here: 191 us
  waiting for transfers between devices  74.8 us (39%)
  Pallas kernels  54.4 us (28%)
  starting transfers between devices  38.3 us (20%)
  matrix products  12.2 us (6%)
  local copies, waits for them, and re-layouts  6.19 us (3%)
  other arithmetic  4.67 us (2%)
    all_to_all x1, waiting for transfers between devices, local(): got = lax.all_to_all(propagator_part, 'row', 0, 0, tiled=True)  46.2 us
    pallas_call x1, Pallas kernels, chol_by_row(): pl.pallas_call(by_row_kernel, grid=(chol_n // depth,), in_specs=[pl.Block...  25.8 us
    pallas_call x1, Pallas kernels, propagator_parts(): pl.pallas_call(propagator_kernel, in_specs=[pl.BlockSpec(memory_space=plt...  14.4 us
    pallas_call x1, Pallas kernels, bias_parts(): pl.pallas_call(bias_kernel, in_specs=[whole_vmem] * 3 + [pl.BlockSpec(mem...  14.2 us
    ppermute x4, waiting for transfers between devices, local(): going_right = lax.ppermute(going_right, 'row', right)  12.3 us
    dot_general x4, matrix products, local(): jnp.einsum('wik,wkn->win', propagator, current, preferred_element_type=f32)  10.7 us
    ppermute x4, waiting for transfers between devices, local(): moving_right = lax.ppermute(moving_right, 'row', right)  10.1 us
    ppermute x1, starting transfers between devices, local(): other_core = lax.ppermute(own_core, 'row', swap)  10 us
  transfers between devices with their start and end apart: 19, of which 15 were waited for; matrix products, arithmetic and copies ran while one was open for 3% of the time, Pallas kernels for 21%

profile of v2, /device:TPU:15, one launch (start us, length us, event | category | flops | bytes accessed | tf_op | source)
XLA Modules:
  0.0 191.4 jit_solution(15583734980607365109)
XLA Ops:
  0.7 0.7 convert_element_type.203
  1.4 1.5 copy.42
  2.9 0.7 reshape.144
  3.7 0.4 convolution_convert_fusion
  4.0 0.5 copy.41
  4.5 0.7 reshape.143
  5.3 0.1 pad_maximum_fusion
  5.4 1.2 copy.43
  6.6 6.6 %all-to-all-start = ((bf16[16,16,2176]{2,1,0:T(8,128)(2,1)}), bf16[16,16,2176]{2,1,0:T(8,128)(2,1)S(1)}, u32[]{:S(2)}, u32[]{:S(2)}) async-start(bf16[16,16,2176]{2,1,0:T(8,128)(2,1)} %copy.43), calls=%async_computation | async-start | bytes 2228224 | tf_op jit(solution)/shard_map/all_to_all | solution.py:221
  13.2 0.6 fusion.58
  13.9 0.7 and_select_fusion.1
  14.5 0.1 select_reduce_fusion.4
  14.6 0.1 select_reduce_fusion.2
  14.7 25.8 %shard_map.113.chol = bf16[16,4096,256]{2,1,0:T(8,128)(2,1)} custom-call(bf16[4096,16,256]{2,1,0:T(8,128)(2,1)} %chol.1), custom_call_target="tpu_custom_call" | custom-call | flops 8589934592 | bytes 67108864 | tf_op jit(solution)/shard_map/pallas_call | solution.py:55
  40.5 0.1 convert_reduce_fusion
  40.7 0.1 select_reduce_fusion.1
  40.8 0.1 and_convert_fusion.pick
  40.9 14.2 %shard_map.114 = bf16[256,4096]{1,0:T(8,128)(2,1)S(1)} custom-call(bf16[256,256]{1,0:T(8,128)(2,1)S(1)} %and_convert_fusion.pick, bf16[256,2176]{1,0:T(8,128)(2,1)S(1)} %bitcast.125, bf16[64,256]{1,0:T(8,128)(2,1)S(1)} %bitcast.127, bf16[16,4096,256]{2,1,0:T(8,128)(2,1)} %shard_map.113.chol), custom_call_target="tpu_custom_call" | custom-call | flops 8589934592 | bytes 33554432 | tf_op jit(solution)/shard_map/pallas_call | solution.py:122
  55.2 0.4 collective-permute-start
  55.6 2.3 %collective-permute-done = bf16[8,16,4096]{2,1,0:T(8,128)(2,1)S(1)} collective-permute-done((bf16[8,16,4096]{2,1,0:T(8,128)(2,1)S(1)}, bf16[8,16,4096]{2,1,0:T(8,128)(2,1)S(1)}, u32[]{:S(2)}, u32[]{:S(2)}) %collective-permute-start) | collective-permute-done | bytes 1048608 | tf_op jit(solution)/shard_map/ppermute | solution.py:272
  58.0 0.4 collective-permute-start.1
  58.3 4.4 %collective-permute-done.1 = bf16[16,4096]{1,0:T(8,128)(2,1)S(1)} collective-permute-done((bf16[16,4096]{1,0:T(8,128)(2,1)S(1)}, bf16[16,4096]{1,0:T(8,128)(2,1)S(1)}, u32[]{:S(2)}, u32[]{:S(2)}) %collective-permute-start.1) | collective-permute-done | bytes 131104 | tf_op jit(solution)/shard_map/ppermute | solution.py:281
  62.8 0.4 collective-permute-start.2
  63.2 1.1 collective-permute-start.5
  64.3 2.4 %collective-permute-done.2 = bf16[16,4096]{1,0:T(8,128)(2,1)S(1)} collective-permute-done((bf16[16,4096]{1,0:T(8,128)(2,1)S(1)}, bf16[16,4096]{1,0:T(8,128)(2,1)S(1)}, u32[]{:S(2)}, u32[]{:S(2)}) %collective-permute-start.2) | collective-permute-done | bytes 131104 | tf_op jit(solution)/shard_map/ppermute | solution.py:281
  66.7 0.7 collective-permute-done.5
  67.3 0.1 fusion.34
  67.5 0.3 collective-permute-start.3
  67.7 1.2 collective-permute-start.6
  69.0 2.3 %collective-permute-done.3 = bf16[16,4096]{1,0:T(8,128)(2,1)S(1)} collective-permute-done((bf16[16,4096]{1,0:T(8,128)(2,1)S(1)}, bf16[16,4096]{1,0:T(8,128)(2,1)S(1)}, u32[]{:S(2)}, u32[]{:S(2)}) %collective-permute-start.3) | collective-permute-done | bytes 131104 | tf_op jit(solution)/shard_map/ppermute | solution.py:281
  71.3 0.2 collective-permute-done.6
  71.6 0.1 fusion.32
  71.7 1.3 collective-permute-start.7
  72.9 0.3 collective-permute-start.4
  73.3 2.5 %collective-permute-done.7 = bf16[16,4096]{1,0:T(8,128)(2,1)S(1)} collective-permute-done((bf16[16,4096]{1,0:T(8,128)(2,1)S(1)}, bf16[16,4096]{1,0:T(8,128)(2,1)S(1)}, u32[]{:S(2)}, u32[]{:S(2)}) %collective-permute-start.7) | collective-permute-done | bytes 131104 | tf_op jit(solution)/shard_map/ppermute | solution.py:283
  75.8 1.0 collective-permute-done.4
  76.8 0.8 bitcast_dynamic-update-slice_fusion.7
  77.6 0.5 collective-permute-start.8
  78.0 1.0 collective-permute-start.9
  79.0 3.7 %collective-permute-done.8 = bf16[16,4096]{1,0:T(8,128)(2,1)S(1)} collective-permute-done((bf16[16,4096]{1,0:T(8,128)(2,1)S(1)}, bf16[16,4096]{1,0:T(8,128)(2,1)S(1)}, u32[]{:S(2)}, u32[]{:S(2)}) %collective-permute-start.8) | collective-permute-done | bytes 131104 | tf_op jit(solution)/shard_map/ppermute | solution.py:297
  82.8 0.1 collective-permute-start.10
  82.9 1.4 collective-permute-start.11
  84.3 2.3 %collective-permute-done.10 = bf16[16,4096]{1,0:T(8,128)(2,1)S(1)} collective-permute-done((bf16[16,4096]{1,0:T(8,128)(2,1)S(1)}, bf16[16,4096]{1,0:T(8,128)(2,1)S(1)}, u32[]{:S(2)}, u32[]{:S(2)}) %collective-permute-start.10) | collective-permute-done | bytes 131104 | tf_op jit(solution)/shard_map/ppermute | solution.py:297
  86.6 0.1 collective-permute-start.12
  86.8 1.4 collective-permute-start.13
  88.2 2.3 %collective-permute-done.12 = bf16[16,4096]{1,0:T(8,128)(2,1)S(1)} collective-permute-done((bf16[16,4096]{1,0:T(8,128)(2,1)S(1)}, bf16[16,4096]{1,0:T(8,128)(2,1)S(1)}, u32[]{:S(2)}, u32[]{:S(2)}) %collective-permute-start.12) | collective-permute-done | bytes 131104 | tf_op jit(solution)/shard_map/ppermute | solution.py:297
  90.4 0.1 collective-permute-start.14
  90.5 0.3 collective-permute-done.13
  90.9 4.1 %collective-permute-done.14 = bf16[16,4096]{1,0:T(8,128)(2,1)S(1)} collective-permute-done((bf16[16,4096]{1,0:T(8,128)(2,1)S(1)}, bf16[16,4096]{1,0:T(8,128)(2,1)S(1)}, u32[]{:S(2)}, u32[]{:S(2)}) %collective-permute-start.14) | collective-permute-done | bytes 131104 | tf_op jit(solution)/shard_map/ppermute | solution.py:297
  95.0 10.0 %collective-permute-start.15 = (bf16[8,16,4096]{2,1,0:T(8,128)(2,1)S(1)}, bf16[8,16,4096]{2,1,0:T(8,128)(2,1)S(1)}, u32[]{:S(2)}, u32[]{:S(2)}) collective-permute-start(bf16[8,16,4096]{2,1,0:T(8,128)(2,1)S(1)} %bitcast_dynamic-update-slice_fusion.own_core), channel_id=1, source_target_pairs={{0,1},{1,0},{4,5},{5,4},{8,9},{9,8},{12,13},{13,12},{14,15},{15,14... | collective-permute-start | bytes 3145736 | tf_op jit(solution)/shard_map/ppermute | solution.py:305
  105.0 0.7 and_select_fusion.3
  105.6 0.2 select_reduce_fusion.5
  105.8 1.1 convolution_convert_fusion.1
  107.0 5.7 %all-to-all-start.1 = ((bf16[16,16,1024]{2,1,0:T(8,128)(2,1)}), bf16[16,16,1024]{2,1,0:T(8,128)(2,1)S(1)}, u32[]{:S(2)}, u32[]{:S(2)}) async-start(bf16[16,16,1024]{2,1,0:T(8,128)(2,1)} %bitcast.133), calls=%async_computation.1 | async-start | bytes 1048576 | tf_op jit(solution)/shard_map/all_to_all | solution.py:259
  112.8 14.4 %shard_map.115 = bf16[16,16,16,256]{3,2,1,0:T(8,128)(2,1)} custom-call(s32[16]{0:T(128)S(1)} %pad_add_fusion.spots, bf16[8,16,4096]{2,1,0:T(8,128)(2,1)S(1)} %bitcast_dynamic-update-slice_fusion.own_core, bf16[8,16,4096]{2,1,0:T(8,128)(2,1)S(1)} %collective-permute-done.15.other_core, bf16[16,4096,256]{2,1,0:T(8,128)(2,1)} %shard_map.113.chol), custom_call_target="tpu_custom_call" | custom-call | flops 8589934592 | bytes 33554432 | tf_op jit(solution)/shard_map/pallas_call | solution.py:178
  127.2 6.0 %all-to-all-start.2 = ((bf16[16,16,16,256]{3,2,1,0:T(8,128)(2,1)}), bf16[16,16,16,256]{3,2,1,0:T(8,128)(2,1)}, u32[]{:S(2)}, u32[]{:S(2)}) async-start(bf16[16,16,16,256]{3,2,1,0:T(8,128)(2,1)} %shard_map.115), calls=%async_computation.2 | async-start | bytes 4194304 | tf_op jit(solution)/shard_map/all_to_all | solution.py:312
  133.2 0.3 copy.44
  133.5 0.7 reshape.147
  134.1 0.3 copy.45
  134.5 46.2 %all-to-all-done.2 = bf16[16,16,16,256]{3,2,1,0:T(8,128)(2,1)} async-done(((bf16[16,16,16,256]{3,2,1,0:T(8,128)(2,1)}), bf16[16,16,16,256]{3,2,1,0:T(8,128)(2,1)}, u32[]{:S(2)}, u32[]{:S(2)}) %all-to-all-start.2) | async-done | bytes 2097184 | tf_op jit(solution)/shard_map/all_to_all | solution.py:312
  180.7 2.4 %fusion.22 = bf16[16,256,64]{1,2,0:T(8,128)(2,1)S(1)} fusion(bf16[16,256,64]{2,1,0:T(8,128)(2,1)S(1)} %bitcast.129, bf16[16,256,256]{2,0,1:T(8,128)(2,1)} %bitcast.34), kind=kOutput, calls=%fused_computation.16 | convolution fusion | flops 134742016 | bytes 3145728 | tf_op jit(solution)/shard_map/wik,wkn->win/dot_general | solution.py:317
  183.2 2.4 %fusion.4 = bf16[16,256,64]{1,2,0:T(8,128)(2,1)S(1)} fusion(bf16[16,256,64]{1,2,0:T(8,128)(2,1)S(1)} %fusion.22, bf16[16,256,256]{2,0,1:T(8,128)(2,1)} %bitcast.34), kind=kOutput, calls=%fused_computation.10 | convolution fusion | flops 134742016 | bytes 3145728 | tf_op jit(solution)/shard_map/wik,wkn->win/dot_general | solution.py:317
  185.6 2.5 %fusion.7 = bf16[16,256,64]{1,2,0:T(8,128)(2,1)S(1)} fusion(bf16[16,256,64]{1,2,0:T(8,128)(2,1)S(1)} %fusion.4, bf16[16,256,256]{2,0,1:T(8,128)(2,1)} %bitcast.34), kind=kOutput, calls=%fused_computation.11 | convolution fusion | flops 134742016 | bytes 3145728 | tf_op jit(solution)/shard_map/wik,wkn->win/dot_general | solution.py:317
  188.1 3.4 %fusion.19 = bf16[16,256,64]{1,2,0:T(8,128)(2,1)} fusion(bf16[16,256,64]{1,2,0:T(8,128)(2,1)S(1)} %fusion.7, bf16[16,256,256]{2,0,1:T(8,128)(2,1)} %bitcast.34, bf16[16,256,64]{1,2,0:T(8,128)(2,1)S(1)} %fusion.4, bf16[16,256,64]{1,2,0:T(8,128)(2,1)S(1)} %fusion.22, bf16[16,256,64]{1,2,0:T(8,128)(2,1)S(1)} %copy.45), kind=kOutput, calls=%fused_computation.15 | convolution fusion | flops 137363456 | bytes 4718592 | tf_op jit(solution)/shard_map/wik,wkn->win/dot_general | solution.py:317
  (40 shorter events, 0.6 us)
Async XLA Ops:
  0.6 3.0 %copy-start = (bf16[16,64,64]{2,1,0:T(8,128)(2,1)S(1)}, bf16[16,64,64]{2,1,0:T(8,128)(2,1)}, u32[]{:S(2)}) copy-start(bf16[16,64,64]{2,1,0:T(8,128)(2,1)} %param.11) | copy-start | bytes 393220
  0.6 3.0 %copy-start.3 = (bf16[16,256,64]{1,2,0:T(8,128)(2,1)S(1)}, bf16[16,256,64]{1,2,0:T(8,128)(2,1)}, u32[]{:S(2)}) copy-start(bf16[16,256,64]{1,2,0:T(8,128)(2,1)} %param.10) | copy-start | bytes 1572868
  5.4 7.8 %copy-start.7 = (s32[8]{0:T(128)S(1)}, s32[8]{0:T(128)}, u32[]{:S(2)}) copy-start(s32[8]{0:T(128)} %constant.125.clone) | copy-start | bytes 100
  5.4 9.1 %copy-start.5 = (s32[8]{0:T(128)S(1)}, s32[8]{0:T(128)}, u32[]{:S(2)}) copy-start(s32[8]{0:T(128)} %constant.124.clone) | copy-start | bytes 100
  5.4 9.2 %copy-start.6 = (s32[16]{0:T(128)S(1)}, s32[16]{0:T(128)}, u32[]{:S(2)}) copy-start(s32[16]{0:T(128)} %param.13) | copy-start | bytes 196
  6.6 33.9 %all-to-all-start = ((bf16[16,16,2176]{2,1,0:T(8,128)(2,1)}), bf16[16,16,2176]{2,1,0:T(8,128)(2,1)S(1)}, u32[]{:S(2)}, u32[]{:S(2)}) async-start(bf16[16,16,2176]{2,1,0:T(8,128)(2,1)} %copy.43), calls=%async_computation | async-start | bytes 2228224 | tf_op jit(solution)/shard_map/all_to_all | solution.py:221
  14.7 26.2 %copy-start.2 = (bf16[256,64]{0,1:T(8,128)(2,1)S(1)}, bf16[256,64]{0,1:T(8,128)(2,1)}, u32[]{:S(2)}) copy-start(bf16[256,64]{0,1:T(8,128)(2,1)} %param.14) | copy-start | bytes 98308
  55.2 21.6 %copy-start.4 = (f32[16,4096]{1,0:T(8,128)S(1)}, f32[16,4096]{1,0:T(8,128)}, u32[]{:S(2)}) copy-start(f32[16,4096]{1,0:T(8,128)} %param.16) | copy-start | bytes 786436
  55.2 2.7 %collective-permute-start = (bf16[8,16,4096]{2,1,0:T(8,128)(2,1)S(1)}, bf16[8,16,4096]{2,1,0:T(8,128)(2,1)S(1)}, u32[]{:S(2)}, u32[]{:S(2)}) collective-permute-start(bf16[8,16,4096]{2,1,0:T(8,128)(2,1)S(1)} %bitcast.132), channel_id=1, source_target_pairs={{0,1},{1,0},{4,5},{5,4},{8,9},{9,8},{12,13},{13,12},{14,15},{15,14... | collective-permute-start | bytes 3145736 | tf_op jit(solution)/shard_map/ppermute | solution.py:272
  58.0 4.8 %collective-permute-start.1 = (bf16[16,4096]{1,0:T(8,128)(2,1)S(1)}, bf16[16,4096]{1,0:T(8,128)(2,1)S(1)}, u32[]{:S(2)}, u32[]{:S(2)}) collective-permute-start(bf16[16,4096]{1,0:T(8,128)(2,1)S(1)} %fusion.37), channel_id=1, source_target_pairs={{0,4},{1,5},{4,8},{5,9},{8,12},{9,13},{12,14},{13,15},{14,10},{15,... | collective-permute-start | bytes 393224 | tf_op jit(solution)/shard_map/ppermute | solution.py:281
  62.8 3.9 %collective-permute-start.2 = (bf16[16,4096]{1,0:T(8,128)(2,1)S(1)}, bf16[16,4096]{1,0:T(8,128)(2,1)S(1)}, u32[]{:S(2)}, u32[]{:S(2)}) collective-permute-start(bf16[16,4096]{1,0:T(8,128)(2,1)S(1)} %get-tuple-element.13), channel_id=1, source_target_pairs={{0,4},{1,5},{4,8},{5,9},{8,12},{9,13},{12,14},{13,15},{14,10},{15,... | collective-permute-start | bytes 393224 | tf_op jit(solution)/shard_map/ppermute | solution.py:281
  63.2 4.1 %collective-permute-start.5 = (bf16[16,4096]{1,0:T(8,128)(2,1)S(1)}, bf16[16,4096]{1,0:T(8,128)(2,1)S(1)}, u32[]{:S(2)}, u32[]{:S(2)}) collective-permute-start(bf16[16,4096]{1,0:T(8,128)(2,1)S(1)} %get-tuple-element.14), channel_id=1, source_target_pairs={{0,2},{1,3},{4,0},{5,1},{8,4},{9,5},{12,8},{13,9},{14,12},{15,13},... | collective-permute-start | bytes 393224 | tf_op jit(solution)/shard_map/ppermute | solution.py:283
  67.5 3.9 %collective-permute-start.3 = (bf16[16,4096]{1,0:T(8,128)(2,1)S(1)}, bf16[16,4096]{1,0:T(8,128)(2,1)S(1)}, u32[]{:S(2)}, u32[]{:S(2)}) collective-permute-start(bf16[16,4096]{1,0:T(8,128)(2,1)S(1)} %get-tuple-element.11), channel_id=1, source_target_pairs={{0,4},{1,5},{4,8},{5,9},{8,12},{9,13},{12,14},{13,15},{14,10},{15,... | collective-permute-start | bytes 393224 | tf_op jit(solution)/shard_map/ppermute | solution.py:281
  67.7 37.2 %copy-start.8 = (s32[8]{0:T(128)S(1)}, s32[8]{0:T(128)}, u32[]{:S(2)}) copy-start(s32[8]{0:T(128)} %constant.126.clone) | copy-start | bytes 100
  67.7 3.8 %collective-permute-start.6 = (bf16[16,4096]{1,0:T(8,128)(2,1)S(1)}, bf16[16,4096]{1,0:T(8,128)(2,1)S(1)}, u32[]{:S(2)}, u32[]{:S(2)}) collective-permute-start(bf16[16,4096]{1,0:T(8,128)(2,1)S(1)} %get-tuple-element.12), channel_id=1, source_target_pairs={{0,2},{1,3},{4,0},{5,1},{8,4},{9,5},{12,8},{13,9},{14,12},{15,13},... | collective-permute-start | bytes 393224 | tf_op jit(solution)/shard_map/ppermute | solution.py:283
  71.7 4.1 %collective-permute-start.7 = (bf16[16,4096]{1,0:T(8,128)(2,1)S(1)}, bf16[16,4096]{1,0:T(8,128)(2,1)S(1)}, u32[]{:S(2)}, u32[]{:S(2)}) collective-permute-start(bf16[16,4096]{1,0:T(8,128)(2,1)S(1)} %get-tuple-element.10), channel_id=1, source_target_pairs={{0,2},{1,3},{4,0},{5,1},{8,4},{9,5},{12,8},{13,9},{14,12},{15,13},... | collective-permute-start | bytes 393224 | tf_op jit(solution)/shard_map/ppermute | solution.py:283
  72.9 3.8 %collective-permute-start.4 = (bf16[16,4096]{1,0:T(8,128)(2,1)S(1)}, bf16[16,4096]{1,0:T(8,128)(2,1)S(1)}, u32[]{:S(2)}, u32[]{:S(2)}) collective-permute-start(bf16[16,4096]{1,0:T(8,128)(2,1)S(1)} %get-tuple-element.9), channel_id=1, source_target_pairs={{0,4},{1,5},{4,8},{5,9},{8,12},{9,13},{12,14},{13,15},{14,10},{15,... | collective-permute-start | bytes 393224 | tf_op jit(solution)/shard_map/ppermute | solution.py:281
  77.6 5.2 %collective-permute-start.8 = (bf16[16,4096]{1,0:T(8,128)(2,1)S(1)}, bf16[16,4096]{1,0:T(8,128)(2,1)S(1)}, u32[]{:S(2)}, u32[]{:S(2)}) collective-permute-start(bf16[16,4096]{1,0:T(8,128)(2,1)S(1)} %get-tuple-element.7), channel_id=1, source_target_pairs={{0,4},{1,5},{4,8},{5,9},{8,12},{9,13},{12,14},{13,15},{14,10},{15,... | collective-permute-start | bytes 393224 | tf_op jit(solution)/shard_map/ppermute | solution.py:297
  78.0 4.9 %collective-permute-start.9 = (bf16[16,4096]{1,0:T(8,128)(2,1)S(1)}, bf16[16,4096]{1,0:T(8,128)(2,1)S(1)}, u32[]{:S(2)}, u32[]{:S(2)}) collective-permute-start(bf16[16,4096]{1,0:T(8,128)(2,1)S(1)} %get-tuple-element.7), channel_id=1, source_target_pairs={{0,2},{1,3},{4,0},{5,1},{8,4},{9,5},{12,8},{13,9},{14,12},{15,13},... | collective-permute-start | bytes 393224 | tf_op jit(solution)/shard_map/ppermute | solution.py:301
  82.8 3.8 %collective-permute-start.10 = (bf16[16,4096]{1,0:T(8,128)(2,1)S(1)}, bf16[16,4096]{1,0:T(8,128)(2,1)S(1)}, u32[]{:S(2)}, u32[]{:S(2)}) collective-permute-start(bf16[16,4096]{1,0:T(8,128)(2,1)S(1)} %collective-permute-done.8), channel_id=1, source_target_pairs={{0,4},{1,5},{4,8},{5,9},{8,12},{9,13},{12,14},{13,15},{14,10},{15,... | collective-permute-start | bytes 393224 | tf_op jit(solution)/shard_map/ppermute | solution.py:297
  82.9 3.9 %collective-permute-start.11 = (bf16[16,4096]{1,0:T(8,128)(2,1)S(1)}, bf16[16,4096]{1,0:T(8,128)(2,1)S(1)}, u32[]{:S(2)}, u32[]{:S(2)}) collective-permute-start(bf16[16,4096]{1,0:T(8,128)(2,1)S(1)} %collective-permute-done.9), channel_id=1, source_target_pairs={{0,2},{1,3},{4,0},{5,1},{8,4},{9,5},{12,8},{13,9},{14,12},{15,13},... | collective-permute-start | bytes 393224 | tf_op jit(solution)/shard_map/ppermute | solution.py:301
  86.6 3.8 %collective-permute-start.12 = (bf16[16,4096]{1,0:T(8,128)(2,1)S(1)}, bf16[16,4096]{1,0:T(8,128)(2,1)S(1)}, u32[]{:S(2)}, u32[]{:S(2)}) collective-permute-start(bf16[16,4096]{1,0:T(8,128)(2,1)S(1)} %collective-permute-done.10), channel_id=1, source_target_pairs={{0,4},{1,5},{4,8},{5,9},{8,12},{9,13},{12,14},{13,15},{14,10},{15,... | collective-permute-start | bytes 393224 | tf_op jit(solution)/shard_map/ppermute | solution.py:297
  86.8 4.1 %collective-permute-start.13 = (bf16[16,4096]{1,0:T(8,128)(2,1)S(1)}, bf16[16,4096]{1,0:T(8,128)(2,1)S(1)}, u32[]{:S(2)}, u32[]{:S(2)}) collective-permute-start(bf16[16,4096]{1,0:T(8,128)(2,1)S(1)} %collective-permute-done.11), channel_id=1, source_target_pairs={{0,2},{1,3},{4,0},{5,1},{8,4},{9,5},{12,8},{13,9},{14,12},{15,13},... | collective-permute-start | bytes 393224 | tf_op jit(solution)/shard_map/ppermute | solution.py:301
  90.4 4.5 %collective-permute-start.14 = (bf16[16,4096]{1,0:T(8,128)(2,1)S(1)}, bf16[16,4096]{1,0:T(8,128)(2,1)S(1)}, u32[]{:S(2)}, u32[]{:S(2)}) collective-permute-start(bf16[16,4096]{1,0:T(8,128)(2,1)S(1)} %collective-permute-done.12), channel_id=1, source_target_pairs={{0,4},{1,5},{4,8},{5,9},{8,12},{9,13},{12,14},{13,15},{14,10},{15,... | collective-permute-start | bytes 393224 | tf_op jit(solution)/shard_map/ppermute | solution.py:297
  95.0 17.8 %collective-permute-start.15 = (bf16[8,16,4096]{2,1,0:T(8,128)(2,1)S(1)}, bf16[8,16,4096]{2,1,0:T(8,128)(2,1)S(1)}, u32[]{:S(2)}, u32[]{:S(2)}) collective-permute-start(bf16[8,16,4096]{2,1,0:T(8,128)(2,1)S(1)} %bitcast_dynamic-update-slice_fusion.own_core), channel_id=1, source_target_pairs={{0,1},{1,0},{4,5},{5,4},{8,9},{9,8},{12,13},{13,12},{14,15},{15,14... | collective-permute-start | bytes 3145736 | tf_op jit(solution)/shard_map/ppermute | solution.py:305
  107.0 20.2 %all-to-all-start.1 = ((bf16[16,16,1024]{2,1,0:T(8,128)(2,1)}), bf16[16,16,1024]{2,1,0:T(8,128)(2,1)S(1)}, u32[]{:S(2)}, u32[]{:S(2)}) async-start(bf16[16,16,1024]{2,1,0:T(8,128)(2,1)} %bitcast.133), calls=%async_computation.1 | async-start | bytes 1048576 | tf_op jit(solution)/shard_map/all_to_all | solution.py:259
  127.2 53.6 %all-to-all-start.2 = ((bf16[16,16,16,256]{3,2,1,0:T(8,128)(2,1)}), bf16[16,16,16,256]{3,2,1,0:T(8,128)(2,1)}, u32[]{:S(2)}, u32[]{:S(2)}) async-start(bf16[16,16,16,256]{3,2,1,0:T(8,128)(2,1)} %shard_map.115), calls=%async_computation.2 | async-start | bytes 4194304 | tf_op jit(solution)/shard_map/all_to_all | solution.py:312
  185.6 5.9 %copy-start.1 = (bf16[16,64,64]{2,1,0:T(8,128)(2,1)S(1)}, bf16[16,64,64]{2,1,0:T(8,128)(2,1)}, u32[]{:S(2)}) copy-start(bf16[16,64,64]{2,1,0:T(8,128)(2,1)} %param.11) | copy-start | bytes 393220

commit v3 on v2

--- a/solution.py
+++ b/solution.py
@@ -26,8 +26,9 @@
 
 
 GROUP = 16
-SLOTS = 4
-SPAN = 256
+SLOTS = 3
+SPAN = 512
+TOGETHER = 4
 MIB = 1 << 20
 whole_vmem = pl.BlockSpec(memory_space=pltpu.VMEM)
 
@@ -143,24 +144,30 @@
     pieces, per_device = own_core.shape[:2]
     span = divisor(chol_n, 1024, 256)
 
+    pair = held.shape[1]
+
     def fetch(block, slot):
-        return pltpu.make_async_copy(chol.at[block], held.at[slot], arrived.at[slot])
+        return pltpu.make_async_copy(
+            chol.at[pl.ds(block * pair, pair)], held.at[slot], arrived.at[slot]
+        )
 
     def put(i):
         return pltpu.make_async_copy(built.at[i], out.at[:, i], sent.at[i])
 
-    def work(i, slot):
-        total = jnp.zeros((fields.shape[0], width), f32)
-        for at in range(0, chol_n, span):
-            total += jnp.dot(
-                fields[:, at : at + span],
-                held[slot, at : at + span],
-                preferred_element_type=f32,
-            )
-        built[i] = total.astype(bf16).reshape(built.shape[1:])
-        put(i).start()
-
-    run = stream(rows, fetch, work)
+    def work(block, slot):
+        for a in range(pair):
+            i = block * pair + a
+            total = jnp.zeros((fields.shape[0], width), f32)
+            for at in range(0, chol_n, span):
+                total += jnp.dot(
+                    fields[:, at : at + span],
+                    held[slot, a, at : at + span],
+                    preferred_element_type=f32,
+                )
+            built[i] = total.astype(bf16).reshape(built.shape[1:])
+            put(i).start()
+
+    run = stream(rows // pair, fetch, work)
     for side, piece in enumerate((own_core, other_core)):
         for n in range(pieces):
             at = pl.multiple_of(spots[side * pieces + n] * per_device, per_device)
@@ -184,7 +191,7 @@
             pltpu.VMEM((devices * per_device, chol_n), bf16),
             pltpu.VMEM((rows, devices, per_device, width), bf16),
             pltpu.SemaphoreType.DMA((rows,)),
-            pltpu.VMEM((SLOTS, chol_n, width), bf16),
+            pltpu.VMEM((SLOTS, divisor(rows, 2, 1), chol_n, width), bf16),
             pltpu.SemaphoreType.DMA((SLOTS,)),
         ],
         compiler_params=pltpu.CompilerParams(vmem_limit_bytes=40 * MIB),
@@ -194,6 +201,56 @@
             transcendentals=0,
         ),
     )(spots, own_core, other_core, by_row)
+
+
+def taylor_kernel(got, orbitals, out, propagator):
+    devices, rows, slots, width = got.shape
+    pack = max(1, GROUP // rows)
+    block = pack * rows
+    size = block * slots
+    to = lax.broadcasted_iota(jnp.int32, (size, size), 0)
+    source = lax.broadcasted_iota(jnp.int32, (size, size), 1)
+    regroup = (source == (to % block) * slots + to // block).astype(f32).astype(bf16)
+    for d in range(0, devices, pack):
+        mixed = got[d : d + pack].reshape(size, width)
+        by_slot = jnp.dot(regroup, mixed, preferred_element_type=f32).astype(bf16)
+        propagator[:, d * rows : d * rows + block, :] = by_slot.reshape(slots, block, width)
+    together = divisor(slots, TOGETHER, 1)
+
+    def step(t, carry):
+        at = [t * together + n for n in range(together)]
+        current = [orbitals[k] for k in at]
+        summed = [c.astype(f32) for c in current]
+        for degree in range(1, 5):
+            for n, k in enumerate(at):
+                product = lax.dot_general(
+                    current[n],
+                    propagator[k],
+                    (((1,), (1,)), ((), ())),
+                    preferred_element_type=f32,
+                )
+                current[n] = (root_step / degree * product).astype(bf16)
+                summed[n] = summed[n] + current[n].astype(f32)
+        for n, k in enumerate(at):
+            out[k] = summed[n].astype(bf16)
+        return carry
+
+    lax.fori_loop(0, slots // together, step, 0)
+
+
+def taylor(got, orbitals):
+    devices, rows, slots, width = got.shape
+    return pl.pallas_call(
+        taylor_kernel,
+        in_specs=[whole_vmem] * 2,
+        out_specs=whole_vmem,
+        out_shape=jax.ShapeDtypeStruct(orbitals.shape, bf16),
+        scratch_shapes=[pltpu.VMEM((slots, devices * rows, width), bf16)],
+        compiler_params=pltpu.CompilerParams(vmem_limit_bytes=16 * MIB),
+        cost_estimate=pl.CostEstimate(
+            flops=8 * width * orbitals.size, bytes_accessed=4 * got.size, transcendentals=0
+        ),
+    )(got, orbitals)
 
 
 def local(walkers, inv_intersection, copies, deal, trial, chol, noise):
@@ -260,8 +317,8 @@
         new_rows.reshape(devices, per_device, own_rows * electrons), "row", 0, 0, tiled=True
     )
     orbitals = jnp.transpose(
-        got_rows.reshape(devices, per_device, own_rows, electrons), (1, 0, 2, 3)
-    ).reshape(per_device, orbitals_n, electrons)
+        got_rows.reshape(devices, per_device, own_rows, electrons), (1, 3, 0, 2)
+    ).reshape(per_device, electrons, orbitals_n)
 
     part = bias_parts(parents_of(owner, slot), first, trial.T, by_row)
     part = part.reshape(2, chips, per_device, chol_n)
@@ -310,14 +367,8 @@
     spots = jnp.concatenate([spots + core, spots + 1 - core])
     propagator_part = propagator_parts(spots, own_core, other_core, by_row)
     got = lax.all_to_all(propagator_part, "row", 0, 0, tiled=True)
-    propagator = jnp.transpose(got, (2, 0, 1, 3)).reshape(per_device, orbitals_n, width)
-    current = orbitals
-    summed = orbitals.astype(f32)
-    for degree in range(1, 5):
-        product = jnp.einsum("wik,wkn->win", propagator, current, preferred_element_type=f32)
-        current = (root_step / degree * product).astype(bf16)
-        summed = summed + current.astype(f32)
-    return (summed.astype(bf16), force_bias)
+    propagated = jnp.transpose(taylor(got, orbitals), (0, 2, 1))
+    return (propagated, force_bias)
 
 
 def solution(mesh):

time: 192 us -> 186 us (0.969)
  matrix products: 12.2 us -> 2.53 us
  waiting for transfers between devices: 74.8 us -> 69.1 us
  local copies, waits for them, and re-layouts: 6.19 us -> 10.3 us
  Pallas kernels: 54.4 us -> 57.6 us
    dot_general x4 -> x0, matrix products: 10.7 us -> none  [local(): jnp.einsum('wik,wkn->win', propagator, current, preferred_element_type=f32)]
    pallas_call x0 -> x1, Pallas kernels: none -> 4.58 us  [taylor(): pl.pallas_call(taylor_kernel, in_specs=[whole_vmem] * 2, out_specs=whole_...]
    ppermute x4, starting transfers between devices: 0.76 us -> 4.2 us  [local(): going_right = lax.ppermute(going_right, 'row', right)]
    all_to_all x1, waiting for transfers between devices: 46.2 us -> 42.8 us  [local(): got = lax.all_to_all(propagator_part, 'row', 0, 0, tiled=True)]
    ppermute x4, waiting for transfers between devices: 12.3 us -> 9.27 us  [local(): going_right = lax.ppermute(going_right, 'row', right)]
    ppermute x3, starting transfers between devices: 3.79 us -> 1.5 us  [local(): going_left = lax.ppermute(going_left, 'row', left)]
  transfers between devices with their start and end apart: 19 -> 19, of which waited for: 15 -> 15; matrix products, arithmetic and copies ran while one was open for 3% -> 4% of each run, Pallas kernels for 21% -> 22%
where the time goes in v3:
time: 186 us; the launch traced here: 185 us
  waiting for transfers between devices  69.1 us (37%)
  Pallas kernels  57.6 us (31%)
  starting transfers between devices  40.2 us (22%)
  local copies, waits for them, and re-layouts  10.3 us (6%)
  other arithmetic  4.63 us (2%)
  matrix products  2.53 us (1%)
    all_to_all x1, waiting for transfers between devices, local(): got = lax.all_to_all(propagator_part, 'row', 0, 0, tiled=True)  42.8 us
    pallas_call x1, Pallas kernels, chol_by_row(): pl.pallas_call(by_row_kernel, grid=(chol_n // depth,), in_specs=[pl.Block...  25.8 us
    pallas_call x1, Pallas kernels, propagator_parts(): pl.pallas_call(propagator_kernel, in_specs=[pl.BlockSpec(memory_space=plt...  14.1 us
    pallas_call x1, Pallas kernels, bias_parts(): pl.pallas_call(bias_kernel, in_specs=[whole_vmem] * 3 + [pl.BlockSpec(mem...  13.2 us
    ppermute x4, waiting for transfers between devices, local(): moving_right = lax.ppermute(moving_right, 'row', right)  11.4 us
    ppermute x1, starting transfers between devices, local(): other_core = lax.ppermute(own_core, 'row', swap)  9.29 us
    ppermute x4, waiting for transfers between devices, local(): going_right = lax.ppermute(going_right, 'row', right)  9.27 us
    all_to_all x1, starting transfers between devices, local(): lax.all_to_all(new_rows.reshape(devices, per_device, own_rows * electrons...  7.34 us
  transfers between devices with their start and end apart: 19, of which 15 were waited for; matrix products, arithmetic and copies ran while one was open for 4% of the time, Pallas kernels for 22%

profile of v3, /device:TPU:15, one launch (start us, length us, event | category | flops | bytes accessed | tf_op | source)
XLA Modules:
  0.0 185.3 jit_solution(14196041104171278442)
XLA Ops:
  0.6 0.7 convert_element_type.173
  1.3 1.5 copy.27
  2.9 1.4 convolution_convert_fusion
  4.3 0.5 copy.26
  4.8 0.7 reshape.140
  5.5 0.7 reshape.141
  6.2 0.1 broadcast_in_dim.81
  6.3 0.1 pad_maximum_fusion
  6.4 1.2 copy.28
  7.6 6.6 %all-to-all-start = ((bf16[16,16,2176]{2,1,0:T(8,128)(2,1)}), bf16[16,16,2176]{2,1,0:T(8,128)(2,1)S(1)}, u32[]{:S(2)}, u32[]{:S(2)}) async-start(bf16[16,16,2176]{2,1,0:T(8,128)(2,1)} %copy.28), calls=%async_computation | async-start | bytes 2228224 | tf_op jit(solution)/shard_map/all_to_all | solution.py:278
  14.2 0.6 fusion.31
  14.8 0.7 and_select_fusion.1
  15.5 0.1 select_reduce_fusion.4
  15.6 0.1 select_reduce_fusion.2
  15.7 25.8 %shard_map.113.chol = bf16[16,4096,256]{2,1,0:T(8,128)(2,1)} custom-call(bf16[4096,16,256]{2,1,0:T(8,128)(2,1)} %chol.1), custom_call_target="tpu_custom_call" | custom-call | flops 8589934592 | bytes 67108864 | tf_op jit(solution)/shard_map/pallas_call | solution.py:56
  41.5 0.1 convert_reduce_fusion
  41.6 0.1 select_reduce_fusion.1
  41.8 0.1 and_convert_fusion.pick
  41.9 13.2 %shard_map.114 = bf16[256,4096]{1,0:T(8,128)(2,1)S(1)} custom-call(bf16[256,256]{1,0:T(8,128)(2,1)S(1)} %and_convert_fusion.pick, bf16[256,2176]{1,0:T(8,128)(2,1)S(1)} %bitcast.116, bf16[64,256]{1,0:T(8,128)(2,1)S(1)} %bitcast.118, bf16[16,4096,256]{2,1,0:T(8,128)(2,1)} %shard_map.113.chol), custom_call_target="tpu_custom_call" | custom-call | flops 8589934592 | bytes 33554432 | tf_op jit(solution)/shard_map/pallas_call | solution.py:123
  55.1 0.1 slice.91
  55.2 0.4 collective-permute-start
  55.6 2.3 %collective-permute-done = bf16[8,16,4096]{2,1,0:T(8,128)(2,1)S(1)} collective-permute-done((bf16[8,16,4096]{2,1,0:T(8,128)(2,1)S(1)}, bf16[8,16,4096]{2,1,0:T(8,128)(2,1)S(1)}, u32[]{:S(2)}, u32[]{:S(2)}) %collective-permute-start) | collective-permute-done | bytes 1048608 | tf_op jit(solution)/shard_map/ppermute | solution.py:329
  57.9 0.3 collective-permute-start.1
  58.3 4.4 %collective-permute-done.1 = bf16[16,4096]{1,0:T(8,128)(2,1)S(1)} collective-permute-done((bf16[16,4096]{1,0:T(8,128)(2,1)S(1)}, bf16[16,4096]{1,0:T(8,128)(2,1)S(1)}, u32[]{:S(2)}, u32[]{:S(2)}) %collective-permute-start.1) | collective-permute-done | bytes 131104 | tf_op jit(solution)/shard_map/ppermute | solution.py:338
  62.8 0.3 collective-permute-start.2
  63.1 1.2 collective-permute-start.5
  64.3 2.4 %collective-permute-done.2 = bf16[16,4096]{1,0:T(8,128)(2,1)S(1)} collective-permute-done((bf16[16,4096]{1,0:T(8,128)(2,1)S(1)}, bf16[16,4096]{1,0:T(8,128)(2,1)S(1)}, u32[]{:S(2)}, u32[]{:S(2)}) %collective-permute-start.2) | collective-permute-done | bytes 131104 | tf_op jit(solution)/shard_map/ppermute | solution.py:338
  66.7 0.6 collective-permute-done.5
  67.2 0.1 fusion.9
  67.3 0.4 collective-permute-start.3
  67.7 1.2 collective-permute-start.6
  68.9 2.3 %collective-permute-done.3 = bf16[16,4096]{1,0:T(8,128)(2,1)S(1)} collective-permute-done((bf16[16,4096]{1,0:T(8,128)(2,1)S(1)}, bf16[16,4096]{1,0:T(8,128)(2,1)S(1)}, u32[]{:S(2)}, u32[]{:S(2)}) %collective-permute-start.3) | collective-permute-done | bytes 131104 | tf_op jit(solution)/shard_map/ppermute | solution.py:338
  71.2 0.3 collective-permute-done.6
  71.5 0.1 fusion.7
  71.6 1.6 collective-permute-start.4
  73.2 2.3 %collective-permute-done.4 = bf16[16,4096]{1,0:T(8,128)(2,1)S(1)} collective-permute-done((bf16[16,4096]{1,0:T(8,128)(2,1)S(1)}, bf16[16,4096]{1,0:T(8,128)(2,1)S(1)}, u32[]{:S(2)}, u32[]{:S(2)}) %collective-permute-start.4) | collective-permute-done | bytes 131104 | tf_op jit(solution)/shard_map/ppermute | solution.py:338
  75.5 1.5 collective-permute-done.7
  77.0 0.8 bitcast_dynamic-update-slice_fusion.7
  77.8 0.8 collective-permute-start.8
  78.6 0.6 collective-permute-start.9
  79.3 2.4 %collective-permute-done.8 = bf16[16,4096]{1,0:T(8,128)(2,1)S(1)} collective-permute-done((bf16[16,4096]{1,0:T(8,128)(2,1)S(1)}, bf16[16,4096]{1,0:T(8,128)(2,1)S(1)}, u32[]{:S(2)}, u32[]{:S(2)}) %collective-permute-start.8) | collective-permute-done | bytes 131104 | tf_op jit(solution)/shard_map/ppermute | solution.py:354
  81.6 1.1 collective-permute-start.10
  82.7 0.5 collective-permute-start.11
  83.2 2.3 %collective-permute-done.10 = bf16[16,4096]{1,0:T(8,128)(2,1)S(1)} collective-permute-done((bf16[16,4096]{1,0:T(8,128)(2,1)S(1)}, bf16[16,4096]{1,0:T(8,128)(2,1)S(1)}, u32[]{:S(2)}, u32[]{:S(2)}) %collective-permute-start.10) | collective-permute-done | bytes 131104 | tf_op jit(solution)/shard_map/ppermute | solution.py:354
  85.4 1.1 collective-permute-start.12
  86.5 0.4 collective-permute-done.11
  86.9 0.4 collective-permute-start.13
  87.3 2.0 %collective-permute-done.12 = bf16[16,4096]{1,0:T(8,128)(2,1)S(1)} collective-permute-done((bf16[16,4096]{1,0:T(8,128)(2,1)S(1)}, bf16[16,4096]{1,0:T(8,128)(2,1)S(1)}, u32[]{:S(2)}, u32[]{:S(2)}) %collective-permute-start.12) | collective-permute-done | bytes 131104 | tf_op jit(solution)/shard_map/ppermute | solution.py:354
  89.2 1.2 collective-permute-start.14
  90.5 0.5 collective-permute-done.13
  91.0 2.7 %collective-permute-done.14 = bf16[16,4096]{1,0:T(8,128)(2,1)S(1)} collective-permute-done((bf16[16,4096]{1,0:T(8,128)(2,1)S(1)}, bf16[16,4096]{1,0:T(8,128)(2,1)S(1)}, u32[]{:S(2)}, u32[]{:S(2)}) %collective-permute-start.14) | collective-permute-done | bytes 131104 | tf_op jit(solution)/shard_map/ppermute | solution.py:354
  93.7 9.3 %collective-permute-start.15 = (bf16[8,16,4096]{2,1,0:T(8,128)(2,1)S(1)}, bf16[8,16,4096]{2,1,0:T(8,128)(2,1)S(1)}, u32[]{:S(2)}, u32[]{:S(2)}) collective-permute-start(bf16[8,16,4096]{2,1,0:T(8,128)(2,1)S(1)} %bitcast_dynamic-update-slice_fusion.own_core), channel_id=1, source_target_pairs={{0,1},{1,0},{4,5},{5,4},{8,9},{9,8},{12,13},{13,12},{14,15},{15,14... | collective-permute-start | bytes 3145736 | tf_op jit(solution)/shard_map/ppermute | solution.py:362
  103.0 0.7 and_select_fusion.5
  103.6 0.2 select_reduce_fusion.5
  103.8 1.1 convolution_convert_fusion.1
  105.0 7.3 %all-to-all-start.2 = ((bf16[16,16,1024]{2,1,0:T(8,128)(2,1)}), bf16[16,16,1024]{2,1,0:T(8,128)(2,1)S(1)}, u32[]{:S(2)}, u32[]{:S(2)}) async-start(bf16[16,16,1024]{2,1,0:T(8,128)(2,1)} %bitcast.124), calls=%async_computation.2 | async-start | bytes 1048576 | tf_op jit(solution)/shard_map/all_to_all | solution.py:316
  112.4 14.1 %shard_map.115 = bf16[16,16,16,256]{3,2,1,0:T(8,128)(2,1)} custom-call(s32[16]{0:T(128)S(1)} %pad_add_fusion.spots, bf16[8,16,4096]{2,1,0:T(8,128)(2,1)S(1)} %bitcast_dynamic-update-slice_fusion.own_core, bf16[8,16,4096]{2,1,0:T(8,128)(2,1)S(1)} %collective-permute-done.15.other_core, bf16[16,4096,256]{2,1,0:T(8,128)(2,1)} %shard_map.113.chol), custom_call_target="tpu_custom_call" | custom-call | flops 8589934592 | bytes 33554432 | tf_op jit(solution)/shard_map/pallas_call | solution.py:185
  126.5 0.8 copy-done.3
  127.3 6.0 %all-to-all-start.1 = ((bf16[16,16,16,256]{3,2,1,0:T(8,128)(2,1)}), bf16[16,16,16,256]{3,2,1,0:T(8,128)(2,1)S(1)}, u32[]{:S(2)}, u32[]{:S(2)}) async-start(bf16[16,16,16,256]{3,2,1,0:T(8,128)(2,1)} %shard_map.115), calls=%async_computation.1 | async-start | bytes 4194304 | tf_op jit(solution)/shard_map/all_to_all | solution.py:369
  133.3 1.8 reshape.145
  135.1 1.3 copy.29
  136.3 1.6 copy.30.orbitals
  137.9 42.8 %all-to-all-done.1.got = bf16[16,16,16,256]{3,2,1,0:T(8,128)(2,1)S(1)} async-done(((bf16[16,16,16,256]{3,2,1,0:T(8,128)(2,1)}), bf16[16,16,16,256]{3,2,1,0:T(8,128)(2,1)S(1)}, u32[]{:S(2)}, u32[]{:S(2)}) %all-to-all-start.1) | async-done | bytes 2097184 | tf_op jit(solution)/shard_map/all_to_all | solution.py:369
  180.7 4.6 %shard_map.116 = bf16[16,64,256]{2,1,0:T(8,128)(2,1)} custom-call(bf16[16,16,16,256]{3,2,1,0:T(8,128)(2,1)S(1)} %all-to-all-done.1.got, bf16[16,64,256]{2,1,0:T(8,128)(2,1)S(1)} %copy.30.orbitals), custom_call_target="tpu_custom_call" | custom-call | flops 536870912 | bytes 4194304 | tf_op jit(solution)/shard_map/pallas_call | solution.py:243
  (37 shorter events, 0.4 us)
Async XLA Ops:
  0.6 2.2 %copy-start = (bf16[16,64,64]{2,1,0:T(8,128)(2,1)S(1)}, bf16[16,64,64]{2,1,0:T(8,128)(2,1)}, u32[]{:S(2)}) copy-start(bf16[16,64,64]{2,1,0:T(8,128)(2,1)} %param.11) | copy-start | bytes 393220
  6.4 7.8 %copy-start.7 = (s32[8]{0:T(128)S(1)}, s32[8]{0:T(128)}, u32[]{:S(2)}) copy-start(s32[8]{0:T(128)} %constant.118.clone) | copy-start | bytes 100
  6.4 9.1 %copy-start.5 = (s32[8]{0:T(128)S(1)}, s32[8]{0:T(128)}, u32[]{:S(2)}) copy-start(s32[8]{0:T(128)} %constant.117.clone) | copy-start | bytes 100
  6.4 9.2 %copy-start.6 = (s32[16]{0:T(128)S(1)}, s32[16]{0:T(128)}, u32[]{:S(2)}) copy-start(s32[16]{0:T(128)} %param.13) | copy-start | bytes 196
  7.6 33.9 %all-to-all-start = ((bf16[16,16,2176]{2,1,0:T(8,128)(2,1)}), bf16[16,16,2176]{2,1,0:T(8,128)(2,1)S(1)}, u32[]{:S(2)}, u32[]{:S(2)}) async-start(bf16[16,16,2176]{2,1,0:T(8,128)(2,1)} %copy.28), calls=%async_computation | async-start | bytes 2228224 | tf_op jit(solution)/shard_map/all_to_all | solution.py:278
  15.7 26.2 %copy-start.2 = (bf16[256,64]{0,1:T(8,128)(2,1)S(1)}, bf16[256,64]{0,1:T(8,128)(2,1)}, u32[]{:S(2)}) copy-start(bf16[256,64]{0,1:T(8,128)(2,1)} %param.14) | copy-start | bytes 98308
  55.2 21.8 %copy-start.4 = (f32[16,4096]{1,0:T(8,128)S(1)}, f32[16,4096]{1,0:T(8,128)}, u32[]{:S(2)}) copy-start(f32[16,4096]{1,0:T(8,128)} %param.16) | copy-start | bytes 786436
  55.2 2.7 %collective-permute-start = (bf16[8,16,4096]{2,1,0:T(8,128)(2,1)S(1)}, bf16[8,16,4096]{2,1,0:T(8,128)(2,1)S(1)}, u32[]{:S(2)}, u32[]{:S(2)}) collective-permute-start(bf16[8,16,4096]{2,1,0:T(8,128)(2,1)S(1)} %bitcast.123), channel_id=1, source_target_pairs={{0,1},{1,0},{4,5},{5,4},{8,9},{9,8},{12,13},{13,12},{14,15},{15,14... | collective-permute-start | bytes 3145736 | tf_op jit(solution)/shard_map/ppermute | solution.py:329
  57.9 4.8 %collective-permute-start.1 = (bf16[16,4096]{1,0:T(8,128)(2,1)S(1)}, bf16[16,4096]{1,0:T(8,128)(2,1)S(1)}, u32[]{:S(2)}, u32[]{:S(2)}) collective-permute-start(bf16[16,4096]{1,0:T(8,128)(2,1)S(1)} %fusion.12), channel_id=1, source_target_pairs={{0,4},{1,5},{4,8},{5,9},{8,12},{9,13},{12,14},{13,15},{14,10},{15,... | collective-permute-start | bytes 393224 | tf_op jit(solution)/shard_map/ppermute | solution.py:338
  62.8 3.9 %collective-permute-start.2 = (bf16[16,4096]{1,0:T(8,128)(2,1)S(1)}, bf16[16,4096]{1,0:T(8,128)(2,1)S(1)}, u32[]{:S(2)}, u32[]{:S(2)}) collective-permute-start(bf16[16,4096]{1,0:T(8,128)(2,1)S(1)} %get-tuple-element.13), channel_id=1, source_target_pairs={{0,4},{1,5},{4,8},{5,9},{8,12},{9,13},{12,14},{13,15},{14,10},{15,... | collective-permute-start | bytes 393224 | tf_op jit(solution)/shard_map/ppermute | solution.py:338
  63.1 4.1 %collective-permute-start.5 = (bf16[16,4096]{1,0:T(8,128)(2,1)S(1)}, bf16[16,4096]{1,0:T(8,128)(2,1)S(1)}, u32[]{:S(2)}, u32[]{:S(2)}) collective-permute-start(bf16[16,4096]{1,0:T(8,128)(2,1)S(1)} %get-tuple-element.14), channel_id=1, source_target_pairs={{0,2},{1,3},{4,0},{5,1},{8,4},{9,5},{12,8},{13,9},{14,12},{15,13},... | collective-permute-start | bytes 393224 | tf_op jit(solution)/shard_map/ppermute | solution.py:340
  67.3 3.9 %collective-permute-start.3 = (bf16[16,4096]{1,0:T(8,128)(2,1)S(1)}, bf16[16,4096]{1,0:T(8,128)(2,1)S(1)}, u32[]{:S(2)}, u32[]{:S(2)}) collective-permute-start(bf16[16,4096]{1,0:T(8,128)(2,1)S(1)} %get-tuple-element.11), channel_id=1, source_target_pairs={{0,4},{1,5},{4,8},{5,9},{8,12},{9,13},{12,14},{13,15},{14,10},{15,... | collective-permute-start | bytes 393224 | tf_op jit(solution)/shard_map/ppermute | solution.py:338
  67.7 35.3 %copy-start.8 = (s32[8]{0:T(128)S(1)}, s32[8]{0:T(128)}, u32[]{:S(2)}) copy-start(s32[8]{0:T(128)} %constant.119.clone) | copy-start | bytes 100
  67.7 3.8 %collective-permute-start.6 = (bf16[16,4096]{1,0:T(8,128)(2,1)S(1)}, bf16[16,4096]{1,0:T(8,128)(2,1)S(1)}, u32[]{:S(2)}, u32[]{:S(2)}) collective-permute-start(bf16[16,4096]{1,0:T(8,128)(2,1)S(1)} %get-tuple-element.12), channel_id=1, source_target_pairs={{0,2},{1,3},{4,0},{5,1},{8,4},{9,5},{12,8},{13,9},{14,12},{15,13},... | collective-permute-start | bytes 393224 | tf_op jit(solution)/shard_map/ppermute | solution.py:340
  71.6 3.9 %collective-permute-start.4 = (bf16[16,4096]{1,0:T(8,128)(2,1)S(1)}, bf16[16,4096]{1,0:T(8,128)(2,1)S(1)}, u32[]{:S(2)}, u32[]{:S(2)}) collective-permute-start(bf16[16,4096]{1,0:T(8,128)(2,1)S(1)} %get-tuple-element.9), channel_id=1, source_target_pairs={{0,4},{1,5},{4,8},{5,9},{8,12},{9,13},{12,14},{13,15},{14,10},{15,... | collective-permute-start | bytes 393224 | tf_op jit(solution)/shard_map/ppermute | solution.py:338
  73.2 3.8 %collective-permute-start.7 = (bf16[16,4096]{1,0:T(8,128)(2,1)S(1)}, bf16[16,4096]{1,0:T(8,128)(2,1)S(1)}, u32[]{:S(2)}, u32[]{:S(2)}) collective-permute-start(bf16[16,4096]{1,0:T(8,128)(2,1)S(1)} %get-tuple-element.10), channel_id=1, source_target_pairs={{0,2},{1,3},{4,0},{5,1},{8,4},{9,5},{12,8},{13,9},{14,12},{15,13},... | collective-permute-start | bytes 393224 | tf_op jit(solution)/shard_map/ppermute | solution.py:340
  77.8 3.8 %collective-permute-start.8 = (bf16[16,4096]{1,0:T(8,128)(2,1)S(1)}, bf16[16,4096]{1,0:T(8,128)(2,1)S(1)}, u32[]{:S(2)}, u32[]{:S(2)}) collective-permute-start(bf16[16,4096]{1,0:T(8,128)(2,1)S(1)} %get-tuple-element.7), channel_id=1, source_target_pairs={{0,4},{1,5},{4,8},{5,9},{8,12},{9,13},{12,14},{13,15},{14,10},{15,... | collective-permute-start | bytes 393224 | tf_op jit(solution)/shard_map/ppermute | solution.py:354
  78.6 4.0 %collective-permute-start.9 = (bf16[16,4096]{1,0:T(8,128)(2,1)S(1)}, bf16[16,4096]{1,0:T(8,128)(2,1)S(1)}, u32[]{:S(2)}, u32[]{:S(2)}) collective-permute-start(bf16[16,4096]{1,0:T(8,128)(2,1)S(1)} %get-tuple-element.7), channel_id=1, source_target_pairs={{0,2},{1,3},{4,0},{5,1},{8,4},{9,5},{12,8},{13,9},{14,12},{15,13},... | collective-permute-start | bytes 393224 | tf_op jit(solution)/shard_map/ppermute | solution.py:358
  81.6 3.8 %collective-permute-start.10 = (bf16[16,4096]{1,0:T(8,128)(2,1)S(1)}, bf16[16,4096]{1,0:T(8,128)(2,1)S(1)}, u32[]{:S(2)}, u32[]{:S(2)}) collective-permute-start(bf16[16,4096]{1,0:T(8,128)(2,1)S(1)} %collective-permute-done.8), channel_id=1, source_target_pairs={{0,4},{1,5},{4,8},{5,9},{8,12},{9,13},{12,14},{13,15},{14,10},{15,... | collective-permute-start | bytes 393224 | tf_op jit(solution)/shard_map/ppermute | solution.py:354
  82.7 4.2 %collective-permute-start.11 = (bf16[16,4096]{1,0:T(8,128)(2,1)S(1)}, bf16[16,4096]{1,0:T(8,128)(2,1)S(1)}, u32[]{:S(2)}, u32[]{:S(2)}) collective-permute-start(bf16[16,4096]{1,0:T(8,128)(2,1)S(1)} %collective-permute-done.9), channel_id=1, source_target_pairs={{0,2},{1,3},{4,0},{5,1},{8,4},{9,5},{12,8},{13,9},{14,12},{15,13},... | collective-permute-start | bytes 393224 | tf_op jit(solution)/shard_map/ppermute | solution.py:358
  85.4 3.8 %collective-permute-start.12 = (bf16[16,4096]{1,0:T(8,128)(2,1)S(1)}, bf16[16,4096]{1,0:T(8,128)(2,1)S(1)}, u32[]{:S(2)}, u32[]{:S(2)}) collective-permute-start(bf16[16,4096]{1,0:T(8,128)(2,1)S(1)} %collective-permute-done.10), channel_id=1, source_target_pairs={{0,4},{1,5},{4,8},{5,9},{8,12},{9,13},{12,14},{13,15},{14,10},{15,... | collective-permute-start | bytes 393224 | tf_op jit(solution)/shard_map/ppermute | solution.py:354
  86.9 4.1 %collective-permute-start.13 = (bf16[16,4096]{1,0:T(8,128)(2,1)S(1)}, bf16[16,4096]{1,0:T(8,128)(2,1)S(1)}, u32[]{:S(2)}, u32[]{:S(2)}) collective-permute-start(bf16[16,4096]{1,0:T(8,128)(2,1)S(1)} %collective-permute-done.11), channel_id=1, source_target_pairs={{0,2},{1,3},{4,0},{5,1},{8,4},{9,5},{12,8},{13,9},{14,12},{15,13},... | collective-permute-start | bytes 393224 | tf_op jit(solution)/shard_map/ppermute | solution.py:358
  89.2 4.4 %collective-permute-start.14 = (bf16[16,4096]{1,0:T(8,128)(2,1)S(1)}, bf16[16,4096]{1,0:T(8,128)(2,1)S(1)}, u32[]{:S(2)}, u32[]{:S(2)}) collective-permute-start(bf16[16,4096]{1,0:T(8,128)(2,1)S(1)} %collective-permute-done.12), channel_id=1, source_target_pairs={{0,4},{1,5},{4,8},{5,9},{8,12},{9,13},{12,14},{13,15},{14,10},{15,... | collective-permute-start | bytes 393224 | tf_op jit(solution)/shard_map/ppermute | solution.py:354
  93.7 18.7 %collective-permute-start.15 = (bf16[8,16,4096]{2,1,0:T(8,128)(2,1)S(1)}, bf16[8,16,4096]{2,1,0:T(8,128)(2,1)S(1)}, u32[]{:S(2)}, u32[]{:S(2)}) collective-permute-start(bf16[8,16,4096]{2,1,0:T(8,128)(2,1)S(1)} %bitcast_dynamic-update-slice_fusion.own_core), channel_id=1, source_target_pairs={{0,1},{1,0},{4,5},{5,4},{8,9},{9,8},{12,13},{13,12},{14,15},{15,14... | collective-permute-start | bytes 3145736 | tf_op jit(solution)/shard_map/ppermute | solution.py:362
  105.0 21.5 %all-to-all-start.2 = ((bf16[16,16,1024]{2,1,0:T(8,128)(2,1)}), bf16[16,16,1024]{2,1,0:T(8,128)(2,1)S(1)}, u32[]{:S(2)}, u32[]{:S(2)}) async-start(bf16[16,16,1024]{2,1,0:T(8,128)(2,1)} %bitcast.124), calls=%async_computation.2 | async-start | bytes 1048576 | tf_op jit(solution)/shard_map/all_to_all | solution.py:316
  126.5 0.8 copy-start.3
  127.3 53.4 %all-to-all-start.1 = ((bf16[16,16,16,256]{3,2,1,0:T(8,128)(2,1)}), bf16[16,16,16,256]{3,2,1,0:T(8,128)(2,1)S(1)}, u32[]{:S(2)}, u32[]{:S(2)}) async-start(bf16[16,16,16,256]{3,2,1,0:T(8,128)(2,1)} %shard_map.115), calls=%async_computation.1 | async-start | bytes 4194304 | tf_op jit(solution)/shard_map/all_to_all | solution.py:369
  136.3 49.0 %copy-start.1 = (bf16[16,64,64]{2,1,0:T(8,128)(2,1)S(1)}, bf16[16,64,64]{2,1,0:T(8,128)(2,1)}, u32[]{:S(2)}) copy-start(bf16[16,64,64]{2,1,0:T(8,128)(2,1)} %param.11) | copy-start | bytes 393220

commit v4 on v3

--- a/solution.py
+++ b/solution.py
@@ -28,9 +28,14 @@
 GROUP = 16
 SLOTS = 3
 SPAN = 512
-TOGETHER = 4
+TOGETHER = 8
+PAYLOAD_MIB = 56
+DEPTH = 4096
+HELD = 5
+MADE = 4
 MIB = 1 << 20
 whole_vmem = pl.BlockSpec(memory_space=pltpu.VMEM)
+in_hbm = pl.BlockSpec(memory_space=pltpu.HBM)
 
 
 def divisor(n, most, unit):
@@ -38,27 +43,81 @@
     return fits[-1] if fits else n
 
 
-def by_row_kernel(chol, out):
-    depth, rows, width = chol.shape
+def stream(blocks, slots, fetch, work):
+    first = min(slots - 1, blocks)
+    for block in range(first):
+        fetch(block, block).start()
+
+    def run():
+        def step(block, carry):
+            slot = lax.rem(block, slots)
+
+            @pl.when(block + slots - 1 < blocks)
+            def _():
+                fetch(block + slots - 1, lax.rem(block + slots - 1, slots)).start()
+
+            fetch(block, slot).wait()
+            work(block, slot)
+            return carry
+
+        lax.fori_loop(0, blocks, step, 0)
+
+    return run
+
+
+def by_row_kernel(chol, out, held, arrived, made, left):
+    chol_n, rows, width = chol.shape
+    depth = held.shape[1]
+    outs = made.shape[0]
+    blocks = chol_n // depth
+
+    def fetch(block, slot):
+        return pltpu.make_async_copy(
+            chol.at[pl.ds(block * depth, depth)], held.at[slot], arrived.at[slot]
+        )
+
+    def put(block, slot):
+        return pltpu.make_async_copy(
+            made.at[slot], out.at[:, pl.ds(block * depth, depth)], left.at[slot]
+        )
+
     size = GROUP * rows
     to = lax.broadcasted_iota(jnp.int32, (size, size), 0)
     source = lax.broadcasted_iota(jnp.int32, (size, size), 1)
     regroup = (to == (source % rows) * GROUP + source // rows).astype(f32).astype(bf16)
-    for at in range(0, depth, GROUP):
-        mixed = chol[at : at + GROUP].reshape(size, width)
-        sorted_rows = jnp.dot(regroup, mixed, preferred_element_type=f32).astype(bf16)
-        out[:, at : at + GROUP, :] = sorted_rows.reshape(rows, GROUP, width)
+
+    def work(block, slot):
+        place = lax.rem(block, outs)
+
+        @pl.when(block >= outs)
+        def _():
+            put(block - outs, place).wait()
+
+        for at in range(0, depth, GROUP):
+            mixed = held[slot, at : at + GROUP].reshape(size, width)
+            sorted_rows = jnp.dot(regroup, mixed, preferred_element_type=f32).astype(bf16)
+            made[place, :, at : at + GROUP, :] = sorted_rows.reshape(rows, GROUP, width)
+        put(block, place).start()
+
+    stream(blocks, held.shape[0], fetch, work)()
+    for block in range(max(0, blocks - outs), blocks):
+        put(block, block % outs).wait()
 
 
 def chol_by_row(chol):
     chol_n, rows, width = chol.shape
-    depth = divisor(chol_n, 8192 // rows, GROUP)
+    depth = divisor(chol_n, DEPTH // rows, GROUP)
     return pl.pallas_call(
         by_row_kernel,
-        grid=(chol_n // depth,),
-        in_specs=[pl.BlockSpec((depth, rows, width), lambda t: (t, 0, 0))],
-        out_specs=pl.BlockSpec((rows, depth, width), lambda t: (0, t, 0)),
+        in_specs=[in_hbm],
+        out_specs=in_hbm,
         out_shape=jax.ShapeDtypeStruct((rows, chol_n, width), bf16),
+        scratch_shapes=[
+            pltpu.VMEM((HELD, depth, rows, width), bf16),
+            pltpu.SemaphoreType.DMA((HELD,)),
+            pltpu.VMEM((MADE, rows, depth, width), bf16),
+            pltpu.SemaphoreType.DMA((MADE,)),
+        ],
         compiler_params=pltpu.CompilerParams(vmem_limit_bytes=40 * MIB),
         cost_estimate=pl.CostEstimate(
             flops=2 * chol.size * GROUP * rows, bytes_accessed=4 * chol.size, transcendentals=0
@@ -66,31 +125,10 @@
     )(chol)
 
 
-def stream(blocks, fetch, work):
-    first = min(SLOTS - 1, blocks)
-    for block in range(first):
-        fetch(block, block).start()
-
-    def run():
-        def step(block, carry):
-            slot = lax.rem(block, SLOTS)
-
-            @pl.when(block + SLOTS - 1 < blocks)
-            def _():
-                fetch(block + SLOTS - 1, lax.rem(block + SLOTS - 1, SLOTS)).start()
-
-            fetch(block, slot).wait()
-            work(block, slot)
-            return carry
-
-        lax.fori_loop(0, blocks, step, 0)
-
-    return run
-
-
-def bias_kernel(pick, theta, trial, chol, out, density, held, arrived):
+def bias_kernel(pick, first, trial, chol, out, density, held, arrived):
     rows, chol_n, width = chol.shape
     electrons = trial.shape[0]
+    everyone = out.shape[0]
     span = held.shape[2]
 
     def fetch(block, slot):
@@ -98,31 +136,30 @@
         return pltpu.make_async_copy(chol.at[:, here], held.at[slot], arrived.at[slot])
 
     def work(block, slot):
-        total = jnp.zeros((pick.shape[0], span), f32)
+        total = jnp.zeros((everyone, span), f32)
         for i in range(rows):
             total += lax.dot_general(
                 density[i], held[slot, i], (((1,), (1,)), ((), ())), preferred_element_type=f32
             )
         out[:, pl.ds(pl.multiple_of(block * span, span), span)] = total.astype(bf16)
 
-    run = stream(chol_n // span, fetch, work)
-    picked = jnp.dot(
-        pick[...], theta[:, : rows * electrons], preferred_element_type=f32
-    ).astype(bf16)
+    run = stream(chol_n // span, SLOTS, fetch, work)
     for i in range(rows):
+        held_rows = first[:, i].reshape(everyone, 2 * electrons)
+        picked = jnp.dot(pick[...], held_rows, preferred_element_type=f32).astype(bf16)
         density[i] = jnp.dot(
-            picked[:, i * electrons : (i + 1) * electrons], trial[...], preferred_element_type=f32
+            picked[:, :electrons], trial[...], preferred_element_type=f32
         ).astype(bf16)
     run()
 
 
-def bias_parts(pick, theta, trial, by_row):
+def bias_parts(pick, first, trial, by_row):
     rows, chol_n, width = by_row.shape
     everyone = pick.shape[0]
     span = divisor(chol_n, SPAN, 128)
     return pl.pallas_call(
         bias_kernel,
-        in_specs=[whole_vmem] * 3 + [pl.BlockSpec(memory_space=pl.ANY)],
+        in_specs=[whole_vmem] * 3 + [in_hbm],
         out_specs=whole_vmem,
         out_shape=jax.ShapeDtypeStruct((everyone, chol_n), bf16),
         scratch_shapes=[
@@ -130,11 +167,11 @@
             pltpu.VMEM((SLOTS, rows, span, width), bf16),
             pltpu.SemaphoreType.DMA((SLOTS,)),
         ],
-        compiler_params=pltpu.CompilerParams(vmem_limit_bytes=40 * MIB),
+        compiler_params=pltpu.CompilerParams(vmem_limit_bytes=24 * MIB),
         cost_estimate=pl.CostEstimate(
             flops=2 * everyone * by_row.size, bytes_accessed=2 * by_row.size, transcendentals=0
         ),
-    )(pick, theta, trial, by_row)
+    )(pick, first, trial, by_row)
 
 
 def propagator_kernel(
@@ -167,7 +204,7 @@
             built[i] = total.astype(bf16).reshape(built.shape[1:])
             put(i).start()
 
-    run = stream(rows // pair, fetch, work)
+    run = stream(rows // pair, SLOTS, fetch, work)
     for side, piece in enumerate((own_core, other_core)):
         for n in range(pieces):
             at = pl.multiple_of(spots[side * pieces + n] * per_device, per_device)
@@ -181,7 +218,6 @@
     rows, chol_n, width = by_row.shape
     chips, per_device, _ = own_core.shape
     devices = 2 * chips
-    in_hbm = pl.BlockSpec(memory_space=pl.ANY)
     return pl.pallas_call(
         propagator_kernel,
         in_specs=[pl.BlockSpec(memory_space=pltpu.SMEM), whole_vmem, whole_vmem, in_hbm],
@@ -194,13 +230,113 @@
             pltpu.VMEM((SLOTS, divisor(rows, 2, 1), chol_n, width), bf16),
             pltpu.SemaphoreType.DMA((SLOTS,)),
         ],
-        compiler_params=pltpu.CompilerParams(vmem_limit_bytes=40 * MIB),
+        compiler_params=pltpu.CompilerParams(vmem_limit_bytes=24 * MIB),
         cost_estimate=pl.CostEstimate(
             flops=2 * devices * per_device * by_row.size,
             bytes_accessed=2 * by_row.size,
             transcendentals=0,
         ),
     )(spots, own_core, other_core, by_row)
+
+
+def move_kernel(pick, first, moved):
+    devices, groups, slots, lanes = moved.shape
+    everyone, both = devices * slots, first.shape[3]
+    together = 2 * lanes // both
+    for group in range(groups):
+        gone = []
+        for i in range(group * together, (group + 1) * together):
+            held_rows = first[:, i].reshape(everyone, both)
+            picked = jnp.dot(pick[...], held_rows, preferred_element_type=f32).astype(bf16)
+            gone.append(picked[:, both // 2 :])
+        moved[:, group] = jnp.concatenate(gone, axis=1).reshape(devices, slots, lanes)
+
+
+def move(pick, first):
+    devices, rows, per_device, both = first.shape
+    rows = rows - 1
+    together = divisor(rows, 2, 1)
+    shape = (devices, rows // together, per_device, together * both // 2)
+    return pl.pallas_call(
+        move_kernel,
+        in_specs=[whole_vmem] * 2,
+        out_specs=whole_vmem,
+        out_shape=jax.ShapeDtypeStruct(shape, bf16),
+        compiler_params=pltpu.CompilerParams(vmem_limit_bytes=16 * MIB),
+        cost_estimate=pl.CostEstimate(
+            flops=2 * pick.size * rows * both, bytes_accessed=2 * first.size, transcendentals=0
+        ),
+    )(pick, first)
+
+
+def payload_kernel(copies, from_walkers, from_inverse, out, walkers, inverse, got, both, built, sent):
+    fetches = [
+        pltpu.make_async_copy(from_walkers, walkers, got.at[0]),
+        pltpu.make_async_copy(from_inverse, inverse, got.at[1]),
+    ]
+    for fetch in fetches:
+        fetch.start()
+    per_device, electrons, _ = walkers.shape
+    devices, rows = built.shape[0], built.shape[1] - 1
+    at = lax.broadcasted_iota(jnp.int32, (electrons, electrons), 0)
+    unit = (at == lax.broadcasted_iota(jnp.int32, at.shape, 1)).astype(f32).astype(bf16)
+    for fetch in fetches:
+        fetch.wait()
+    counts = jnp.zeros((per_device, 2 * electrons), f32)
+    walker = lax.broadcasted_iota(jnp.int32, counts.shape, 0)
+    for w in range(per_device):
+        counts = jnp.where(walker == w, copies[w].astype(f32), counts)
+        both[w] = lax.dot_general(
+            walkers[w],
+            jnp.concatenate([inverse[w], unit], axis=1),
+            (((0,), (0,)), ((), ())),
+            preferred_element_type=f32,
+        ).astype(bf16)
+    counts = counts.astype(bf16)
+    pack = max(1, GROUP // rows)
+    block = pack * rows
+    size = block * per_device
+    to = lax.broadcasted_iota(jnp.int32, (size, size), 0)
+    source = lax.broadcasted_iota(jnp.int32, (size, size), 1)
+    regroup = (source == (to % per_device) * block + to // per_device).astype(f32).astype(bf16)
+
+    def put(d):
+        return pltpu.make_async_copy(built.at[d], out.at[d], sent.at[d])
+
+    for d in range(0, devices, pack):
+        mixed = both[:, d * rows : d * rows + block, :].reshape(size, 2 * electrons)
+        by_row = jnp.dot(regroup, mixed, preferred_element_type=f32).astype(bf16)
+        by_row = by_row.reshape(block, per_device, 2 * electrons)
+        for n in range(pack):
+            built[d + n, :rows] = by_row[n * rows : (n + 1) * rows]
+            built[d + n, rows] = counts
+            put(d + n).start()
+    for d in range(devices):
+        put(d).wait()
+
+
+def payload(copies, walkers, inverse, devices):
+    per_device, electrons, orbitals_n = walkers.shape
+    rows = orbitals_n // devices
+    shape = (devices, rows + 1, per_device, 2 * electrons)
+    return pl.pallas_call(
+        payload_kernel,
+        in_specs=[pl.BlockSpec(memory_space=pltpu.SMEM), in_hbm, in_hbm],
+        out_specs=in_hbm,
+        out_shape=jax.ShapeDtypeStruct(shape, bf16),
+        scratch_shapes=[
+            pltpu.VMEM(walkers.shape, bf16),
+            pltpu.VMEM(inverse.shape, bf16),
+            pltpu.SemaphoreType.DMA((2,)),
+            pltpu.VMEM((per_device, orbitals_n, 2 * electrons), bf16),
+            pltpu.VMEM(shape, bf16),
+            pltpu.SemaphoreType.DMA((devices,)),
+        ],
+        compiler_params=pltpu.CompilerParams(vmem_limit_bytes=PAYLOAD_MIB * MIB),
+        cost_estimate=pl.CostEstimate(
+            flops=4 * electrons * walkers.size, bytes_accessed=6 * walkers.size, transcendentals=0
+        ),
+    )(copies, walkers, inverse)
 
 
 def taylor_kernel(got, orbitals, out, propagator):
@@ -265,25 +401,14 @@
 
     by_row = chol_by_row(chol)
 
-    theta = jnp.einsum(
-        "wmk,wkn->wmn", walkers, inv_intersection, preferred_element_type=f32
-    ).astype(bf16)
-
-    def by_owner(a):
-        a = a.reshape(per_device, devices, own_rows * electrons)
-        return jnp.transpose(a, (1, 0, 2))
-
-    counts = jnp.broadcast_to(copies.astype(bf16)[None, :, None], (devices, per_device, 128))
-    wide = own_rows * electrons
     first = lax.all_to_all(
-        jnp.concatenate([by_owner(theta), by_owner(walkers), counts], axis=2),
+        payload(copies, jnp.transpose(walkers, (0, 2, 1)), inv_intersection, devices),
         "row",
         0,
         0,
         tiled=True,
-    ).reshape(everyone, 2 * wide + 128)
-    count_column = first[:, 2 * wide :][:, :1].astype(f32)
-    walker_rows = first[:, wide : 2 * wide]
+    )
+    count_column = first[:, own_rows, :, :1].reshape(everyone, 1).astype(f32)
 
     ids = jnp.arange(everyone, dtype=jnp.int32)
     before = (ids[:, None] <= ids[None, :]).astype(f32)
@@ -310,17 +435,14 @@
         jnp.where(spot[:, None] == residues[None, :chips], ring_ids[None, :], 0), axis=1
     )
     owner = 2 * to_chip + (core ^ flip)
-    new_rows = jnp.dot(
-        parents_of(ids // per_device, slot), walker_rows, preferred_element_type=f32
-    ).astype(bf16)
-    got_rows = lax.all_to_all(
-        new_rows.reshape(devices, per_device, own_rows * electrons), "row", 0, 0, tiled=True
-    )
+    part = bias_parts(parents_of(owner, slot), first, trial.T, by_row)
+    moved = move(parents_of(ids // per_device, slot), first)
+
+    got_rows = lax.all_to_all(moved, "row", 0, 0, tiled=True)
     orbitals = jnp.transpose(
-        got_rows.reshape(devices, per_device, own_rows, electrons), (1, 3, 0, 2)
+        got_rows.reshape(devices, moved.shape[1], per_device, -1, electrons), (2, 4, 0, 1, 3)
     ).reshape(per_device, electrons, orbitals_n)
 
-    part = bias_parts(parents_of(owner, slot), first, trial.T, by_row)
     part = part.reshape(2, chips, per_device, chol_n)
 
     swap = ring_move(devices, 1, 0)
@@ -328,12 +450,18 @@
     left = ring_move(devices, 0, -1)
     swapped = lax.ppermute(part[1], "row", swap)
 
+    halves = (2, chips, 2, per_device // 2, chol_n)
+
+    def own_left(k):
+        pieces = part.reshape(halves)[0, k % chips], swapped.reshape(halves[1:])[k % chips]
+        return pieces[0].astype(f32) + pieces[1].astype(f32)
+
     def own_term(k):
         return part[0, k % chips].astype(f32) + swapped[k % chips].astype(f32)
 
     to_right, to_left = chips // 2, chips - 1 - chips // 2
     moving_right = own_term(to_right).astype(bf16)
-    moving_left = own_term(-to_left).astype(bf16)
+    moving_left = own_left(-to_left).astype(bf16)
     for t in range(to_right):
         moving_right = lax.ppermute(moving_right, "row", right)
         if t < to_left:
@@ -341,10 +469,10 @@
         if t < to_right - 1:
             moving_right = (moving_right.astype(f32) + own_term(to_right - 1 - t)).astype(bf16)
         if t < to_left - 1:
-            moving_left = (moving_left.astype(f32) + own_term(-(to_left - 1 - t))).astype(bf16)
+            moving_left = (moving_left.astype(f32) + own_left(-(to_left - 1 - t))).astype(bf16)
     bias_raw = own_term(0) + moving_right.astype(f32)
     if to_left:
-        bias_raw = bias_raw + moving_left.astype(f32)
+        bias_raw = bias_raw + moving_left.astype(f32).reshape(bias_raw.shape)
     force_bias = root_step * bias_raw
     fields = (noise + jnp.clip(force_bias, -1.0, 1.0)).astype(bf16)
 

time: 186 us -> 178 us (0.957)
  local copies, waits for them, and re-layouts: 10.3 us -> 6.69 us
  starting transfers between devices: 40.2 us -> 37.4 us
  Pallas kernels: 57.6 us -> 60.4 us
  matrix products: 2.53 us -> 0 us
    pallas_call x2 -> x4, Pallas kernels: 39 us -> 42.1 us  [the longest x1 22.9 us: chol_by_row(): pl.pallas_call(by_row_kernel, in_specs=[in_hbm], out_specs=in_hbm, out_sh...]
    all_to_all x2, starting transfers between devices: 13.9 us -> 11.3 us  [the longest x1 6.57 us: local(): lax.all_to_all(payload(copies, jnp.transpose(walkers, (0, 2, 1)), inv_int...]
    dot_general x2 -> x0, matrix products: 2.53 us -> none  [the longest x1 1.39 us: local(): jnp.einsum('wmk,wkn->wmn', walkers, inv_intersection, preferred_element_t...]
    ppermute x3, waiting for transfers between devices: 2.39 us -> 0.01 us  [local(): moving_left = lax.ppermute(moving_left, 'row', left)]
    all_to_all x2, waiting for transfers between devices: 0.01 us -> 1.91 us  [the longest x1 1.91 us: local(): lax.all_to_all(payload(copies, jnp.transpose(walkers, (0, 2, 1)), inv_int...]
    reshape x4 -> x3, local copies, waits for them, and re-layouts: 4.77 us -> 5.65 us  [the longest x2 3.67 us: local(): got_rows.reshape(devices, moved.shape[1], per_device, -1, electrons)]
  transfers between devices with their start and end apart: 19 -> 19, of which waited for: 15 -> 12; matrix products, arithmetic and copies ran while one was open for 4% -> 5% of each run, Pallas kernels for 22% -> 22%
where the time goes in v4:
time: 178 us; the launch traced here: 177 us
  waiting for transfers between devices  68 us (38%)
  Pallas kernels  60.4 us (34%)
  starting transfers between devices  37.4 us (21%)
  local copies, waits for them, and re-layouts  6.69 us (4%)
  other arithmetic  3.9 us (2%)
    all_to_all x1, waiting for transfers between devices, local(): got = lax.all_to_all(propagator_part, 'row', 0, 0, tiled=True)  41.8 us
    pallas_call x1, Pallas kernels, chol_by_row(): pl.pallas_call(by_row_kernel, in_specs=[in_hbm], out_specs=in_hbm, out_sh...  22.9 us
    pallas_call x1, Pallas kernels, propagator_parts(): pl.pallas_call(propagator_kernel, in_specs=[pl.BlockSpec(memory_space=plt...  14.1 us
    pallas_call x1, Pallas kernels, bias_parts(): pl.pallas_call(bias_kernel, in_specs=[whole_vmem] * 3 + [in_hbm], out_spe...  13.7 us
    ppermute x4, waiting for transfers between devices, local(): moving_right = lax.ppermute(moving_right, 'row', right)  10.8 us
    ppermute x4, waiting for transfers between devices, local(): going_right = lax.ppermute(going_right, 'row', right)  10.7 us
    ppermute x1, starting transfers between devices, local(): other_core = lax.ppermute(own_core, 'row', swap)  8.82 us
    all_to_all x1, starting transfers between devices, local(): lax.all_to_all(payload(copies, jnp.transpose(walkers, (0, 2, 1)), inv_int...  6.57 us
  transfers between devices with their start and end apart: 19, of which 12 were waited for; matrix products, arithmetic and copies ran while one was open for 5% of the time, Pallas kernels for 22%

profile of v4, /device:TPU:15, one launch (start us, length us, event | category | flops | bytes accessed | tf_op | source)
XLA Modules:
  0.0 177.3 jit_solution(10638128998289666241)
XLA Ops:
  0.6 0.0 copy-start.5
  0.6 0.0 copy-start.3
  0.7 3.9 %shard_map.113 = bf16[16,17,16,128]{3,2,1,0:T(8,128)(2,1)} custom-call(s32[16]{0:T(128)} %copies.1, bf16[16,64,256]{2,1,0:T(8,128)(2,1)} %bitcast.124, bf16[16,64,64]{2,1,0:T(8,128)(2,1)} %from_inverse.1), custom_call_target="tpu_custom_call" | custom-call | flops 67108864 | bytes 1572864 | tf_op jit(solution)/shard_map/pallas_call | solution.py:322
  4.5 6.6 %all-to-all-start = ((bf16[16,17,16,128]{3,2,1,0:T(8,128)(2,1)}), bf16[16,17,16,128]{3,2,1,0:T(8,128)(2,1)S(1)}, u32[]{:S(2)}, u32[]{:S(2)}) async-start(bf16[16,17,16,128]{3,2,1,0:T(8,128)(2,1)} %shard_map.113), calls=%async_computation | async-start | bytes 2228224 | tf_op jit(solution)/shard_map/all_to_all | solution.py:404
  11.1 0.6 fusion.23
  11.8 0.7 and_select_fusion.1
  12.4 0.1 select_reduce_fusion.4
  12.5 0.1 select_reduce_fusion.2
  12.6 22.9 %shard_map.114.chol = bf16[16,4096,256]{2,1,0:T(8,128)(2,1)} custom-call(bf16[4096,16,256]{2,1,0:T(8,128)(2,1)} %chol.1), custom_call_target="tpu_custom_call" | custom-call | flops 8589934592 | bytes 67108864 | tf_op jit(solution)/shard_map/pallas_call | solution.py:110
  35.6 1.9 %all-to-all-done.first = bf16[16,17,16,128]{3,2,1,0:T(8,128)(2,1)S(1)} async-done(((bf16[16,17,16,128]{3,2,1,0:T(8,128)(2,1)}), bf16[16,17,16,128]{3,2,1,0:T(8,128)(2,1)S(1)}, u32[]{:S(2)}, u32[]{:S(2)}) %all-to-all-start) | async-done | bytes 1114144 | tf_op jit(solution)/shard_map/all_to_all | solution.py:404
  37.5 0.1 convert_reduce_fusion
  37.6 0.1 reshape.156
  37.7 0.1 select_reduce_fusion.1
  37.8 0.1 and_convert_fusion
  37.9 13.7 %shard_map.115 = bf16[256,4096]{1,0:T(8,128)(2,1)S(1)} custom-call(bf16[256,256]{1,0:T(8,128)(2,1)S(1)} %get-tuple-element.10.pick, bf16[16,17,16,128]{3,2,1,0:T(8,128)(2,1)S(1)} %all-to-all-done.first, bf16[64,256]{1,0:T(8,128)(2,1)S(1)} %bitcast.121, bf16[16,4096,256]{2,1,0:T(8,128)(2,1)} %shard_map.114.chol), custom_call_target="tpu_custom_call" | custom-call | flops 8589934592 | bytes 33554432 | tf_op jit(solution)/shard_map/pallas_call | solution.py:160
  51.7 0.1 slice.88
  51.7 0.0 copy-start.2
  51.8 0.3 collective-permute-start
  52.0 2.4 %collective-permute-done = bf16[8,16,4096]{2,1,0:T(8,128)(2,1)S(1)} collective-permute-done((bf16[8,16,4096]{2,1,0:T(8,128)(2,1)S(1)}, bf16[8,16,4096]{2,1,0:T(8,128)(2,1)S(1)}, u32[]{:S(2)}, u32[]{:S(2)}) %collective-permute-start) | collective-permute-done | bytes 1048608 | tf_op jit(solution)/shard_map/ppermute | solution.py:451
  54.5 0.1 collective-permute-start.1
  54.6 1.5 collective-permute-start.5
  56.1 3.3 %collective-permute-done.1 = bf16[16,4096]{1,0:T(8,128)(2,1)S(1)} collective-permute-done((bf16[16,4096]{1,0:T(8,128)(2,1)S(1)}, bf16[16,4096]{1,0:T(8,128)(2,1)S(1)}, u32[]{:S(2)}, u32[]{:S(2)}) %collective-permute-start.1) | collective-permute-done | bytes 131104 | tf_op jit(solution)/shard_map/ppermute | solution.py:466
  59.5 0.1 fusion.11
  59.5 0.4 collective-permute-start.2
  59.9 0.1 fusion.4
  60.0 1.2 collective-permute-start.6
  61.2 2.2 %collective-permute-done.2 = bf16[16,4096]{1,0:T(8,128)(2,1)S(1)} collective-permute-done((bf16[16,4096]{1,0:T(8,128)(2,1)S(1)}, bf16[16,4096]{1,0:T(8,128)(2,1)S(1)}, u32[]{:S(2)}, u32[]{:S(2)}) %collective-permute-start.2) | collective-permute-done | bytes 131104 | tf_op jit(solution)/shard_map/ppermute | solution.py:466
  63.4 0.1 fusion.9
  63.4 0.0 copy-start.6
  63.5 0.9 collective-permute-start.3
  64.4 0.1 fusion.2
  64.4 0.8 collective-permute-start.7
  65.2 2.1 %collective-permute-done.3 = bf16[16,4096]{1,0:T(8,128)(2,1)S(1)} collective-permute-done((bf16[16,4096]{1,0:T(8,128)(2,1)S(1)}, bf16[16,4096]{1,0:T(8,128)(2,1)S(1)}, u32[]{:S(2)}, u32[]{:S(2)}) %collective-permute-start.3) | collective-permute-done | bytes 131104 | tf_op jit(solution)/shard_map/ppermute | solution.py:466
  67.3 0.1 fusion.7
  67.4 0.9 collective-permute-start.4
  68.3 3.1 %collective-permute-done.4 = bf16[16,4096]{1,0:T(8,128)(2,1)S(1)} collective-permute-done((bf16[16,4096]{1,0:T(8,128)(2,1)S(1)}, bf16[16,4096]{1,0:T(8,128)(2,1)S(1)}, u32[]{:S(2)}, u32[]{:S(2)}) %collective-permute-start.4) | collective-permute-done | bytes 131104 | tf_op jit(solution)/shard_map/ppermute | solution.py:466
  71.4 0.8 bitcast_dynamic-update-slice_fusion.7
  72.2 0.7 collective-permute-start.8
  72.9 0.7 collective-permute-start.9
  73.6 2.9 %collective-permute-done.8 = bf16[16,4096]{1,0:T(8,128)(2,1)S(1)} collective-permute-done((bf16[16,4096]{1,0:T(8,128)(2,1)S(1)}, bf16[16,4096]{1,0:T(8,128)(2,1)S(1)}, u32[]{:S(2)}, u32[]{:S(2)}) %collective-permute-start.8) | collective-permute-done | bytes 131104 | tf_op jit(solution)/shard_map/ppermute | solution.py:482
  76.5 0.2 collective-permute-start.10
  76.7 1.3 collective-permute-start.11
  78.1 2.9 %collective-permute-done.10 = bf16[16,4096]{1,0:T(8,128)(2,1)S(1)} collective-permute-done((bf16[16,4096]{1,0:T(8,128)(2,1)S(1)}, bf16[16,4096]{1,0:T(8,128)(2,1)S(1)}, u32[]{:S(2)}, u32[]{:S(2)}) %collective-permute-start.10) | collective-permute-done | bytes 131104 | tf_op jit(solution)/shard_map/ppermute | solution.py:482
  80.9 0.8 collective-permute-start.12
  81.7 0.7 collective-permute-start.13
  82.5 2.3 %collective-permute-done.12 = bf16[16,4096]{1,0:T(8,128)(2,1)S(1)} collective-permute-done((bf16[16,4096]{1,0:T(8,128)(2,1)S(1)}, bf16[16,4096]{1,0:T(8,128)(2,1)S(1)}, u32[]{:S(2)}, u32[]{:S(2)}) %collective-permute-start.12) | collective-permute-done | bytes 131104 | tf_op jit(solution)/shard_map/ppermute | solution.py:482
  84.8 0.8 collective-permute-start.14
  85.5 0.4 collective-permute-done.13
  85.9 2.7 %collective-permute-done.14 = bf16[16,4096]{1,0:T(8,128)(2,1)S(1)} collective-permute-done((bf16[16,4096]{1,0:T(8,128)(2,1)S(1)}, bf16[16,4096]{1,0:T(8,128)(2,1)S(1)}, u32[]{:S(2)}, u32[]{:S(2)}) %collective-permute-start.14) | collective-permute-done | bytes 131104 | tf_op jit(solution)/shard_map/ppermute | solution.py:482
  88.6 8.8 %collective-permute-start.15 = (bf16[8,16,4096]{2,1,0:T(8,128)(2,1)S(1)}, bf16[8,16,4096]{2,1,0:T(8,128)(2,1)S(1)}, u32[]{:S(2)}, u32[]{:S(2)}) collective-permute-start(bf16[8,16,4096]{2,1,0:T(8,128)(2,1)S(1)} %bitcast_dynamic-update-slice_fusion.own_core), channel_id=1, source_target_pairs={{0,1},{1,0},{4,5},{5,4},{8,9},{9,8},{12,13},{13,12},{14,15},{15,14... | collective-permute-start | bytes 3145736 | tf_op jit(solution)/shard_map/ppermute | solution.py:490
  97.4 0.7 and_select_fusion.5
  98.1 0.2 select_reduce_fusion.5
  98.2 1.6 shard_map.117
  99.8 4.8 %all-to-all-start.2 = ((bf16[16,8,16,128]{3,2,1,0:T(8,128)(2,1)}), bf16[16,8,16,128]{3,2,1,0:T(8,128)(2,1)S(1)}, u32[]{:S(2)}, u32[]{:S(2)}) async-start(bf16[16,8,16,128]{3,2,1,0:T(8,128)(2,1)} %shard_map.117), calls=%async_computation.2 | async-start | bytes 1048576 | tf_op jit(solution)/shard_map/all_to_all | solution.py:441
  104.6 0.1 pad_add_fusion.spots
  104.7 14.1 %shard_map.116 = bf16[16,16,16,256]{3,2,1,0:T(8,128)(2,1)} custom-call(s32[16]{0:T(128)S(1)} %pad_add_fusion.spots, bf16[8,16,4096]{2,1,0:T(8,128)(2,1)S(1)} %bitcast_dynamic-update-slice_fusion.own_core, bf16[8,16,4096]{2,1,0:T(8,128)(2,1)S(1)} %collective-permute-done.15.other_core, bf16[16,4096,256]{2,1,0:T(8,128)(2,1)} %shard_map.114.chol), custom_call_target="tpu_custom_call" | custom-call | flops 8589934592 | bytes 33554432 | tf_op jit(solution)/shard_map/pallas_call | solution.py:221
  118.7 0.0 copy-start.1
  118.8 0.8 copy-done.1
  119.5 6.0 %all-to-all-start.1 = ((bf16[16,16,16,256]{3,2,1,0:T(8,128)(2,1)}), bf16[16,16,16,256]{3,2,1,0:T(8,128)(2,1)S(1)}, u32[]{:S(2)}, u32[]{:S(2)}) async-start(bf16[16,16,16,256]{3,2,1,0:T(8,128)(2,1)} %shard_map.116), calls=%async_computation.1 | async-start | bytes 4194304 | tf_op jit(solution)/shard_map/all_to_all | solution.py:497
  125.6 2.4 %reshape.154 = bf16[16,8,16,2,64]{4,3,2,1,0:T(2,128)(2,1)S(1)} reshape(bf16[16,8,16,128]{3,2,1,0:T(8,128)(2,1)} %copy-done.1) | data formatting | bytes 1048576 | tf_op jit(solution)/shard_map/reshape | solution.py:443
  128.0 1.2 copy.15
  129.2 2.0 %copy.16.orbitals = bf16[16,64,256]{2,1,0:T(8,128)(2,1)S(1)} copy(bf16[16,64,256]{1,0,2:T(8,128)(2,1)} %bitcast.122) | data formatting | bytes 1048576 | tf_op jit(solution)/shard_map/reshape | solution.py:444
  131.2 41.8 %all-to-all-done.1.got = bf16[16,16,16,256]{3,2,1,0:T(8,128)(2,1)S(1)} async-done(((bf16[16,16,16,256]{3,2,1,0:T(8,128)(2,1)}), bf16[16,16,16,256]{3,2,1,0:T(8,128)(2,1)S(1)}, u32[]{:S(2)}, u32[]{:S(2)}) %all-to-all-start.1) | async-done | bytes 2097184 | tf_op jit(solution)/shard_map/all_to_all | solution.py:497
  173.0 4.3 %shard_map.118 = bf16[16,64,256]{2,1,0:T(8,128)(2,1)} custom-call(bf16[16,16,16,256]{3,2,1,0:T(8,128)(2,1)S(1)} %all-to-all-done.1.got, bf16[16,64,256]{2,1,0:T(8,128)(2,1)S(1)} %copy.16.orbitals), custom_call_target="tpu_custom_call" | custom-call | flops 536870912 | bytes 4194304 | tf_op jit(solution)/shard_map/pallas_call | solution.py:379
  (29 shorter events, 0.2 us)
Async XLA Ops:
  0.6 10.5 %copy-start.5 = (s32[8]{0:T(128)S(1)}, s32[8]{0:T(128)}, u32[]{:S(2)}) copy-start(s32[8]{0:T(128)} %constant.118.clone) | copy-start | bytes 100
  0.6 11.8 %copy-start.3 = (s32[8]{0:T(128)S(1)}, s32[8]{0:T(128)}, u32[]{:S(2)}) copy-start(s32[8]{0:T(128)} %constant.117.clone) | copy-start | bytes 100
  0.7 11.9 %copy-start.4 = (s32[16]{0:T(128)S(1)}, s32[16]{0:T(128)}, u32[]{:S(2)}) copy-start(s32[16]{0:T(128)} %param.13) | copy-start | bytes 196
  4.5 32.9 %all-to-all-start = ((bf16[16,17,16,128]{3,2,1,0:T(8,128)(2,1)}), bf16[16,17,16,128]{3,2,1,0:T(8,128)(2,1)S(1)}, u32[]{:S(2)}, u32[]{:S(2)}) async-start(bf16[16,17,16,128]{3,2,1,0:T(8,128)(2,1)} %shard_map.113), calls=%async_computation | async-start | bytes 2228224 | tf_op jit(solution)/shard_map/all_to_all | solution.py:404
  12.6 25.3 %copy-start = (bf16[256,64]{0,1:T(8,128)(2,1)S(1)}, bf16[256,64]{0,1:T(8,128)(2,1)}, u32[]{:S(2)}) copy-start(bf16[256,64]{0,1:T(8,128)(2,1)} %param.14) | copy-start | bytes 98308
  51.7 19.6 %copy-start.2 = (f32[16,4096]{1,0:T(8,128)S(1)}, f32[16,4096]{1,0:T(8,128)}, u32[]{:S(2)}) copy-start(f32[16,4096]{1,0:T(8,128)} %param.16) | copy-start | bytes 786436
  51.8 2.7 %collective-permute-start = (bf16[8,16,4096]{2,1,0:T(8,128)(2,1)S(1)}, bf16[8,16,4096]{2,1,0:T(8,128)(2,1)S(1)}, u32[]{:S(2)}, u32[]{:S(2)}) collective-permute-start(bf16[8,16,4096]{2,1,0:T(8,128)(2,1)S(1)} %bitcast.123), channel_id=1, source_target_pairs={{0,1},{1,0},{4,5},{5,4},{8,9},{9,8},{12,13},{13,12},{14,15},{15,14... | collective-permute-start | bytes 3145736 | tf_op jit(solution)/shard_map/ppermute | solution.py:451
  54.5 4.9 %collective-permute-start.1 = (bf16[16,4096]{1,0:T(8,128)(2,1)S(1)}, bf16[16,4096]{1,0:T(8,128)(2,1)S(1)}, u32[]{:S(2)}, u32[]{:S(2)}) collective-permute-start(bf16[16,4096]{1,0:T(8,128)(2,1)S(1)} %fusion.12), channel_id=1, source_target_pairs={{0,4},{1,5},{4,8},{5,9},{8,12},{9,13},{12,14},{13,15},{14,10},{15,... | collective-permute-start | bytes 393224 | tf_op jit(solution)/shard_map/ppermute | solution.py:466
  54.6 5.3 %collective-permute-start.5 = (bf16[2,8,4096]{2,1,0:T(8,128)(2,1)S(1)}, bf16[2,8,4096]{2,1,0:T(8,128)(2,1)S(1)}, u32[]{:S(2)}, u32[]{:S(2)}) collective-permute-start(bf16[2,8,4096]{2,1,0:T(8,128)(2,1)S(1)} %fusion.5), channel_id=1, source_target_pairs={{0,2},{1,3},{4,0},{5,1},{8,4},{9,5},{12,8},{13,9},{14,12},{15,13},... | collective-permute-start | bytes 393224 | tf_op jit(solution)/shard_map/ppermute | solution.py:468
  59.5 3.9 %collective-permute-start.2 = (bf16[16,4096]{1,0:T(8,128)(2,1)S(1)}, bf16[16,4096]{1,0:T(8,128)(2,1)S(1)}, u32[]{:S(2)}, u32[]{:S(2)}) collective-permute-start(bf16[16,4096]{1,0:T(8,128)(2,1)S(1)} %fusion.11), channel_id=1, source_target_pairs={{0,4},{1,5},{4,8},{5,9},{8,12},{9,13},{12,14},{13,15},{14,10},{15,... | collective-permute-start | bytes 393224 | tf_op jit(solution)/shard_map/ppermute | solution.py:466
  60.0 4.4 %collective-permute-start.6 = (bf16[2,8,4096]{2,1,0:T(8,128)(2,1)S(1)}, bf16[2,8,4096]{2,1,0:T(8,128)(2,1)S(1)}, u32[]{:S(2)}, u32[]{:S(2)}) collective-permute-start(bf16[2,8,4096]{2,1,0:T(8,128)(2,1)S(1)} %fusion.4), channel_id=1, source_target_pairs={{0,2},{1,3},{4,0},{5,1},{8,4},{9,5},{12,8},{13,9},{14,12},{15,13},... | collective-permute-start | bytes 393224 | tf_op jit(solution)/shard_map/ppermute | solution.py:468
  63.4 34.0 %copy-start.6 = (s32[8]{0:T(128)S(1)}, s32[8]{0:T(128)}, u32[]{:S(2)}) copy-start(s32[8]{0:T(128)} %constant.119.clone) | copy-start | bytes 100
  63.5 3.9 %collective-permute-start.3 = (bf16[16,4096]{1,0:T(8,128)(2,1)S(1)}, bf16[16,4096]{1,0:T(8,128)(2,1)S(1)}, u32[]{:S(2)}, u32[]{:S(2)}) collective-permute-start(bf16[16,4096]{1,0:T(8,128)(2,1)S(1)} %fusion.9), channel_id=1, source_target_pairs={{0,4},{1,5},{4,8},{5,9},{8,12},{9,13},{12,14},{13,15},{14,10},{15,... | collective-permute-start | bytes 393224 | tf_op jit(solution)/shard_map/ppermute | solution.py:466
  64.4 3.9 %collective-permute-start.7 = (bf16[2,8,4096]{2,1,0:T(8,128)(2,1)S(1)}, bf16[2,8,4096]{2,1,0:T(8,128)(2,1)S(1)}, u32[]{:S(2)}, u32[]{:S(2)}) collective-permute-start(bf16[2,8,4096]{2,1,0:T(8,128)(2,1)S(1)} %fusion.2), channel_id=1, source_target_pairs={{0,2},{1,3},{4,0},{5,1},{8,4},{9,5},{12,8},{13,9},{14,12},{15,13},... | collective-permute-start | bytes 393224 | tf_op jit(solution)/shard_map/ppermute | solution.py:468
  67.4 4.0 %collective-permute-start.4 = (bf16[16,4096]{1,0:T(8,128)(2,1)S(1)}, bf16[16,4096]{1,0:T(8,128)(2,1)S(1)}, u32[]{:S(2)}, u32[]{:S(2)}) collective-permute-start(bf16[16,4096]{1,0:T(8,128)(2,1)S(1)} %fusion.7), channel_id=1, source_target_pairs={{0,4},{1,5},{4,8},{5,9},{8,12},{9,13},{12,14},{13,15},{14,10},{15,... | collective-permute-start | bytes 393224 | tf_op jit(solution)/shard_map/ppermute | solution.py:466
  72.2 4.3 %collective-permute-start.8 = (bf16[16,4096]{1,0:T(8,128)(2,1)S(1)}, bf16[16,4096]{1,0:T(8,128)(2,1)S(1)}, u32[]{:S(2)}, u32[]{:S(2)}) collective-permute-start(bf16[16,4096]{1,0:T(8,128)(2,1)S(1)} %get-tuple-element.7), channel_id=1, source_target_pairs={{0,4},{1,5},{4,8},{5,9},{8,12},{9,13},{12,14},{13,15},{14,10},{15,... | collective-permute-start | bytes 393224 | tf_op jit(solution)/shard_map/ppermute | solution.py:482
  72.9 3.8 %collective-permute-start.9 = (bf16[16,4096]{1,0:T(8,128)(2,1)S(1)}, bf16[16,4096]{1,0:T(8,128)(2,1)S(1)}, u32[]{:S(2)}, u32[]{:S(2)}) collective-permute-start(bf16[16,4096]{1,0:T(8,128)(2,1)S(1)} %get-tuple-element.7), channel_id=1, source_target_pairs={{0,2},{1,3},{4,0},{5,1},{8,4},{9,5},{12,8},{13,9},{14,12},{15,13},... | collective-permute-start | bytes 393224 | tf_op jit(solution)/shard_map/ppermute | solution.py:486
  76.5 4.4 %collective-permute-start.10 = (bf16[16,4096]{1,0:T(8,128)(2,1)S(1)}, bf16[16,4096]{1,0:T(8,128)(2,1)S(1)}, u32[]{:S(2)}, u32[]{:S(2)}) collective-permute-start(bf16[16,4096]{1,0:T(8,128)(2,1)S(1)} %collective-permute-done.8), channel_id=1, source_target_pairs={{0,4},{1,5},{4,8},{5,9},{8,12},{9,13},{12,14},{13,15},{14,10},{15,... | collective-permute-start | bytes 393224 | tf_op jit(solution)/shard_map/ppermute | solution.py:482
  76.7 5.0 %collective-permute-start.11 = (bf16[16,4096]{1,0:T(8,128)(2,1)S(1)}, bf16[16,4096]{1,0:T(8,128)(2,1)S(1)}, u32[]{:S(2)}, u32[]{:S(2)}) collective-permute-start(bf16[16,4096]{1,0:T(8,128)(2,1)S(1)} %collective-permute-done.9), channel_id=1, source_target_pairs={{0,2},{1,3},{4,0},{5,1},{8,4},{9,5},{12,8},{13,9},{14,12},{15,13},... | collective-permute-start | bytes 393224 | tf_op jit(solution)/shard_map/ppermute | solution.py:486
  80.9 3.8 %collective-permute-start.12 = (bf16[16,4096]{1,0:T(8,128)(2,1)S(1)}, bf16[16,4096]{1,0:T(8,128)(2,1)S(1)}, u32[]{:S(2)}, u32[]{:S(2)}) collective-permute-start(bf16[16,4096]{1,0:T(8,128)(2,1)S(1)} %collective-permute-done.10), channel_id=1, source_target_pairs={{0,4},{1,5},{4,8},{5,9},{8,12},{9,13},{12,14},{13,15},{14,10},{15,... | collective-permute-start | bytes 393224 | tf_op jit(solution)/shard_map/ppermute | solution.py:482
  81.7 4.2 %collective-permute-start.13 = (bf16[16,4096]{1,0:T(8,128)(2,1)S(1)}, bf16[16,4096]{1,0:T(8,128)(2,1)S(1)}, u32[]{:S(2)}, u32[]{:S(2)}) collective-permute-start(bf16[16,4096]{1,0:T(8,128)(2,1)S(1)} %collective-permute-done.11), channel_id=1, source_target_pairs={{0,2},{1,3},{4,0},{5,1},{8,4},{9,5},{12,8},{13,9},{14,12},{15,13},... | collective-permute-start | bytes 393224 | tf_op jit(solution)/shard_map/ppermute | solution.py:486
  84.8 3.8 %collective-permute-start.14 = (bf16[16,4096]{1,0:T(8,128)(2,1)S(1)}, bf16[16,4096]{1,0:T(8,128)(2,1)S(1)}, u32[]{:S(2)}, u32[]{:S(2)}) collective-permute-start(bf16[16,4096]{1,0:T(8,128)(2,1)S(1)} %collective-permute-done.12), channel_id=1, source_target_pairs={{0,4},{1,5},{4,8},{5,9},{8,12},{9,13},{12,14},{13,15},{14,10},{15,... | collective-permute-start | bytes 393224 | tf_op jit(solution)/shard_map/ppermute | solution.py:482
  88.6 16.1 %collective-permute-start.15 = (bf16[8,16,4096]{2,1,0:T(8,128)(2,1)S(1)}, bf16[8,16,4096]{2,1,0:T(8,128)(2,1)S(1)}, u32[]{:S(2)}, u32[]{:S(2)}) collective-permute-start(bf16[8,16,4096]{2,1,0:T(8,128)(2,1)S(1)} %bitcast_dynamic-update-slice_fusion.own_core), channel_id=1, source_target_pairs={{0,1},{1,0},{4,5},{5,4},{8,9},{9,8},{12,13},{13,12},{14,15},{15,14... | collective-permute-start | bytes 3145736 | tf_op jit(solution)/shard_map/ppermute | solution.py:490
  99.8 18.9 %all-to-all-start.2 = ((bf16[16,8,16,128]{3,2,1,0:T(8,128)(2,1)}), bf16[16,8,16,128]{3,2,1,0:T(8,128)(2,1)S(1)}, u32[]{:S(2)}, u32[]{:S(2)}) async-start(bf16[16,8,16,128]{3,2,1,0:T(8,128)(2,1)} %shard_map.117), calls=%async_computation.2 | async-start | bytes 1048576 | tf_op jit(solution)/shard_map/all_to_all | solution.py:441
  118.7 0.8 copy-start.1
  119.5 53.4 %all-to-all-start.1 = ((bf16[16,16,16,256]{3,2,1,0:T(8,128)(2,1)}), bf16[16,16,16,256]{3,2,1,0:T(8,128)(2,1)S(1)}, u32[]{:S(2)}, u32[]{:S(2)}) async-start(bf16[16,16,16,256]{3,2,1,0:T(8,128)(2,1)} %shard_map.116), calls=%async_computation.1 | async-start | bytes 4194304 | tf_op jit(solution)/shard_map/all_to_all | solution.py:497

commit v5 on v4

--- a/solution.py
+++ b/solution.py
@@ -389,6 +389,29 @@
     )(got, orbitals)
 
 
+def fields_kernel(own, from_left, from_right, noise, moved, bias, fields):
+    del moved
+    total = own[...].astype(f32) + from_left[...].astype(f32) + from_right[...].astype(f32)
+    bias[...] = root_step * total
+    fields[...] = (noise[...] + jnp.clip(root_step * total, -1.0, 1.0)).astype(bf16)
+
+
+def make_fields(own, from_left, from_right, noise, moved):
+    return pl.pallas_call(
+        fields_kernel,
+        in_specs=[whole_vmem] * 4 + [pl.BlockSpec(memory_space=pl.ANY)],
+        out_specs=[whole_vmem] * 2,
+        out_shape=[
+            jax.ShapeDtypeStruct(noise.shape, f32),
+            jax.ShapeDtypeStruct(noise.shape, bf16),
+        ],
+        compiler_params=pltpu.CompilerParams(vmem_limit_bytes=8 * MIB),
+        cost_estimate=pl.CostEstimate(
+            flops=6 * noise.size, bytes_accessed=16 * noise.size, transcendentals=0
+        ),
+    )(own, from_left, from_right, noise, moved)
+
+
 def local(walkers, inv_intersection, copies, deal, trial, chol, noise):
     devices = lax.axis_size("row")
     me = lax.axis_index("row")
@@ -448,18 +471,25 @@
     swap = ring_move(devices, 1, 0)
     right = ring_move(devices, 0, 1)
     left = ring_move(devices, 0, -1)
-    swapped = lax.ppermute(part[1], "row", swap)
-
-    halves = (2, chips, 2, per_device // 2, chol_n)
+    to_right, to_left = chips // 2, chips - 1 - chips // 2
+    edges = sorted({0, to_right, min(to_right + 2, chips), chips})
+    spans = sorted(zip(edges, edges[1:]), key=lambda span: span[0] != to_right)
+    swaps = [(low, lax.ppermute(part[1, low:high], "row", swap)) for low, high in spans]
+
+    def swapped(k):
+        low, held = max((s for s in swaps if s[0] <= k), key=lambda s: s[0])
+        return held[k - low]
+
+    halves = (2, per_device // 2, chol_n)
 
     def own_left(k):
-        pieces = part.reshape(halves)[0, k % chips], swapped.reshape(halves[1:])[k % chips]
-        return pieces[0].astype(f32) + pieces[1].astype(f32)
+        k = k % chips
+        return part[0, k].reshape(halves).astype(f32) + swapped(k).reshape(halves).astype(f32)
 
     def own_term(k):
-        return part[0, k % chips].astype(f32) + swapped[k % chips].astype(f32)
-
-    to_right, to_left = chips // 2, chips - 1 - chips // 2
+        k = k % chips
+        return part[0, k].astype(f32) + swapped(k).astype(f32)
+
     moving_right = own_term(to_right).astype(bf16)
     moving_left = own_left(-to_left).astype(bf16)
     for t in range(to_right):
@@ -470,11 +500,11 @@
             moving_right = (moving_right.astype(f32) + own_term(to_right - 1 - t)).astype(bf16)
         if t < to_left - 1:
             moving_left = (moving_left.astype(f32) + own_left(-(to_left - 1 - t))).astype(bf16)
-    bias_raw = own_term(0) + moving_right.astype(f32)
-    if to_left:
-        bias_raw = bias_raw + moving_left.astype(f32).reshape(bias_raw.shape)
-    force_bias = root_step * bias_raw
-    fields = (noise + jnp.clip(force_bias, -1.0, 1.0)).astype(bf16)
+    if not to_left:
+        moving_left = jnp.zeros_like(moving_right)
+    force_bias, fields = make_fields(
+        own_term(0), moving_right, moving_left.reshape(noise.shape), noise, moved
+    )
 
     pieces, offsets = [fields], [0]
     going_right = going_left = fields

time: 178 us -> 176 us (0.989)
  waiting for transfers between devices: 68 us -> 65.9 us
    ppermute x3, waiting for transfers between devices: 0.36 us -> 4.66 us  [local(): going_left = lax.ppermute(going_left, 'row', left)]
    ppermute x4, waiting for transfers between devices: 10.7 us -> 7.51 us  [local(): going_right = lax.ppermute(going_right, 'row', right)]
  transfers between devices with their start and end apart: 19 -> 21, of which waited for: 12 -> 13; matrix products, arithmetic and copies ran while one was open for 5% -> 5% of each run, Pallas kernels for 22% -> 22%
where the time goes in v5:
time: 176 us; the launch traced here: 175 us
  waiting for transfers between devices  65.9 us (37%)
  Pallas kernels  61.2 us (35%)
  starting transfers between devices  37.6 us (21%)
  local copies, waits for them, and re-layouts  6.7 us (4%)
  other arithmetic  2.96 us (2%)
    all_to_all x1, waiting for transfers between devices, local(): got = lax.all_to_all(propagator_part, 'row', 0, 0, tiled=True)  41.8 us
    pallas_call x1, Pallas kernels, chol_by_row(): pl.pallas_call(by_row_kernel, in_specs=[in_hbm], out_specs=in_hbm, out_sh...  22.9 us
    pallas_call x1, Pallas kernels, propagator_parts(): pl.pallas_call(propagator_kernel, in_specs=[pl.BlockSpec(memory_space=plt...  14.1 us
    pallas_call x1, Pallas kernels, bias_parts(): pl.pallas_call(bias_kernel, in_specs=[whole_vmem] * 3 + [in_hbm], out_spe...  13.7 us
    ppermute x4, waiting for transfers between devices, local(): moving_right = lax.ppermute(moving_right, 'row', right)  9.2 us
    ppermute x1, starting transfers between devices, local(): other_core = lax.ppermute(own_core, 'row', swap)  8.27 us
    ppermute x4, waiting for transfers between devices, local(): going_right = lax.ppermute(going_right, 'row', right)  7.51 us
    all_to_all x1, starting transfers between devices, local(): lax.all_to_all(payload(copies, jnp.transpose(walkers, (0, 2, 1)), inv_int...  6.57 us
  transfers between devices with their start and end apart: 21, of which 13 were waited for; matrix products, arithmetic and copies ran while one was open for 5% of the time, Pallas kernels for 22%

profile of v5, /device:TPU:15, one launch (start us, length us, event | category | flops | bytes accessed | tf_op | source)
XLA Modules:
  0.0 175.2 jit_solution(12795132488326865505)
XLA Ops:
  0.6 0.0 copy-start.5
  0.6 0.0 copy-start.3
  0.7 3.9 %shard_map.113 = bf16[16,17,16,128]{3,2,1,0:T(8,128)(2,1)} custom-call(s32[16]{0:T(128)} %copies.1, bf16[16,64,256]{2,1,0:T(8,128)(2,1)} %bitcast.124, bf16[16,64,64]{2,1,0:T(8,128)(2,1)} %from_inverse.1), custom_call_target="tpu_custom_call" | custom-call | flops 67108864 | bytes 1572864 | tf_op jit(solution)/shard_map/pallas_call | solution.py:322
  4.6 6.6 %all-to-all-start = ((bf16[16,17,16,128]{3,2,1,0:T(8,128)(2,1)}), bf16[16,17,16,128]{3,2,1,0:T(8,128)(2,1)S(1)}, u32[]{:S(2)}, u32[]{:S(2)}) async-start(bf16[16,17,16,128]{3,2,1,0:T(8,128)(2,1)} %shard_map.113), calls=%async_computation | async-start | bytes 2228224 | tf_op jit(solution)/shard_map/all_to_all | solution.py:427
  11.1 0.6 fusion.21
  11.8 0.6 and_select_fusion.1
  12.4 0.1 select_reduce_fusion.4
  12.5 0.1 select_reduce_fusion.2
  12.6 22.9 %shard_map.114.chol = bf16[16,4096,256]{2,1,0:T(8,128)(2,1)} custom-call(bf16[4096,16,256]{2,1,0:T(8,128)(2,1)} %chol.1), custom_call_target="tpu_custom_call" | custom-call | flops 8589934592 | bytes 67108864 | tf_op jit(solution)/shard_map/pallas_call | solution.py:110
  35.5 2.0 %all-to-all-done.first = bf16[16,17,16,128]{3,2,1,0:T(8,128)(2,1)S(1)} async-done(((bf16[16,17,16,128]{3,2,1,0:T(8,128)(2,1)}), bf16[16,17,16,128]{3,2,1,0:T(8,128)(2,1)S(1)}, u32[]{:S(2)}, u32[]{:S(2)}) %all-to-all-start) | async-done | bytes 1114144 | tf_op jit(solution)/shard_map/all_to_all | solution.py:427
  37.5 0.1 convert_reduce_fusion
  37.6 0.1 reshape.141
  37.7 0.1 select_reduce_fusion.1
  37.8 0.1 and_convert_fusion
  38.0 13.7 %shard_map.115 = bf16[256,4096]{1,0:T(8,128)(2,1)S(1)} custom-call(bf16[256,256]{1,0:T(8,128)(2,1)S(1)} %get-tuple-element.15.pick, bf16[16,17,16,128]{3,2,1,0:T(8,128)(2,1)S(1)} %all-to-all-done.first, bf16[64,256]{1,0:T(8,128)(2,1)S(1)} %bitcast.122, bf16[16,4096,256]{2,1,0:T(8,128)(2,1)} %shard_map.114.chol), custom_call_target="tpu_custom_call" | custom-call | flops 8589934592 | bytes 33554432 | tf_op jit(solution)/shard_map/pallas_call | solution.py:160
  51.7 0.3 collective-permute-start.1
  52.0 0.4 collective-permute-start.7
  52.4 0.2 collective-permute-start
  52.6 0.7 collective-permute-done.1
  53.4 0.1 collective-permute-start.2
  53.5 1.5 collective-permute-start.6
  55.0 3.3 %collective-permute-done.2 = bf16[16,4096]{1,0:T(8,128)(2,1)S(1)} collective-permute-done((bf16[16,4096]{1,0:T(8,128)(2,1)S(1)}, bf16[16,4096]{1,0:T(8,128)(2,1)S(1)}, u32[]{:S(2)}, u32[]{:S(2)}) %collective-permute-start.2) | collective-permute-done | bytes 131104 | tf_op jit(solution)/shard_map/ppermute | solution.py:496
  58.3 0.1 fusion.10
  58.4 0.4 collective-permute-start.3
  58.8 0.1 fusion.3
  58.8 1.2 collective-permute-start.8
  60.0 2.2 %collective-permute-done.3 = bf16[16,4096]{1,0:T(8,128)(2,1)S(1)} collective-permute-done((bf16[16,4096]{1,0:T(8,128)(2,1)S(1)}, bf16[16,4096]{1,0:T(8,128)(2,1)S(1)}, u32[]{:S(2)}, u32[]{:S(2)}) %collective-permute-start.3) | collective-permute-done | bytes 131104 | tf_op jit(solution)/shard_map/ppermute | solution.py:496
  62.2 0.1 fusion.8
  62.3 0.9 collective-permute-start.4
  63.2 0.1 fusion.1
  63.2 0.8 collective-permute-start.9
  64.0 2.1 %collective-permute-done.4 = bf16[16,4096]{1,0:T(8,128)(2,1)S(1)} collective-permute-done((bf16[16,4096]{1,0:T(8,128)(2,1)S(1)}, bf16[16,4096]{1,0:T(8,128)(2,1)S(1)}, u32[]{:S(2)}, u32[]{:S(2)}) %collective-permute-start.4) | collective-permute-done | bytes 131104 | tf_op jit(solution)/shard_map/ppermute | solution.py:496
  66.2 0.1 fusion.6
  66.3 0.9 collective-permute-start.5
  67.1 1.6 shard_map.116.moved
  68.7 1.5 collective-permute-done.5.from_left
  70.2 0.8 shard_map.117
  71.0 0.2 collective-permute-start.11
  71.2 1.3 collective-permute-start.10
  72.5 2.3 %collective-permute-done.11 = bf16[16,4096]{1,0:T(8,128)(2,1)S(1)} collective-permute-done((bf16[16,4096]{1,0:T(8,128)(2,1)S(1)}, bf16[16,4096]{1,0:T(8,128)(2,1)S(1)}, u32[]{:S(2)}, u32[]{:S(2)}) %collective-permute-start.11) | collective-permute-done | bytes 131104 | tf_op jit(solution)/shard_map/ppermute | solution.py:516
  74.8 0.2 collective-permute-start.13
  75.0 0.4 collective-permute-done.10
  75.4 0.9 collective-permute-start.12
  76.3 2.3 %collective-permute-done.13 = bf16[16,4096]{1,0:T(8,128)(2,1)S(1)} collective-permute-done((bf16[16,4096]{1,0:T(8,128)(2,1)S(1)}, bf16[16,4096]{1,0:T(8,128)(2,1)S(1)}, u32[]{:S(2)}, u32[]{:S(2)}) %collective-permute-start.13) | collective-permute-done | bytes 131104 | tf_op jit(solution)/shard_map/ppermute | solution.py:516
  78.6 1.0 collective-permute-start.15
  79.6 0.4 collective-permute-done.12
  80.0 0.6 collective-permute-start.14
  80.6 3.5 %collective-permute-done.14 = bf16[16,4096]{1,0:T(8,128)(2,1)S(1)} collective-permute-done((bf16[16,4096]{1,0:T(8,128)(2,1)S(1)}, bf16[16,4096]{1,0:T(8,128)(2,1)S(1)}, u32[]{:S(2)}, u32[]{:S(2)}) %collective-permute-start.14) | collective-permute-done | bytes 131104 | tf_op jit(solution)/shard_map/ppermute | solution.py:512
  84.1 0.6 collective-permute-start.16
  84.8 3.2 %collective-permute-done.16 = bf16[16,4096]{1,0:T(8,128)(2,1)S(1)} collective-permute-done((bf16[16,4096]{1,0:T(8,128)(2,1)S(1)}, bf16[16,4096]{1,0:T(8,128)(2,1)S(1)}, u32[]{:S(2)}, u32[]{:S(2)}) %collective-permute-start.16) | collective-permute-done | bytes 131104 | tf_op jit(solution)/shard_map/ppermute | solution.py:512
  88.0 8.3 %collective-permute-start.17 = (bf16[8,16,4096]{2,1,0:T(8,128)(2,1)S(1)}, bf16[8,16,4096]{2,1,0:T(8,128)(2,1)S(1)}, u32[]{:S(2)}, u32[]{:S(2)}) collective-permute-start(bf16[8,16,4096]{2,1,0:T(8,128)(2,1)S(1)} %bitcast_dynamic-update-slice_fusion.own_core), channel_id=1, source_target_pairs={{0,1},{1,0},{4,5},{5,4},{8,9},{9,8},{12,13},{13,12},{14,15},{15,14... | collective-permute-start | bytes 3145736 | tf_op jit(solution)/shard_map/ppermute | solution.py:520
  96.3 0.6 and_select_fusion.5
  96.8 0.2 select_reduce_fusion.5
  97.0 5.5 %all-to-all-start.2 = ((bf16[16,8,16,128]{3,2,1,0:T(8,128)(2,1)}), bf16[16,8,16,128]{3,2,1,0:T(8,128)(2,1)S(1)}, u32[]{:S(2)}, u32[]{:S(2)}) async-start(bf16[16,8,16,128]{3,2,1,0:T(8,128)(2,1)} %shard_map.116.moved), calls=%async_computation.2 | async-start | bytes 1048576 | tf_op jit(solution)/shard_map/all_to_all | solution.py:464
  102.5 0.1 pad_add_fusion.spots
  102.6 14.1 %shard_map.118 = bf16[16,16,16,256]{3,2,1,0:T(8,128)(2,1)} custom-call(s32[16]{0:T(128)S(1)} %pad_add_fusion.spots, bf16[8,16,4096]{2,1,0:T(8,128)(2,1)S(1)} %bitcast_dynamic-update-slice_fusion.own_core, bf16[8,16,4096]{2,1,0:T(8,128)(2,1)S(1)} %collective-permute-done.17.other_core, bf16[16,4096,256]{2,1,0:T(8,128)(2,1)} %shard_map.114.chol), custom_call_target="tpu_custom_call" | custom-call | flops 8589934592 | bytes 33554432 | tf_op jit(solution)/shard_map/pallas_call | solution.py:221
  116.7 0.0 copy-start.2
  116.7 0.8 copy-done.2
  117.5 6.0 %all-to-all-start.1 = ((bf16[16,16,16,256]{3,2,1,0:T(8,128)(2,1)}), bf16[16,16,16,256]{3,2,1,0:T(8,128)(2,1)S(1)}, u32[]{:S(2)}, u32[]{:S(2)}) async-start(bf16[16,16,16,256]{3,2,1,0:T(8,128)(2,1)} %shard_map.118), calls=%async_computation.1 | async-start | bytes 4194304 | tf_op jit(solution)/shard_map/all_to_all | solution.py:527
  123.5 2.4 %reshape.139 = bf16[16,8,16,2,64]{4,3,2,1,0:T(2,128)(2,1)S(1)} reshape(bf16[16,8,16,128]{3,2,1,0:T(8,128)(2,1)} %copy-done.2) | data formatting | bytes 1048576 | tf_op jit(solution)/shard_map/reshape | solution.py:466
  126.0 1.2 copy.15
  127.2 2.0 %copy.16.orbitals = bf16[16,64,256]{2,1,0:T(8,128)(2,1)S(1)} copy(bf16[16,64,256]{1,0,2:T(8,128)(2,1)} %bitcast.123) | data formatting | bytes 1048576 | tf_op jit(solution)/shard_map/reshape | solution.py:467
  129.2 41.8 %all-to-all-done.1.got = bf16[16,16,16,256]{3,2,1,0:T(8,128)(2,1)S(1)} async-done(((bf16[16,16,16,256]{3,2,1,0:T(8,128)(2,1)}), bf16[16,16,16,256]{3,2,1,0:T(8,128)(2,1)S(1)}, u32[]{:S(2)}, u32[]{:S(2)}) %all-to-all-start.1) | async-done | bytes 2097184 | tf_op jit(solution)/shard_map/all_to_all | solution.py:527
  170.9 4.3 %shard_map.119 = bf16[16,64,256]{2,1,0:T(8,128)(2,1)} custom-call(bf16[16,16,16,256]{3,2,1,0:T(8,128)(2,1)S(1)} %all-to-all-done.1.got, bf16[16,64,256]{2,1,0:T(8,128)(2,1)S(1)} %copy.16.orbitals), custom_call_target="tpu_custom_call" | custom-call | flops 536870912 | bytes 4194304 | tf_op jit(solution)/shard_map/pallas_call | solution.py:379
  (35 shorter events, 0.3 us)
Async XLA Ops:
  0.6 10.5 %copy-start.5 = (s32[8]{0:T(128)S(1)}, s32[8]{0:T(128)}, u32[]{:S(2)}) copy-start(s32[8]{0:T(128)} %constant.112.clone) | copy-start | bytes 100
  0.6 11.7 %copy-start.3 = (s32[8]{0:T(128)S(1)}, s32[8]{0:T(128)}, u32[]{:S(2)}) copy-start(s32[8]{0:T(128)} %constant.111.clone) | copy-start | bytes 100
  0.7 11.8 %copy-start.4 = (s32[16]{0:T(128)S(1)}, s32[16]{0:T(128)}, u32[]{:S(2)}) copy-start(s32[16]{0:T(128)} %param.13) | copy-start | bytes 196
  4.6 32.9 %all-to-all-start = ((bf16[16,17,16,128]{3,2,1,0:T(8,128)(2,1)}), bf16[16,17,16,128]{3,2,1,0:T(8,128)(2,1)S(1)}, u32[]{:S(2)}, u32[]{:S(2)}) async-start(bf16[16,17,16,128]{3,2,1,0:T(8,128)(2,1)} %shard_map.113), calls=%async_computation | async-start | bytes 2228224 | tf_op jit(solution)/shard_map/all_to_all | solution.py:427
  12.6 25.4 %copy-start.1 = (bf16[256,64]{0,1:T(8,128)(2,1)S(1)}, bf16[256,64]{0,1:T(8,128)(2,1)}, u32[]{:S(2)}) copy-start(bf16[256,64]{0,1:T(8,128)(2,1)} %param.14) | copy-start | bytes 98308
  51.7 1.6 collective-permute-start.1
  52.0 6.7 %collective-permute-start.7 = (bf16[2,16,4096]{2,1,0:T(8,128)(2,1)S(1)}, bf16[2,16,4096]{2,1,0:T(8,128)(2,1)S(1)}, u32[]{:S(2)}, u32[]{:S(2)}) collective-permute-start(bf16[2,16,4096]{2,1,0:T(8,128)(2,1)S(1)} %get-tuple-element.12), channel_id=1, source_target_pairs={{0,1},{1,0},{4,5},{5,4},{8,9},{9,8},{12,13},{13,12},{14,15},{15,14... | collective-permute-start | bytes 786440 | tf_op jit(solution)/shard_map/ppermute | solution.py:477
  52.4 5.9 %collective-permute-start = (bf16[4,16,4096]{2,1,0:T(8,128)(2,1)S(1)}, bf16[4,16,4096]{2,1,0:T(8,128)(2,1)S(1)}, u32[]{:S(2)}, u32[]{:S(2)}) collective-permute-start(bf16[4,16,4096]{2,1,0:T(8,128)(2,1)S(1)} %slice_bitcast_fusion), channel_id=1, source_target_pairs={{0,1},{1,0},{4,5},{5,4},{8,9},{9,8},{12,13},{13,12},{14,15},{15,14... | collective-permute-start | bytes 1572872 | tf_op jit(solution)/shard_map/ppermute | solution.py:477
  53.4 4.9 %collective-permute-start.2 = (bf16[16,4096]{1,0:T(8,128)(2,1)S(1)}, bf16[16,4096]{1,0:T(8,128)(2,1)S(1)}, u32[]{:S(2)}, u32[]{:S(2)}) collective-permute-start(bf16[16,4096]{1,0:T(8,128)(2,1)S(1)} %fusion.11), channel_id=1, source_target_pairs={{0,4},{1,5},{4,8},{5,9},{8,12},{9,13},{12,14},{13,15},{14,10},{15,... | collective-permute-start | bytes 393224 | tf_op jit(solution)/shard_map/ppermute | solution.py:496
  53.5 5.3 %collective-permute-start.6 = (bf16[2,8,4096]{2,1,0:T(8,128)(2,1)S(1)}, bf16[2,8,4096]{2,1,0:T(8,128)(2,1)S(1)}, u32[]{:S(2)}, u32[]{:S(2)}) collective-permute-start(bf16[2,8,4096]{2,1,0:T(8,128)(2,1)S(1)} %fusion.4), channel_id=1, source_target_pairs={{0,2},{1,3},{4,0},{5,1},{8,4},{9,5},{12,8},{13,9},{14,12},{15,13},... | collective-permute-start | bytes 393224 | tf_op jit(solution)/shard_map/ppermute | solution.py:498
  58.4 11.8 %copy-start = (f32[16,4096]{1,0:T(8,128)S(1)}, f32[16,4096]{1,0:T(8,128)}, u32[]{:S(2)}) copy-start(f32[16,4096]{1,0:T(8,128)} %noise.1) | copy-start | bytes 786436
  58.4 3.9 %collective-permute-start.3 = (bf16[16,4096]{1,0:T(8,128)(2,1)S(1)}, bf16[16,4096]{1,0:T(8,128)(2,1)S(1)}, u32[]{:S(2)}, u32[]{:S(2)}) collective-permute-start(bf16[16,4096]{1,0:T(8,128)(2,1)S(1)} %fusion.10), channel_id=1, source_target_pairs={{0,4},{1,5},{4,8},{5,9},{8,12},{9,13},{12,14},{13,15},{14,10},{15,... | collective-permute-start | bytes 393224 | tf_op jit(solution)/shard_map/ppermute | solution.py:496
  58.8 4.4 %collective-permute-start.8 = (bf16[2,8,4096]{2,1,0:T(8,128)(2,1)S(1)}, bf16[2,8,4096]{2,1,0:T(8,128)(2,1)S(1)}, u32[]{:S(2)}, u32[]{:S(2)}) collective-permute-start(bf16[2,8,4096]{2,1,0:T(8,128)(2,1)S(1)} %fusion.3), channel_id=1, source_target_pairs={{0,2},{1,3},{4,0},{5,1},{8,4},{9,5},{12,8},{13,9},{14,12},{15,13},... | collective-permute-start | bytes 393224 | tf_op jit(solution)/shard_map/ppermute | solution.py:498
  62.3 3.9 %collective-permute-start.4 = (bf16[16,4096]{1,0:T(8,128)(2,1)S(1)}, bf16[16,4096]{1,0:T(8,128)(2,1)S(1)}, u32[]{:S(2)}, u32[]{:S(2)}) collective-permute-start(bf16[16,4096]{1,0:T(8,128)(2,1)S(1)} %fusion.8), channel_id=1, source_target_pairs={{0,4},{1,5},{4,8},{5,9},{8,12},{9,13},{12,14},{13,15},{14,10},{15,... | collective-permute-start | bytes 393224 | tf_op jit(solution)/shard_map/ppermute | solution.py:496
  63.2 5.5 %collective-permute-start.9 = (bf16[2,8,4096]{2,1,0:T(8,128)(2,1)S(1)}, bf16[2,8,4096]{2,1,0:T(8,128)(2,1)S(1)}, u32[]{:S(2)}, u32[]{:S(2)}) collective-permute-start(bf16[2,8,4096]{2,1,0:T(8,128)(2,1)S(1)} %fusion.1), channel_id=1, source_target_pairs={{0,2},{1,3},{4,0},{5,1},{8,4},{9,5},{12,8},{13,9},{14,12},{15,13},... | collective-permute-start | bytes 393224 | tf_op jit(solution)/shard_map/ppermute | solution.py:498
  66.3 4.0 %collective-permute-start.5 = (bf16[16,4096]{1,0:T(8,128)(2,1)S(1)}, bf16[16,4096]{1,0:T(8,128)(2,1)S(1)}, u32[]{:S(2)}, u32[]{:S(2)}) collective-permute-start(bf16[16,4096]{1,0:T(8,128)(2,1)S(1)} %get-tuple-element.10), channel_id=1, source_target_pairs={{0,4},{1,5},{4,8},{5,9},{8,12},{9,13},{12,14},{13,15},{14,10},{15,... | collective-permute-start | bytes 393224 | tf_op jit(solution)/shard_map/ppermute | solution.py:496
  68.7 27.6 %copy-start.6 = (s32[8]{0:T(128)S(1)}, s32[8]{0:T(128)}, u32[]{:S(2)}) copy-start(s32[8]{0:T(128)} %constant.113.clone) | copy-start | bytes 100
  71.0 3.8 %collective-permute-start.11 = (bf16[16,4096]{1,0:T(8,128)(2,1)S(1)}, bf16[16,4096]{1,0:T(8,128)(2,1)S(1)}, u32[]{:S(2)}, u32[]{:S(2)}) collective-permute-start(bf16[16,4096]{1,0:T(8,128)(2,1)S(1)} %get-tuple-element.4), channel_id=1, source_target_pairs={{0,2},{1,3},{4,0},{5,1},{8,4},{9,5},{12,8},{13,9},{14,12},{15,13},... | collective-permute-start | bytes 393224 | tf_op jit(solution)/shard_map/ppermute | solution.py:516
  71.2 4.2 %collective-permute-start.10 = (bf16[16,4096]{1,0:T(8,128)(2,1)S(1)}, bf16[16,4096]{1,0:T(8,128)(2,1)S(1)}, u32[]{:S(2)}, u32[]{:S(2)}) collective-permute-start(bf16[16,4096]{1,0:T(8,128)(2,1)S(1)} %get-tuple-element.4), channel_id=1, source_target_pairs={{0,4},{1,5},{4,8},{5,9},{8,12},{9,13},{12,14},{13,15},{14,10},{15,... | collective-permute-start | bytes 393224 | tf_op jit(solution)/shard_map/ppermute | solution.py:512
  74.8 3.8 %collective-permute-start.13 = (bf16[16,4096]{1,0:T(8,128)(2,1)S(1)}, bf16[16,4096]{1,0:T(8,128)(2,1)S(1)}, u32[]{:S(2)}, u32[]{:S(2)}) collective-permute-start(bf16[16,4096]{1,0:T(8,128)(2,1)S(1)} %collective-permute-done.11), channel_id=1, source_target_pairs={{0,2},{1,3},{4,0},{5,1},{8,4},{9,5},{12,8},{13,9},{14,12},{15,13},... | collective-permute-start | bytes 393224 | tf_op jit(solution)/shard_map/ppermute | solution.py:516
  75.4 4.7 %collective-permute-start.12 = (bf16[16,4096]{1,0:T(8,128)(2,1)S(1)}, bf16[16,4096]{1,0:T(8,128)(2,1)S(1)}, u32[]{:S(2)}, u32[]{:S(2)}) collective-permute-start(bf16[16,4096]{1,0:T(8,128)(2,1)S(1)} %collective-permute-done.10), channel_id=1, source_target_pairs={{0,4},{1,5},{4,8},{5,9},{8,12},{9,13},{12,14},{13,15},{14,10},{15,... | collective-permute-start | bytes 393224 | tf_op jit(solution)/shard_map/ppermute | solution.py:512
  78.6 6.1 %collective-permute-start.15 = (bf16[16,4096]{1,0:T(8,128)(2,1)S(1)}, bf16[16,4096]{1,0:T(8,128)(2,1)S(1)}, u32[]{:S(2)}, u32[]{:S(2)}) collective-permute-start(bf16[16,4096]{1,0:T(8,128)(2,1)S(1)} %collective-permute-done.13), channel_id=1, source_target_pairs={{0,2},{1,3},{4,0},{5,1},{8,4},{9,5},{12,8},{13,9},{14,12},{15,13},... | collective-permute-start | bytes 393224 | tf_op jit(solution)/shard_map/ppermute | solution.py:516
  80.0 4.1 %collective-permute-start.14 = (bf16[16,4096]{1,0:T(8,128)(2,1)S(1)}, bf16[16,4096]{1,0:T(8,128)(2,1)S(1)}, u32[]{:S(2)}, u32[]{:S(2)}) collective-permute-start(bf16[16,4096]{1,0:T(8,128)(2,1)S(1)} %collective-permute-done.12), channel_id=1, source_target_pairs={{0,4},{1,5},{4,8},{5,9},{8,12},{9,13},{12,14},{13,15},{14,10},{15,... | collective-permute-start | bytes 393224 | tf_op jit(solution)/shard_map/ppermute | solution.py:512
  84.1 3.8 %collective-permute-start.16 = (bf16[16,4096]{1,0:T(8,128)(2,1)S(1)}, bf16[16,4096]{1,0:T(8,128)(2,1)S(1)}, u32[]{:S(2)}, u32[]{:S(2)}) collective-permute-start(bf16[16,4096]{1,0:T(8,128)(2,1)S(1)} %collective-permute-done.14), channel_id=1, source_target_pairs={{0,4},{1,5},{4,8},{5,9},{8,12},{9,13},{12,14},{13,15},{14,10},{15,... | collective-permute-start | bytes 393224 | tf_op jit(solution)/shard_map/ppermute | solution.py:512
  88.0 14.6 %collective-permute-start.17 = (bf16[8,16,4096]{2,1,0:T(8,128)(2,1)S(1)}, bf16[8,16,4096]{2,1,0:T(8,128)(2,1)S(1)}, u32[]{:S(2)}, u32[]{:S(2)}) collective-permute-start(bf16[8,16,4096]{2,1,0:T(8,128)(2,1)S(1)} %bitcast_dynamic-update-slice_fusion.own_core), channel_id=1, source_target_pairs={{0,1},{1,0},{4,5},{5,4},{8,9},{9,8},{12,13},{13,12},{14,15},{15,14... | collective-permute-start | bytes 3145736 | tf_op jit(solution)/shard_map/ppermute | solution.py:520
  97.0 19.7 %all-to-all-start.2 = ((bf16[16,8,16,128]{3,2,1,0:T(8,128)(2,1)}), bf16[16,8,16,128]{3,2,1,0:T(8,128)(2,1)S(1)}, u32[]{:S(2)}, u32[]{:S(2)}) async-start(bf16[16,8,16,128]{3,2,1,0:T(8,128)(2,1)} %shard_map.116.moved), calls=%async_computation.2 | async-start | bytes 1048576 | tf_op jit(solution)/shard_map/all_to_all | solution.py:464
  116.7 0.8 copy-start.2
  117.5 53.4 %all-to-all-start.1 = ((bf16[16,16,16,256]{3,2,1,0:T(8,128)(2,1)}), bf16[16,16,16,256]{3,2,1,0:T(8,128)(2,1)S(1)}, u32[]{:S(2)}, u32[]{:S(2)}) async-start(bf16[16,16,16,256]{3,2,1,0:T(8,128)(2,1)} %shard_map.118), calls=%async_computation.1 | async-start | bytes 4194304 | tf_op jit(solution)/shard_map/all_to_all | solution.py:527

commit v6 on v5

--- a/solution.py
+++ b/solution.py
@@ -28,7 +28,7 @@
 GROUP = 16
 SLOTS = 3
 SPAN = 512
-TOGETHER = 8
+TOGETHER = 16
 PAYLOAD_MIB = 56
 DEPTH = 4096
 HELD = 5
@@ -419,8 +419,9 @@
     chol_n, own_rows, width = chol.shape
     everyone = devices * per_device
     chips = devices // 2
-    ring = chip_ring(devices)
-    place = [ring.index(m) for m in range(chips)]
+
+    def chip_at(place):
+        return jnp.where(place < (chips + 1) // 2, 2 * place, 2 * (chips - 1 - place) + 1)
 
     by_row = chol_by_row(chol)
 
@@ -448,15 +449,11 @@
         return ((position >= starts[None, :]) & (position < ends[None, :])).astype(bf16)
 
     chip, core = me // 2, me % 2
-    ring_ids = jnp.array(ring, jnp.int32)
-    own_place = jnp.sum(jnp.where(residues[:chips] == chip, jnp.array(place, jnp.int32), 0))
+    own_place = jnp.where(chip % 2 == 0, chip // 2, chips - 1 - chip // 2)
     slot = ids % per_device
     step = (ids // per_device) % chips
     flip = ids // (per_device * chips)
-    spot = (own_place + step) % chips
-    to_chip = jnp.sum(
-        jnp.where(spot[:, None] == residues[None, :chips], ring_ids[None, :], 0), axis=1
-    )
+    to_chip = chip_at((own_place + step) % chips)
     owner = 2 * to_chip + (core ^ flip)
     part = bias_parts(parents_of(owner, slot), first, trial.T, by_row)
     moved = move(parents_of(ids // per_device, slot), first)
@@ -518,10 +515,7 @@
             offsets.append(t + 1)
     own_core = jnp.stack(pieces)
     other_core = lax.ppermute(own_core, "row", swap)
-    spots = (own_place + jnp.array(offsets, jnp.int32)) % chips
-    spots = 2 * jnp.sum(
-        jnp.where(spots[:, None] == residues[None, :chips], ring_ids[None, :], 0), axis=1
-    )
+    spots = jnp.stack([2 * chip_at((own_place + offset) % chips) for offset in offsets])
     spots = jnp.concatenate([spots + core, spots + 1 - core])
     propagator_part = propagator_parts(spots, own_core, other_core, by_row)
     got = lax.all_to_all(propagator_part, "row", 0, 0, tiled=True)

time: 176 us -> 175 us (level)
  other arithmetic: 2.96 us -> 0.93 us
  transfers between devices with their start and end apart: 21 -> 21, of which waited for: 13 -> 13; matrix products, arithmetic and copies ran while one was open for 5% -> 4% of each run, Pallas kernels for 22% -> 22%
where the time goes in v6:
time: 175 us; the launch traced here: 174 us
  waiting for transfers between devices  67.1 us (38%)
  Pallas kernels  60.9 us (35%)
  starting transfers between devices  37.7 us (22%)
  local copies, waits for them, and re-layouts  6.78 us (4%)
    all_to_all x1, waiting for transfers between devices, local(): got = lax.all_to_all(propagator_part, 'row', 0, 0, tiled=True)  41.7 us
    pallas_call x1, Pallas kernels, chol_by_row(): pl.pallas_call(by_row_kernel, in_specs=[in_hbm], out_specs=in_hbm, out_sh...  22.9 us
    pallas_call x1, Pallas kernels, propagator_parts(): pl.pallas_call(propagator_kernel, in_specs=[pl.BlockSpec(memory_space=plt...  14.1 us
    pallas_call x1, Pallas kernels, bias_parts(): pl.pallas_call(bias_kernel, in_specs=[whole_vmem] * 3 + [in_hbm], out_spe...  13.7 us
    ppermute x4, waiting for transfers between devices, local(): moving_right = lax.ppermute(moving_right, 'row', right)  9.21 us
    ppermute x1, starting transfers between devices, local(): other_core = lax.ppermute(own_core, 'row', swap)  8.27 us
    ppermute x4, waiting for transfers between devices, local(): going_right = lax.ppermute(going_right, 'row', right)  7.46 us
    all_to_all x1, starting transfers between devices, local(): lax.all_to_all(payload(copies, jnp.transpose(walkers, (0, 2, 1)), inv_int...  6.57 us
  transfers between devices with their start and end apart: 21, of which 13 were waited for; matrix products, arithmetic and copies ran while one was open for 4% of the time, Pallas kernels for 22%

profile of v6, /device:TPU:15, one launch (start us, length us, event | category | flops | bytes accessed | tf_op | source)
XLA Modules:
  0.0 174.3 jit_solution(8500388059279172659)
XLA Ops:
  0.6 3.9 %shard_map.86 = bf16[16,17,16,128]{3,2,1,0:T(8,128)(2,1)} custom-call(s32[16]{0:T(128)} %copies.1, bf16[16,64,256]{2,1,0:T(8,128)(2,1)} %bitcast.132, bf16[16,64,64]{2,1,0:T(8,128)(2,1)} %from_inverse.1), custom_call_target="tpu_custom_call" | custom-call | flops 67108864 | bytes 1572864 | tf_op jit(solution)/shard_map/pallas_call | solution.py:322
  4.5 6.6 %all-to-all-start = ((bf16[16,17,16,128]{3,2,1,0:T(8,128)(2,1)}), bf16[16,17,16,128]{3,2,1,0:T(8,128)(2,1)S(1)}, u32[]{:S(2)}, u32[]{:S(2)}) async-start(bf16[16,17,16,128]{3,2,1,0:T(8,128)(2,1)} %shard_map.86), calls=%async_computation | async-start | bytes 2228224 | tf_op jit(solution)/shard_map/all_to_all | solution.py:428
  11.1 0.1 select_reduce_fusion.2
  11.2 22.9 %shard_map.87.chol = bf16[16,4096,256]{2,1,0:T(8,128)(2,1)} custom-call(bf16[4096,16,256]{2,1,0:T(8,128)(2,1)} %chol.1), custom_call_target="tpu_custom_call" | custom-call | flops 8589934592 | bytes 67108864 | tf_op jit(solution)/shard_map/pallas_call | solution.py:110
  34.1 3.3 %all-to-all-done.first = bf16[16,17,16,128]{3,2,1,0:T(8,128)(2,1)S(1)} async-done(((bf16[16,17,16,128]{3,2,1,0:T(8,128)(2,1)}), bf16[16,17,16,128]{3,2,1,0:T(8,128)(2,1)S(1)}, u32[]{:S(2)}, u32[]{:S(2)}) %all-to-all-start) | async-done | bytes 1114144 | tf_op jit(solution)/shard_map/all_to_all | solution.py:428
  37.5 0.1 convert_reduce_fusion
  37.6 0.1 reshape.139
  37.6 0.1 select_reduce_fusion.1
  37.8 0.1 and_convert_fusion
  37.9 13.7 %shard_map.88 = bf16[256,4096]{1,0:T(8,128)(2,1)S(1)} custom-call(bf16[256,256]{1,0:T(8,128)(2,1)S(1)} %get-tuple-element.15.pick, bf16[16,17,16,128]{3,2,1,0:T(8,128)(2,1)S(1)} %all-to-all-done.first, bf16[64,256]{1,0:T(8,128)(2,1)S(1)} %bitcast.130, bf16[16,4096,256]{2,1,0:T(8,128)(2,1)} %shard_map.87.chol), custom_call_target="tpu_custom_call" | custom-call | flops 8589934592 | bytes 33554432 | tf_op jit(solution)/shard_map/pallas_call | solution.py:160
  51.7 0.3 collective-permute-start.1
  52.0 0.4 collective-permute-start.7
  52.4 0.2 collective-permute-start
  52.6 0.7 collective-permute-done.1
  53.3 0.1 collective-permute-start.2
  53.5 1.5 collective-permute-start.6
  54.9 3.3 %collective-permute-done.2 = bf16[16,4096]{1,0:T(8,128)(2,1)S(1)} collective-permute-done((bf16[16,4096]{1,0:T(8,128)(2,1)S(1)}, bf16[16,4096]{1,0:T(8,128)(2,1)S(1)}, u32[]{:S(2)}, u32[]{:S(2)}) %collective-permute-start.2) | collective-permute-done | bytes 131104 | tf_op jit(solution)/shard_map/ppermute | solution.py:493
  58.3 0.0 collective-permute-done
  58.3 0.1 fusion.10
  58.3 0.0 copy-start
  58.4 0.4 collective-permute-start.3
  58.7 0.1 fusion.3
  58.8 1.2 collective-permute-start.8
  60.0 2.2 %collective-permute-done.3 = bf16[16,4096]{1,0:T(8,128)(2,1)S(1)} collective-permute-done((bf16[16,4096]{1,0:T(8,128)(2,1)S(1)}, bf16[16,4096]{1,0:T(8,128)(2,1)S(1)}, u32[]{:S(2)}, u32[]{:S(2)}) %collective-permute-start.3) | collective-permute-done | bytes 131104 | tf_op jit(solution)/shard_map/ppermute | solution.py:493
  62.2 0.1 fusion.8
  62.3 0.9 collective-permute-start.4
  63.2 0.0 collective-permute-done.8
  63.2 0.1 fusion.1
  63.2 0.8 collective-permute-start.9
  64.0 2.1 %collective-permute-done.4 = bf16[16,4096]{1,0:T(8,128)(2,1)S(1)} collective-permute-done((bf16[16,4096]{1,0:T(8,128)(2,1)S(1)}, bf16[16,4096]{1,0:T(8,128)(2,1)S(1)}, u32[]{:S(2)}, u32[]{:S(2)}) %collective-permute-start.4) | collective-permute-done | bytes 131104 | tf_op jit(solution)/shard_map/ppermute | solution.py:493
  66.2 0.1 fusion.6
  66.2 0.9 collective-permute-start.5
  67.1 1.6 shard_map.89.moved
  68.7 0.0 collective-permute-done.9
  68.7 1.5 collective-permute-done.5.from_left
  70.2 0.8 shard_map.90
  71.0 0.2 collective-permute-start.11
  71.2 1.3 collective-permute-start.10
  72.4 2.3 %collective-permute-done.11 = bf16[16,4096]{1,0:T(8,128)(2,1)S(1)} collective-permute-done((bf16[16,4096]{1,0:T(8,128)(2,1)S(1)}, bf16[16,4096]{1,0:T(8,128)(2,1)S(1)}, u32[]{:S(2)}, u32[]{:S(2)}) %collective-permute-start.11) | collective-permute-done | bytes 131104 | tf_op jit(solution)/shard_map/ppermute | solution.py:513
  74.8 0.2 collective-permute-start.13
  75.0 0.4 collective-permute-done.10
  75.3 0.9 collective-permute-start.12
  76.3 2.3 %collective-permute-done.13 = bf16[16,4096]{1,0:T(8,128)(2,1)S(1)} collective-permute-done((bf16[16,4096]{1,0:T(8,128)(2,1)S(1)}, bf16[16,4096]{1,0:T(8,128)(2,1)S(1)}, u32[]{:S(2)}, u32[]{:S(2)}) %collective-permute-start.13) | collective-permute-done | bytes 131104 | tf_op jit(solution)/shard_map/ppermute | solution.py:513
  78.6 1.0 collective-permute-start.15
  79.6 0.4 collective-permute-done.12
  80.0 0.6 collective-permute-start.14
  80.6 3.5 %collective-permute-done.14 = bf16[16,4096]{1,0:T(8,128)(2,1)S(1)} collective-permute-done((bf16[16,4096]{1,0:T(8,128)(2,1)S(1)}, bf16[16,4096]{1,0:T(8,128)(2,1)S(1)}, u32[]{:S(2)}, u32[]{:S(2)}) %collective-permute-start.14) | collective-permute-done | bytes 131104 | tf_op jit(solution)/shard_map/ppermute | solution.py:509
  84.1 0.6 collective-permute-start.16
  84.8 3.2 %collective-permute-done.16 = bf16[16,4096]{1,0:T(8,128)(2,1)S(1)} collective-permute-done((bf16[16,4096]{1,0:T(8,128)(2,1)S(1)}, bf16[16,4096]{1,0:T(8,128)(2,1)S(1)}, u32[]{:S(2)}, u32[]{:S(2)}) %collective-permute-start.16) | collective-permute-done | bytes 131104 | tf_op jit(solution)/shard_map/ppermute | solution.py:509
  88.0 8.3 %collective-permute-start.17 = (bf16[8,16,4096]{2,1,0:T(8,128)(2,1)S(1)}, bf16[8,16,4096]{2,1,0:T(8,128)(2,1)S(1)}, u32[]{:S(2)}, u32[]{:S(2)}) collective-permute-start(bf16[8,16,4096]{2,1,0:T(8,128)(2,1)S(1)} %bitcast_dynamic-update-slice_fusion.own_core), channel_id=1, source_target_pairs={{0,1},{1,0},{4,5},{5,4},{8,9},{9,8},{12,13},{13,12},{14,15},{15,14... | collective-permute-start | bytes 3145736 | tf_op jit(solution)/shard_map/ppermute | solution.py:517
  96.2 0.1 stack.62
  96.3 5.6 %all-to-all-start.2 = ((bf16[16,8,16,128]{3,2,1,0:T(8,128)(2,1)}), bf16[16,8,16,128]{3,2,1,0:T(8,128)(2,1)S(1)}, u32[]{:S(2)}, u32[]{:S(2)}) async-start(bf16[16,8,16,128]{3,2,1,0:T(8,128)(2,1)} %shard_map.89.moved), calls=%async_computation.2 | async-start | bytes 1048576 | tf_op jit(solution)/shard_map/all_to_all | solution.py:461
  101.9 0.1 pad_add_fusion.spots
  102.0 0.0 collective-permute-done.17.other_core
  102.0 14.1 %shard_map.91 = bf16[16,16,16,256]{3,2,1,0:T(8,128)(2,1)} custom-call(s32[16]{0:T(128)S(1)} %pad_add_fusion.spots, bf16[8,16,4096]{2,1,0:T(8,128)(2,1)S(1)} %bitcast_dynamic-update-slice_fusion.own_core, bf16[8,16,4096]{2,1,0:T(8,128)(2,1)S(1)} %collective-permute-done.17.other_core, bf16[16,4096,256]{2,1,0:T(8,128)(2,1)} %shard_map.87.chol), custom_call_target="tpu_custom_call" | custom-call | flops 8589934592 | bytes 33554432 | tf_op jit(solution)/shard_map/pallas_call | solution.py:221
  116.0 0.0 all-to-all-done.2
  116.1 0.0 copy-start.2
  116.1 0.8 copy-done.2
  116.9 6.0 %all-to-all-start.1 = ((bf16[16,16,16,256]{3,2,1,0:T(8,128)(2,1)}), bf16[16,16,16,256]{3,2,1,0:T(8,128)(2,1)S(1)}, u32[]{:S(2)}, u32[]{:S(2)}) async-start(bf16[16,16,16,256]{3,2,1,0:T(8,128)(2,1)} %shard_map.91), calls=%async_computation.1 | async-start | bytes 4194304 | tf_op jit(solution)/shard_map/all_to_all | solution.py:521
  122.9 2.4 %reshape.137 = bf16[16,8,16,2,64]{4,3,2,1,0:T(2,128)(2,1)S(1)} reshape(bf16[16,8,16,128]{3,2,1,0:T(8,128)(2,1)} %copy-done.2) | data formatting | bytes 1048576 | tf_op jit(solution)/shard_map/reshape | solution.py:463
  125.3 1.2 copy.12
  126.6 2.0 %copy.13.orbitals = bf16[16,64,256]{2,1,0:T(8,128)(2,1)S(1)} copy(bf16[16,64,256]{1,0,2:T(8,128)(2,1)} %bitcast.131) | data formatting | bytes 1048576 | tf_op jit(solution)/shard_map/reshape | solution.py:464
  128.5 41.7 %all-to-all-done.1.got = bf16[16,16,16,256]{3,2,1,0:T(8,128)(2,1)S(1)} async-done(((bf16[16,16,16,256]{3,2,1,0:T(8,128)(2,1)}), bf16[16,16,16,256]{3,2,1,0:T(8,128)(2,1)S(1)}, u32[]{:S(2)}, u32[]{:S(2)}) %all-to-all-start.1) | async-done | bytes 2097184 | tf_op jit(solution)/shard_map/all_to_all | solution.py:521
  170.3 4.0 %shard_map.92 = bf16[16,64,256]{2,1,0:T(8,128)(2,1)} custom-call(bf16[16,16,16,256]{3,2,1,0:T(8,128)(2,1)S(1)} %all-to-all-done.1.got, bf16[16,64,256]{2,1,0:T(8,128)(2,1)S(1)} %copy.13.orbitals), custom_call_target="tpu_custom_call" | custom-call | flops 536870912 | bytes 4194304 | tf_op jit(solution)/shard_map/pallas_call | solution.py:379
  (24 shorter events, 0.3 us)
Async XLA Ops:
  0.6 10.5 %copy-start.3 = (s32[16]{0:T(128)S(1)}, s32[16]{0:T(128)}, u32[]{:S(2)}) copy-start(s32[16]{0:T(128)} %param.10) | copy-start | bytes 196
  4.5 32.9 %all-to-all-start = ((bf16[16,17,16,128]{3,2,1,0:T(8,128)(2,1)}), bf16[16,17,16,128]{3,2,1,0:T(8,128)(2,1)S(1)}, u32[]{:S(2)}, u32[]{:S(2)}) async-start(bf16[16,17,16,128]{3,2,1,0:T(8,128)(2,1)} %shard_map.86), calls=%async_computation | async-start | bytes 2228224 | tf_op jit(solution)/shard_map/all_to_all | solution.py:428
  11.2 26.7 %copy-start.1 = (bf16[256,64]{0,1:T(8,128)(2,1)S(1)}, bf16[256,64]{0,1:T(8,128)(2,1)}, u32[]{:S(2)}) copy-start(bf16[256,64]{0,1:T(8,128)(2,1)} %param.11) | copy-start | bytes 98308
  51.7 1.6 collective-permute-start.1
  52.0 6.7 %collective-permute-start.7 = (bf16[2,16,4096]{2,1,0:T(8,128)(2,1)S(1)}, bf16[2,16,4096]{2,1,0:T(8,128)(2,1)S(1)}, u32[]{:S(2)}, u32[]{:S(2)}) collective-permute-start(bf16[2,16,4096]{2,1,0:T(8,128)(2,1)S(1)} %get-tuple-element.12), channel_id=1, source_target_pairs={{0,1},{1,0},{4,5},{5,4},{8,9},{9,8},{12,13},{13,12},{14,15},{15,14... | collective-permute-start | bytes 786440 | tf_op jit(solution)/shard_map/ppermute | solution.py:474
  52.4 5.9 %collective-permute-start = (bf16[4,16,4096]{2,1,0:T(8,128)(2,1)S(1)}, bf16[4,16,4096]{2,1,0:T(8,128)(2,1)S(1)}, u32[]{:S(2)}, u32[]{:S(2)}) collective-permute-start(bf16[4,16,4096]{2,1,0:T(8,128)(2,1)S(1)} %slice_bitcast_fusion), channel_id=1, source_target_pairs={{0,1},{1,0},{4,5},{5,4},{8,9},{9,8},{12,13},{13,12},{14,15},{15,14... | collective-permute-start | bytes 1572872 | tf_op jit(solution)/shard_map/ppermute | solution.py:474
  53.3 4.9 %collective-permute-start.2 = (bf16[16,4096]{1,0:T(8,128)(2,1)S(1)}, bf16[16,4096]{1,0:T(8,128)(2,1)S(1)}, u32[]{:S(2)}, u32[]{:S(2)}) collective-permute-start(bf16[16,4096]{1,0:T(8,128)(2,1)S(1)} %fusion.11), channel_id=1, source_target_pairs={{0,4},{1,5},{4,8},{5,9},{8,12},{9,13},{12,14},{13,15},{14,10},{15,... | collective-permute-start | bytes 393224 | tf_op jit(solution)/shard_map/ppermute | solution.py:493
  53.5 5.3 %collective-permute-start.6 = (bf16[2,8,4096]{2,1,0:T(8,128)(2,1)S(1)}, bf16[2,8,4096]{2,1,0:T(8,128)(2,1)S(1)}, u32[]{:S(2)}, u32[]{:S(2)}) collective-permute-start(bf16[2,8,4096]{2,1,0:T(8,128)(2,1)S(1)} %fusion.4), channel_id=1, source_target_pairs={{0,2},{1,3},{4,0},{5,1},{8,4},{9,5},{12,8},{13,9},{14,12},{15,13},... | collective-permute-start | bytes 393224 | tf_op jit(solution)/shard_map/ppermute | solution.py:495
  58.3 11.8 %copy-start = (f32[16,4096]{1,0:T(8,128)S(1)}, f32[16,4096]{1,0:T(8,128)}, u32[]{:S(2)}) copy-start(f32[16,4096]{1,0:T(8,128)} %noise.1) | copy-start | bytes 786436
  58.4 3.9 %collective-permute-start.3 = (bf16[16,4096]{1,0:T(8,128)(2,1)S(1)}, bf16[16,4096]{1,0:T(8,128)(2,1)S(1)}, u32[]{:S(2)}, u32[]{:S(2)}) collective-permute-start(bf16[16,4096]{1,0:T(8,128)(2,1)S(1)} %fusion.10), channel_id=1, source_target_pairs={{0,4},{1,5},{4,8},{5,9},{8,12},{9,13},{12,14},{13,15},{14,10},{15,... | collective-permute-start | bytes 393224 | tf_op jit(solution)/shard_map/ppermute | solution.py:493
  58.8 4.4 %collective-permute-start.8 = (bf16[2,8,4096]{2,1,0:T(8,128)(2,1)S(1)}, bf16[2,8,4096]{2,1,0:T(8,128)(2,1)S(1)}, u32[]{:S(2)}, u32[]{:S(2)}) collective-permute-start(bf16[2,8,4096]{2,1,0:T(8,128)(2,1)S(1)} %fusion.3), channel_id=1, source_target_pairs={{0,2},{1,3},{4,0},{5,1},{8,4},{9,5},{12,8},{13,9},{14,12},{15,13},... | collective-permute-start | bytes 393224 | tf_op jit(solution)/shard_map/ppermute | solution.py:495
  62.3 3.9 %collective-permute-start.4 = (bf16[16,4096]{1,0:T(8,128)(2,1)S(1)}, bf16[16,4096]{1,0:T(8,128)(2,1)S(1)}, u32[]{:S(2)}, u32[]{:S(2)}) collective-permute-start(bf16[16,4096]{1,0:T(8,128)(2,1)S(1)} %fusion.8), channel_id=1, source_target_pairs={{0,4},{1,5},{4,8},{5,9},{8,12},{9,13},{12,14},{13,15},{14,10},{15,... | collective-permute-start | bytes 393224 | tf_op jit(solution)/shard_map/ppermute | solution.py:493
  63.2 5.5 %collective-permute-start.9 = (bf16[2,8,4096]{2,1,0:T(8,128)(2,1)S(1)}, bf16[2,8,4096]{2,1,0:T(8,128)(2,1)S(1)}, u32[]{:S(2)}, u32[]{:S(2)}) collective-permute-start(bf16[2,8,4096]{2,1,0:T(8,128)(2,1)S(1)} %fusion.1), channel_id=1, source_target_pairs={{0,2},{1,3},{4,0},{5,1},{8,4},{9,5},{12,8},{13,9},{14,12},{15,13},... | collective-permute-start | bytes 393224 | tf_op jit(solution)/shard_map/ppermute | solution.py:495
  66.2 4.0 %collective-permute-start.5 = (bf16[16,4096]{1,0:T(8,128)(2,1)S(1)}, bf16[16,4096]{1,0:T(8,128)(2,1)S(1)}, u32[]{:S(2)}, u32[]{:S(2)}) collective-permute-start(bf16[16,4096]{1,0:T(8,128)(2,1)S(1)} %get-tuple-element.10), channel_id=1, source_target_pairs={{0,4},{1,5},{4,8},{5,9},{8,12},{9,13},{12,14},{13,15},{14,10},{15,... | collective-permute-start | bytes 393224 | tf_op jit(solution)/shard_map/ppermute | solution.py:493
  71.0 3.8 %collective-permute-start.11 = (bf16[16,4096]{1,0:T(8,128)(2,1)S(1)}, bf16[16,4096]{1,0:T(8,128)(2,1)S(1)}, u32[]{:S(2)}, u32[]{:S(2)}) collective-permute-start(bf16[16,4096]{1,0:T(8,128)(2,1)S(1)} %get-tuple-element.4), channel_id=1, source_target_pairs={{0,2},{1,3},{4,0},{5,1},{8,4},{9,5},{12,8},{13,9},{14,12},{15,13},... | collective-permute-start | bytes 393224 | tf_op jit(solution)/shard_map/ppermute | solution.py:513
  71.2 4.2 %collective-permute-start.10 = (bf16[16,4096]{1,0:T(8,128)(2,1)S(1)}, bf16[16,4096]{1,0:T(8,128)(2,1)S(1)}, u32[]{:S(2)}, u32[]{:S(2)}) collective-permute-start(bf16[16,4096]{1,0:T(8,128)(2,1)S(1)} %get-tuple-element.4), channel_id=1, source_target_pairs={{0,4},{1,5},{4,8},{5,9},{8,12},{9,13},{12,14},{13,15},{14,10},{15,... | collective-permute-start | bytes 393224 | tf_op jit(solution)/shard_map/ppermute | solution.py:509
  74.8 3.8 %collective-permute-start.13 = (bf16[16,4096]{1,0:T(8,128)(2,1)S(1)}, bf16[16,4096]{1,0:T(8,128)(2,1)S(1)}, u32[]{:S(2)}, u32[]{:S(2)}) collective-permute-start(bf16[16,4096]{1,0:T(8,128)(2,1)S(1)} %collective-permute-done.11), channel_id=1, source_target_pairs={{0,2},{1,3},{4,0},{5,1},{8,4},{9,5},{12,8},{13,9},{14,12},{15,13},... | collective-permute-start | bytes 393224 | tf_op jit(solution)/shard_map/ppermute | solution.py:513
  75.3 4.7 %collective-permute-start.12 = (bf16[16,4096]{1,0:T(8,128)(2,1)S(1)}, bf16[16,4096]{1,0:T(8,128)(2,1)S(1)}, u32[]{:S(2)}, u32[]{:S(2)}) collective-permute-start(bf16[16,4096]{1,0:T(8,128)(2,1)S(1)} %collective-permute-done.10), channel_id=1, source_target_pairs={{0,4},{1,5},{4,8},{5,9},{8,12},{9,13},{12,14},{13,15},{14,10},{15,... | collective-permute-start | bytes 393224 | tf_op jit(solution)/shard_map/ppermute | solution.py:509
  78.6 6.1 %collective-permute-start.15 = (bf16[16,4096]{1,0:T(8,128)(2,1)S(1)}, bf16[16,4096]{1,0:T(8,128)(2,1)S(1)}, u32[]{:S(2)}, u32[]{:S(2)}) collective-permute-start(bf16[16,4096]{1,0:T(8,128)(2,1)S(1)} %collective-permute-done.13), channel_id=1, source_target_pairs={{0,2},{1,3},{4,0},{5,1},{8,4},{9,5},{12,8},{13,9},{14,12},{15,13},... | collective-permute-start | bytes 393224 | tf_op jit(solution)/shard_map/ppermute | solution.py:513
  80.0 4.1 %collective-permute-start.14 = (bf16[16,4096]{1,0:T(8,128)(2,1)S(1)}, bf16[16,4096]{1,0:T(8,128)(2,1)S(1)}, u32[]{:S(2)}, u32[]{:S(2)}) collective-permute-start(bf16[16,4096]{1,0:T(8,128)(2,1)S(1)} %collective-permute-done.12), channel_id=1, source_target_pairs={{0,4},{1,5},{4,8},{5,9},{8,12},{9,13},{12,14},{13,15},{14,10},{15,... | collective-permute-start | bytes 393224 | tf_op jit(solution)/shard_map/ppermute | solution.py:509
  84.1 3.8 %collective-permute-start.16 = (bf16[16,4096]{1,0:T(8,128)(2,1)S(1)}, bf16[16,4096]{1,0:T(8,128)(2,1)S(1)}, u32[]{:S(2)}, u32[]{:S(2)}) collective-permute-start(bf16[16,4096]{1,0:T(8,128)(2,1)S(1)} %collective-permute-done.14), channel_id=1, source_target_pairs={{0,4},{1,5},{4,8},{5,9},{8,12},{9,13},{12,14},{13,15},{14,10},{15,... | collective-permute-start | bytes 393224 | tf_op jit(solution)/shard_map/ppermute | solution.py:509
  88.0 14.0 %collective-permute-start.17 = (bf16[8,16,4096]{2,1,0:T(8,128)(2,1)S(1)}, bf16[8,16,4096]{2,1,0:T(8,128)(2,1)S(1)}, u32[]{:S(2)}, u32[]{:S(2)}) collective-permute-start(bf16[8,16,4096]{2,1,0:T(8,128)(2,1)S(1)} %bitcast_dynamic-update-slice_fusion.own_core), channel_id=1, source_target_pairs={{0,1},{1,0},{4,5},{5,4},{8,9},{9,8},{12,13},{13,12},{14,15},{15,14... | collective-permute-start | bytes 3145736 | tf_op jit(solution)/shard_map/ppermute | solution.py:517
  96.3 19.7 %all-to-all-start.2 = ((bf16[16,8,16,128]{3,2,1,0:T(8,128)(2,1)}), bf16[16,8,16,128]{3,2,1,0:T(8,128)(2,1)S(1)}, u32[]{:S(2)}, u32[]{:S(2)}) async-start(bf16[16,8,16,128]{3,2,1,0:T(8,128)(2,1)} %shard_map.89.moved), calls=%async_computation.2 | async-start | bytes 1048576 | tf_op jit(solution)/shard_map/all_to_all | solution.py:461
  116.1 0.8 copy-start.2
  116.9 53.4 %all-to-all-start.1 = ((bf16[16,16,16,256]{3,2,1,0:T(8,128)(2,1)}), bf16[16,16,16,256]{3,2,1,0:T(8,128)(2,1)S(1)}, u32[]{:S(2)}, u32[]{:S(2)}) async-start(bf16[16,16,16,256]{3,2,1,0:T(8,128)(2,1)} %shard_map.91), calls=%async_computation.1 | async-start | bytes 4194304 | tf_op jit(solution)/shard_map/all_to_all | solution.py:521

commit v7 on v6

--- a/solution.py
+++ b/solution.py
@@ -505,14 +505,17 @@
 
     pieces, offsets = [fields], [0]
     going_right = going_left = fields
-    for t in range(to_right):
+    for t in range(to_left):
         going_right = lax.ppermute(going_right, "row", right)
-        pieces.append(going_right)
-        offsets.append(-(t + 1))
-        if t < to_left:
-            going_left = lax.ppermute(going_left, "row", left)
-            pieces.append(going_left)
-            offsets.append(t + 1)
+        going_left = lax.ppermute(going_left, "row", left)
+        pieces += [going_right, going_left]
+        offsets += [-(t + 1), t + 1]
+    if to_right > to_left:
+        half = per_device // 2
+        upper = lax.ppermute(going_right[:half], "row", right)
+        lower = lax.ppermute(going_left[half:], "row", left)
+        pieces.append(jnp.concatenate([upper, lower], axis=0))
+        offsets.append(-to_right)
     own_core = jnp.stack(pieces)
     other_core = lax.ppermute(own_core, "row", swap)
     spots = jnp.stack([2 * chip_at((own_place + offset) % chips) for offset in offsets])

time: 175 us -> 174 us (level)
    ppermute x4 -> x3, waiting for transfers between devices: 7.46 us -> 1.52 us  [local(): going_right = lax.ppermute(going_right, 'row', right)]
    ppermute x0 -> x2, waiting for transfers between devices: none -> 2.35 us  [the longest x1 1.54 us: local(): lower = lax.ppermute(going_left[half:], 'row', left)]
    ppermute x3, waiting for transfers between devices: 4.66 us -> 6.97 us  [local(): going_left = lax.ppermute(going_left, 'row', left)]
  transfers between devices with their start and end apart: 21 -> 22, of which waited for: 13 -> 15; matrix products, arithmetic and copies ran while one was open for 4% -> 4% of each run, Pallas kernels for 22% -> 22%
where the time goes in v7:
time: 174 us
  waiting for transfers between devices  65.8 us (38%)
  Pallas kernels  60.9 us (35%)
  starting transfers between devices  38.7 us (22%)
  local copies, waits for them, and re-layouts  6.79 us (4%)
    all_to_all x1, waiting for transfers between devices, local(): got = lax.all_to_all(propagator_part, 'row', 0, 0, tiled=True)  41.7 us
    pallas_call x1, Pallas kernels, chol_by_row(): pl.pallas_call(by_row_kernel, in_specs=[in_hbm], out_specs=in_hbm, out_sh...  22.9 us
    pallas_call x1, Pallas kernels, propagator_parts(): pl.pallas_call(propagator_kernel, in_specs=[pl.BlockSpec(memory_space=plt...  14.1 us
    pallas_call x1, Pallas kernels, bias_parts(): pl.pallas_call(bias_kernel, in_specs=[whole_vmem] * 3 + [in_hbm], out_spe...  13.7 us
    ppermute x4, waiting for transfers between devices, local(): moving_right = lax.ppermute(moving_right, 'row', right)  9.21 us
    ppermute x1, starting transfers between devices, local(): other_core = lax.ppermute(own_core, 'row', swap)  8.27 us
    ppermute x3, waiting for transfers between devices, local(): going_left = lax.ppermute(going_left, 'row', left)  6.97 us
    all_to_all x1, starting transfers between devices, local(): lax.all_to_all(payload(copies, jnp.transpose(walkers, (0, 2, 1)), inv_int...  6.57 us
  transfers between devices with their start and end apart: 22, of which 15 were waited for; matrix products, arithmetic and copies ran while one was open for 4% of the time, Pallas kernels for 22%

profile of v7, /device:TPU:15, one launch (start us, length us, event | category | flops | bytes accessed | tf_op | source)
XLA Modules:
  0.0 174.0 jit_solution(8465052040594248457)
XLA Ops:
  0.6 3.9 %shard_map.86 = bf16[16,17,16,128]{3,2,1,0:T(8,128)(2,1)} custom-call(s32[16]{0:T(128)} %copies.1, bf16[16,64,256]{2,1,0:T(8,128)(2,1)} %bitcast.134, bf16[16,64,64]{2,1,0:T(8,128)(2,1)} %from_inverse.1), custom_call_target="tpu_custom_call" | custom-call | flops 67108864 | bytes 1572864 | tf_op jit(solution)/shard_map/pallas_call | solution.py:322
  4.5 6.6 %all-to-all-start = ((bf16[16,17,16,128]{3,2,1,0:T(8,128)(2,1)}), bf16[16,17,16,128]{3,2,1,0:T(8,128)(2,1)S(1)}, u32[]{:S(2)}, u32[]{:S(2)}) async-start(bf16[16,17,16,128]{3,2,1,0:T(8,128)(2,1)} %shard_map.86), calls=%async_computation | async-start | bytes 2228224 | tf_op jit(solution)/shard_map/all_to_all | solution.py:428
  11.2 0.1 select_reduce_fusion.2
  11.3 22.9 %shard_map.87.chol = bf16[16,4096,256]{2,1,0:T(8,128)(2,1)} custom-call(bf16[4096,16,256]{2,1,0:T(8,128)(2,1)} %chol.1), custom_call_target="tpu_custom_call" | custom-call | flops 8589934592 | bytes 67108864 | tf_op jit(solution)/shard_map/pallas_call | solution.py:110
  34.2 3.3 %all-to-all-done.first = bf16[16,17,16,128]{3,2,1,0:T(8,128)(2,1)S(1)} async-done(((bf16[16,17,16,128]{3,2,1,0:T(8,128)(2,1)}), bf16[16,17,16,128]{3,2,1,0:T(8,128)(2,1)S(1)}, u32[]{:S(2)}, u32[]{:S(2)}) %all-to-all-start) | async-done | bytes 1114144 | tf_op jit(solution)/shard_map/all_to_all | solution.py:428
  37.5 0.1 convert_reduce_fusion
  37.6 0.1 reshape.139
  37.7 0.1 select_reduce_fusion.1
  37.8 0.1 and_convert_fusion
  37.9 13.7 %shard_map.88 = bf16[256,4096]{1,0:T(8,128)(2,1)S(1)} custom-call(bf16[256,256]{1,0:T(8,128)(2,1)S(1)} %get-tuple-element.15.pick, bf16[16,17,16,128]{3,2,1,0:T(8,128)(2,1)S(1)} %all-to-all-done.first, bf16[64,256]{1,0:T(8,128)(2,1)S(1)} %bitcast.132, bf16[16,4096,256]{2,1,0:T(8,128)(2,1)} %shard_map.87.chol), custom_call_target="tpu_custom_call" | custom-call | flops 8589934592 | bytes 33554432 | tf_op jit(solution)/shard_map/pallas_call | solution.py:160
  51.7 0.3 collective-permute-start.1
  52.0 0.4 collective-permute-start.7
  52.4 0.2 collective-permute-start
  52.6 0.7 collective-permute-done.1
  53.4 0.1 collective-permute-start.2
  53.5 1.5 collective-permute-start.6
  55.0 3.3 %collective-permute-done.2 = bf16[16,4096]{1,0:T(8,128)(2,1)S(1)} collective-permute-done((bf16[16,4096]{1,0:T(8,128)(2,1)S(1)}, bf16[16,4096]{1,0:T(8,128)(2,1)S(1)}, u32[]{:S(2)}, u32[]{:S(2)}) %collective-permute-start.2) | collective-permute-done | bytes 131104 | tf_op jit(solution)/shard_map/ppermute | solution.py:493
  58.3 0.1 fusion.10
  58.4 0.0 copy-start
  58.4 0.4 collective-permute-start.3
  58.7 0.0 collective-permute-done.7
  58.8 0.0 collective-permute-done.6
  58.8 0.1 fusion.3
  58.8 1.2 collective-permute-start.8
  60.0 2.2 %collective-permute-done.3 = bf16[16,4096]{1,0:T(8,128)(2,1)S(1)} collective-permute-done((bf16[16,4096]{1,0:T(8,128)(2,1)S(1)}, bf16[16,4096]{1,0:T(8,128)(2,1)S(1)}, u32[]{:S(2)}, u32[]{:S(2)}) %collective-permute-start.3) | collective-permute-done | bytes 131104 | tf_op jit(solution)/shard_map/ppermute | solution.py:493
  62.2 0.1 fusion.8
  62.3 0.9 collective-permute-start.4
  63.2 0.1 fusion.1
  63.3 0.8 collective-permute-start.9
  64.0 2.1 %collective-permute-done.4 = bf16[16,4096]{1,0:T(8,128)(2,1)S(1)} collective-permute-done((bf16[16,4096]{1,0:T(8,128)(2,1)S(1)}, bf16[16,4096]{1,0:T(8,128)(2,1)S(1)}, u32[]{:S(2)}, u32[]{:S(2)}) %collective-permute-start.4) | collective-permute-done | bytes 131104 | tf_op jit(solution)/shard_map/ppermute | solution.py:493
  66.2 0.1 fusion.6
  66.3 0.9 collective-permute-start.5
  67.1 1.6 shard_map.89.moved
  68.7 1.5 collective-permute-done.5.from_left
  70.2 0.8 shard_map.90
  71.0 0.2 collective-permute-start.11
  71.2 1.3 collective-permute-start.10
  72.4 2.3 %collective-permute-done.11 = bf16[16,4096]{1,0:T(8,128)(2,1)S(1)} collective-permute-done((bf16[16,4096]{1,0:T(8,128)(2,1)S(1)}, bf16[16,4096]{1,0:T(8,128)(2,1)S(1)}, u32[]{:S(2)}, u32[]{:S(2)}) %collective-permute-start.11) | collective-permute-done | bytes 131104 | tf_op jit(solution)/shard_map/ppermute | solution.py:510
  74.8 0.2 collective-permute-start.13
  75.0 0.4 collective-permute-done.10
  75.3 0.9 collective-permute-start.12
  76.3 2.3 %collective-permute-done.13 = bf16[16,4096]{1,0:T(8,128)(2,1)S(1)} collective-permute-done((bf16[16,4096]{1,0:T(8,128)(2,1)S(1)}, bf16[16,4096]{1,0:T(8,128)(2,1)S(1)}, u32[]{:S(2)}, u32[]{:S(2)}) %collective-permute-start.13) | collective-permute-done | bytes 131104 | tf_op jit(solution)/shard_map/ppermute | solution.py:510
  78.6 1.0 collective-permute-start.15
  79.6 0.4 collective-permute-done.12
  80.0 0.6 collective-permute-start.14
  80.7 2.3 %collective-permute-done.15 = bf16[16,4096]{1,0:T(8,128)(2,1)S(1)} collective-permute-done((bf16[16,4096]{1,0:T(8,128)(2,1)S(1)}, bf16[16,4096]{1,0:T(8,128)(2,1)S(1)}, u32[]{:S(2)}, u32[]{:S(2)}) %collective-permute-start.15) | collective-permute-done | bytes 131104 | tf_op jit(solution)/shard_map/ppermute | solution.py:510
  83.0 0.4 collective-permute-start.17
  83.4 0.7 collective-permute-done.14
  84.1 0.7 collective-permute-start.16
  84.9 1.5 collective-permute-done.17
  86.4 0.8 collective-permute-done.16
  87.3 8.3 %collective-permute-start.18 = (bf16[8,16,4096]{2,1,0:T(8,128)(2,1)S(1)}, bf16[8,16,4096]{2,1,0:T(8,128)(2,1)S(1)}, u32[]{:S(2)}, u32[]{:S(2)}) collective-permute-start(bf16[8,16,4096]{2,1,0:T(8,128)(2,1)S(1)} %fusion.12.own_core), channel_id=1, source_target_pairs={{0,1},{1,0},{4,5},{5,4},{8,9},{9,8},{12,13},{13,12},{14,15},{15,14... | collective-permute-start | bytes 3145736 | tf_op jit(solution)/shard_map/ppermute | solution.py:520
  95.5 0.1 stack.62
  95.6 6.0 %all-to-all-start.2 = ((bf16[16,8,16,128]{3,2,1,0:T(8,128)(2,1)}), bf16[16,8,16,128]{3,2,1,0:T(8,128)(2,1)S(1)}, u32[]{:S(2)}, u32[]{:S(2)}) async-start(bf16[16,8,16,128]{3,2,1,0:T(8,128)(2,1)} %shard_map.89.moved), calls=%async_computation.2 | async-start | bytes 1048576 | tf_op jit(solution)/shard_map/all_to_all | solution.py:461
  101.6 0.1 pad_add_fusion.spots
  101.7 14.1 %shard_map.91 = bf16[16,16,16,256]{3,2,1,0:T(8,128)(2,1)} custom-call(s32[16]{0:T(128)S(1)} %pad_add_fusion.spots, bf16[8,16,4096]{2,1,0:T(8,128)(2,1)S(1)} %fusion.12.own_core, bf16[8,16,4096]{2,1,0:T(8,128)(2,1)S(1)} %collective-permute-done.18.other_core, bf16[16,4096,256]{2,1,0:T(8,128)(2,1)} %shard_map.87.chol), custom_call_target="tpu_custom_call" | custom-call | flops 8589934592 | bytes 33554432 | tf_op jit(solution)/shard_map/pallas_call | solution.py:221
  115.8 0.0 copy-start.2
  115.8 0.8 copy-done.2
  116.6 6.0 %all-to-all-start.1 = ((bf16[16,16,16,256]{3,2,1,0:T(8,128)(2,1)}), bf16[16,16,16,256]{3,2,1,0:T(8,128)(2,1)S(1)}, u32[]{:S(2)}, u32[]{:S(2)}) async-start(bf16[16,16,16,256]{3,2,1,0:T(8,128)(2,1)} %shard_map.91), calls=%async_computation.1 | async-start | bytes 4194304 | tf_op jit(solution)/shard_map/all_to_all | solution.py:524
  122.6 2.4 %reshape.137 = bf16[16,8,16,2,64]{4,3,2,1,0:T(2,128)(2,1)S(1)} reshape(bf16[16,8,16,128]{3,2,1,0:T(8,128)(2,1)} %copy-done.2) | data formatting | bytes 1048576 | tf_op jit(solution)/shard_map/reshape | solution.py:463
  125.1 1.3 copy.12
  126.3 2.0 %copy.13.orbitals = bf16[16,64,256]{2,1,0:T(8,128)(2,1)S(1)} copy(bf16[16,64,256]{1,0,2:T(8,128)(2,1)} %bitcast.133) | data formatting | bytes 1048576 | tf_op jit(solution)/shard_map/reshape | solution.py:464
  128.3 41.7 %all-to-all-done.1.got = bf16[16,16,16,256]{3,2,1,0:T(8,128)(2,1)S(1)} async-done(((bf16[16,16,16,256]{3,2,1,0:T(8,128)(2,1)}), bf16[16,16,16,256]{3,2,1,0:T(8,128)(2,1)S(1)}, u32[]{:S(2)}, u32[]{:S(2)}) %all-to-all-start.1) | async-done | bytes 2097184 | tf_op jit(solution)/shard_map/all_to_all | solution.py:524
  170.0 4.0 %shard_map.92 = bf16[16,64,256]{2,1,0:T(8,128)(2,1)} custom-call(bf16[16,16,16,256]{3,2,1,0:T(8,128)(2,1)S(1)} %all-to-all-done.1.got, bf16[16,64,256]{2,1,0:T(8,128)(2,1)S(1)} %copy.13.orbitals), custom_call_target="tpu_custom_call" | custom-call | flops 536870912 | bytes 4194304 | tf_op jit(solution)/shard_map/pallas_call | solution.py:379
  (28 shorter events, 0.3 us)
Async XLA Ops:
  0.6 10.5 %copy-start.3 = (s32[16]{0:T(128)S(1)}, s32[16]{0:T(128)}, u32[]{:S(2)}) copy-start(s32[16]{0:T(128)} %param.10) | copy-start | bytes 196
  4.5 32.9 %all-to-all-start = ((bf16[16,17,16,128]{3,2,1,0:T(8,128)(2,1)}), bf16[16,17,16,128]{3,2,1,0:T(8,128)(2,1)S(1)}, u32[]{:S(2)}, u32[]{:S(2)}) async-start(bf16[16,17,16,128]{3,2,1,0:T(8,128)(2,1)} %shard_map.86), calls=%async_computation | async-start | bytes 2228224 | tf_op jit(solution)/shard_map/all_to_all | solution.py:428
  11.2 26.7 %copy-start.1 = (bf16[256,64]{0,1:T(8,128)(2,1)S(1)}, bf16[256,64]{0,1:T(8,128)(2,1)}, u32[]{:S(2)}) copy-start(bf16[256,64]{0,1:T(8,128)(2,1)} %param.11) | copy-start | bytes 98308
  51.7 1.6 collective-permute-start.1
  52.0 6.7 %collective-permute-start.7 = (bf16[2,16,4096]{2,1,0:T(8,128)(2,1)S(1)}, bf16[2,16,4096]{2,1,0:T(8,128)(2,1)S(1)}, u32[]{:S(2)}, u32[]{:S(2)}) collective-permute-start(bf16[2,16,4096]{2,1,0:T(8,128)(2,1)S(1)} %get-tuple-element.12), channel_id=1, source_target_pairs={{0,1},{1,0},{4,5},{5,4},{8,9},{9,8},{12,13},{13,12},{14,15},{15,14... | collective-permute-start | bytes 786440 | tf_op jit(solution)/shard_map/ppermute | solution.py:474
  52.4 5.9 %collective-permute-start = (bf16[4,16,4096]{2,1,0:T(8,128)(2,1)S(1)}, bf16[4,16,4096]{2,1,0:T(8,128)(2,1)S(1)}, u32[]{:S(2)}, u32[]{:S(2)}) collective-permute-start(bf16[4,16,4096]{2,1,0:T(8,128)(2,1)S(1)} %slice_bitcast_fusion), channel_id=1, source_target_pairs={{0,1},{1,0},{4,5},{5,4},{8,9},{9,8},{12,13},{13,12},{14,15},{15,14... | collective-permute-start | bytes 1572872 | tf_op jit(solution)/shard_map/ppermute | solution.py:474
  53.4 4.9 %collective-permute-start.2 = (bf16[16,4096]{1,0:T(8,128)(2,1)S(1)}, bf16[16,4096]{1,0:T(8,128)(2,1)S(1)}, u32[]{:S(2)}, u32[]{:S(2)}) collective-permute-start(bf16[16,4096]{1,0:T(8,128)(2,1)S(1)} %fusion.11), channel_id=1, source_target_pairs={{0,4},{1,5},{4,8},{5,9},{8,12},{9,13},{12,14},{13,15},{14,10},{15,... | collective-permute-start | bytes 393224 | tf_op jit(solution)/shard_map/ppermute | solution.py:493
  53.5 5.3 %collective-permute-start.6 = (bf16[2,8,4096]{2,1,0:T(8,128)(2,1)S(1)}, bf16[2,8,4096]{2,1,0:T(8,128)(2,1)S(1)}, u32[]{:S(2)}, u32[]{:S(2)}) collective-permute-start(bf16[2,8,4096]{2,1,0:T(8,128)(2,1)S(1)} %fusion.4), channel_id=1, source_target_pairs={{0,2},{1,3},{4,0},{5,1},{8,4},{9,5},{12,8},{13,9},{14,12},{15,13},... | collective-permute-start | bytes 393224 | tf_op jit(solution)/shard_map/ppermute | solution.py:495
  58.4 11.8 %copy-start = (f32[16,4096]{1,0:T(8,128)S(1)}, f32[16,4096]{1,0:T(8,128)}, u32[]{:S(2)}) copy-start(f32[16,4096]{1,0:T(8,128)} %noise.1) | copy-start | bytes 786436
  58.4 3.9 %collective-permute-start.3 = (bf16[16,4096]{1,0:T(8,128)(2,1)S(1)}, bf16[16,4096]{1,0:T(8,128)(2,1)S(1)}, u32[]{:S(2)}, u32[]{:S(2)}) collective-permute-start(bf16[16,4096]{1,0:T(8,128)(2,1)S(1)} %fusion.10), channel_id=1, source_target_pairs={{0,4},{1,5},{4,8},{5,9},{8,12},{9,13},{12,14},{13,15},{14,10},{15,... | collective-permute-start | bytes 393224 | tf_op jit(solution)/shard_map/ppermute | solution.py:493
  58.8 4.4 %collective-permute-start.8 = (bf16[2,8,4096]{2,1,0:T(8,128)(2,1)S(1)}, bf16[2,8,4096]{2,1,0:T(8,128)(2,1)S(1)}, u32[]{:S(2)}, u32[]{:S(2)}) collective-permute-start(bf16[2,8,4096]{2,1,0:T(8,128)(2,1)S(1)} %fusion.3), channel_id=1, source_target_pairs={{0,2},{1,3},{4,0},{5,1},{8,4},{9,5},{12,8},{13,9},{14,12},{15,13},... | collective-permute-start | bytes 393224 | tf_op jit(solution)/shard_map/ppermute | solution.py:495
  62.3 3.9 %collective-permute-start.4 = (bf16[16,4096]{1,0:T(8,128)(2,1)S(1)}, bf16[16,4096]{1,0:T(8,128)(2,1)S(1)}, u32[]{:S(2)}, u32[]{:S(2)}) collective-permute-start(bf16[16,4096]{1,0:T(8,128)(2,1)S(1)} %fusion.8), channel_id=1, source_target_pairs={{0,4},{1,5},{4,8},{5,9},{8,12},{9,13},{12,14},{13,15},{14,10},{15,... | collective-permute-start | bytes 393224 | tf_op jit(solution)/shard_map/ppermute | solution.py:493
  63.3 5.5 %collective-permute-start.9 = (bf16[2,8,4096]{2,1,0:T(8,128)(2,1)S(1)}, bf16[2,8,4096]{2,1,0:T(8,128)(2,1)S(1)}, u32[]{:S(2)}, u32[]{:S(2)}) collective-permute-start(bf16[2,8,4096]{2,1,0:T(8,128)(2,1)S(1)} %fusion.1), channel_id=1, source_target_pairs={{0,2},{1,3},{4,0},{5,1},{8,4},{9,5},{12,8},{13,9},{14,12},{15,13},... | collective-permute-start | bytes 393224 | tf_op jit(solution)/shard_map/ppermute | solution.py:495
  66.3 4.0 %collective-permute-start.5 = (bf16[16,4096]{1,0:T(8,128)(2,1)S(1)}, bf16[16,4096]{1,0:T(8,128)(2,1)S(1)}, u32[]{:S(2)}, u32[]{:S(2)}) collective-permute-start(bf16[16,4096]{1,0:T(8,128)(2,1)S(1)} %get-tuple-element.10), channel_id=1, source_target_pairs={{0,4},{1,5},{4,8},{5,9},{8,12},{9,13},{12,14},{13,15},{14,10},{15,... | collective-permute-start | bytes 393224 | tf_op jit(solution)/shard_map/ppermute | solution.py:493
  71.0 3.8 %collective-permute-start.11 = (bf16[16,4096]{1,0:T(8,128)(2,1)S(1)}, bf16[16,4096]{1,0:T(8,128)(2,1)S(1)}, u32[]{:S(2)}, u32[]{:S(2)}) collective-permute-start(bf16[16,4096]{1,0:T(8,128)(2,1)S(1)} %get-tuple-element.4), channel_id=1, source_target_pairs={{0,2},{1,3},{4,0},{5,1},{8,4},{9,5},{12,8},{13,9},{14,12},{15,13},... | collective-permute-start | bytes 393224 | tf_op jit(solution)/shard_map/ppermute | solution.py:510
  71.2 4.2 %collective-permute-start.10 = (bf16[16,4096]{1,0:T(8,128)(2,1)S(1)}, bf16[16,4096]{1,0:T(8,128)(2,1)S(1)}, u32[]{:S(2)}, u32[]{:S(2)}) collective-permute-start(bf16[16,4096]{1,0:T(8,128)(2,1)S(1)} %get-tuple-element.4), channel_id=1, source_target_pairs={{0,4},{1,5},{4,8},{5,9},{8,12},{9,13},{12,14},{13,15},{14,10},{15,... | collective-permute-start | bytes 393224 | tf_op jit(solution)/shard_map/ppermute | solution.py:509
  74.8 3.8 %collective-permute-start.13 = (bf16[16,4096]{1,0:T(8,128)(2,1)S(1)}, bf16[16,4096]{1,0:T(8,128)(2,1)S(1)}, u32[]{:S(2)}, u32[]{:S(2)}) collective-permute-start(bf16[16,4096]{1,0:T(8,128)(2,1)S(1)} %collective-permute-done.11), channel_id=1, source_target_pairs={{0,2},{1,3},{4,0},{5,1},{8,4},{9,5},{12,8},{13,9},{14,12},{15,13},... | collective-permute-start | bytes 393224 | tf_op jit(solution)/shard_map/ppermute | solution.py:510
  75.3 4.7 %collective-permute-start.12 = (bf16[16,4096]{1,0:T(8,128)(2,1)S(1)}, bf16[16,4096]{1,0:T(8,128)(2,1)S(1)}, u32[]{:S(2)}, u32[]{:S(2)}) collective-permute-start(bf16[16,4096]{1,0:T(8,128)(2,1)S(1)} %collective-permute-done.10), channel_id=1, source_target_pairs={{0,4},{1,5},{4,8},{5,9},{8,12},{9,13},{12,14},{13,15},{14,10},{15,... | collective-permute-start | bytes 393224 | tf_op jit(solution)/shard_map/ppermute | solution.py:509
  78.6 4.4 %collective-permute-start.15 = (bf16[16,4096]{1,0:T(8,128)(2,1)S(1)}, bf16[16,4096]{1,0:T(8,128)(2,1)S(1)}, u32[]{:S(2)}, u32[]{:S(2)}) collective-permute-start(bf16[16,4096]{1,0:T(8,128)(2,1)S(1)} %collective-permute-done.13), channel_id=1, source_target_pairs={{0,2},{1,3},{4,0},{5,1},{8,4},{9,5},{12,8},{13,9},{14,12},{15,13},... | collective-permute-start | bytes 393224 | tf_op jit(solution)/shard_map/ppermute | solution.py:510
  80.0 4.1 %collective-permute-start.14 = (bf16[16,4096]{1,0:T(8,128)(2,1)S(1)}, bf16[16,4096]{1,0:T(8,128)(2,1)S(1)}, u32[]{:S(2)}, u32[]{:S(2)}) collective-permute-start(bf16[16,4096]{1,0:T(8,128)(2,1)S(1)} %collective-permute-done.12), channel_id=1, source_target_pairs={{0,4},{1,5},{4,8},{5,9},{8,12},{9,13},{12,14},{13,15},{14,10},{15,... | collective-permute-start | bytes 393224 | tf_op jit(solution)/shard_map/ppermute | solution.py:509
  83.0 3.5 %collective-permute-start.17 = (bf16[8,4096]{1,0:T(8,128)(2,1)S(1)}, bf16[8,4096]{1,0:T(8,128)(2,1)S(1)}, u32[]{:S(2)}, u32[]{:S(2)}) collective-permute-start(bf16[8,4096]{1,0:T(8,128)(2,1)S(1)} %slice.109), channel_id=1, source_target_pairs={{0,2},{1,3},{4,0},{5,1},{8,4},{9,5},{12,8},{13,9},{14,12},{15,13},... | collective-permute-start | bytes 196616 | tf_op jit(solution)/shard_map/ppermute | solution.py:516
  84.1 3.1 %collective-permute-start.16 = (bf16[8,4096]{1,0:T(8,128)(2,1)S(1)}, bf16[8,4096]{1,0:T(8,128)(2,1)S(1)}, u32[]{:S(2)}, u32[]{:S(2)}) collective-permute-start(bf16[8,4096]{1,0:T(8,128)(2,1)S(1)} %slice.108), channel_id=1, source_target_pairs={{0,4},{1,5},{4,8},{5,9},{8,12},{9,13},{12,14},{13,15},{14,10},{15,... | collective-permute-start | bytes 196616 | tf_op jit(solution)/shard_map/ppermute | solution.py:515
  87.3 14.4 %collective-permute-start.18 = (bf16[8,16,4096]{2,1,0:T(8,128)(2,1)S(1)}, bf16[8,16,4096]{2,1,0:T(8,128)(2,1)S(1)}, u32[]{:S(2)}, u32[]{:S(2)}) collective-permute-start(bf16[8,16,4096]{2,1,0:T(8,128)(2,1)S(1)} %fusion.12.own_core), channel_id=1, source_target_pairs={{0,1},{1,0},{4,5},{5,4},{8,9},{9,8},{12,13},{13,12},{14,15},{15,14... | collective-permute-start | bytes 3145736 | tf_op jit(solution)/shard_map/ppermute | solution.py:520
  95.6 20.1 %all-to-all-start.2 = ((bf16[16,8,16,128]{3,2,1,0:T(8,128)(2,1)}), bf16[16,8,16,128]{3,2,1,0:T(8,128)(2,1)S(1)}, u32[]{:S(2)}, u32[]{:S(2)}) async-start(bf16[16,8,16,128]{3,2,1,0:T(8,128)(2,1)} %shard_map.89.moved), calls=%async_computation.2 | async-start | bytes 1048576 | tf_op jit(solution)/shard_map/all_to_all | solution.py:461
  115.8 0.8 copy-start.2
  116.6 53.4 %all-to-all-start.1 = ((bf16[16,16,16,256]{3,2,1,0:T(8,128)(2,1)}), bf16[16,16,16,256]{3,2,1,0:T(8,128)(2,1)S(1)}, u32[]{:S(2)}, u32[]{:S(2)}) async-start(bf16[16,16,16,256]{3,2,1,0:T(8,128)(2,1)} %shard_map.91), calls=%async_computation.1 | async-start | bytes 4194304 | tf_op jit(solution)/shard_map/all_to_all | solution.py:524

commit v8 on v7

--- a/solution.py
+++ b/solution.py
@@ -26,12 +26,12 @@
 
 
 GROUP = 16
-SLOTS = 3
+SLOTS = 4
 SPAN = 512
 TOGETHER = 16
 PAYLOAD_MIB = 56
 DEPTH = 4096
-HELD = 5
+HELD = 8
 MADE = 4
 MIB = 1 << 20
 whole_vmem = pl.BlockSpec(memory_space=pltpu.VMEM)
@@ -167,7 +167,7 @@
             pltpu.VMEM((SLOTS, rows, span, width), bf16),
             pltpu.SemaphoreType.DMA((SLOTS,)),
         ],
-        compiler_params=pltpu.CompilerParams(vmem_limit_bytes=24 * MIB),
+        compiler_params=pltpu.CompilerParams(vmem_limit_bytes=32 * MIB),
         cost_estimate=pl.CostEstimate(
             flops=2 * everyone * by_row.size, bytes_accessed=2 * by_row.size, transcendentals=0
         ),
@@ -230,7 +230,7 @@
             pltpu.VMEM((SLOTS, divisor(rows, 2, 1), chol_n, width), bf16),
             pltpu.SemaphoreType.DMA((SLOTS,)),
         ],
-        compiler_params=pltpu.CompilerParams(vmem_limit_bytes=24 * MIB),
+        compiler_params=pltpu.CompilerParams(vmem_limit_bytes=32 * MIB),
         cost_estimate=pl.CostEstimate(
             flops=2 * devices * per_device * by_row.size,
             bytes_accessed=2 * by_row.size,

time: 174 us -> 174 us (level)
  no operation moved by 1% of the time
where the time goes in v8:
time: 174 us
  waiting for transfers between devices  66 us (38%)
  Pallas kernels  60.7 us (35%)
  starting transfers between devices  38.7 us (22%)
  local copies, waits for them, and re-layouts  6.79 us (4%)
    all_to_all x1, waiting for transfers between devices, local(): got = lax.all_to_all(propagator_part, 'row', 0, 0, tiled=True)  41.7 us
    pallas_call x1, Pallas kernels, chol_by_row(): pl.pallas_call(by_row_kernel, in_specs=[in_hbm], out_specs=in_hbm, out_sh...  22.8 us
    pallas_call x1, Pallas kernels, propagator_parts(): pl.pallas_call(propagator_kernel, in_specs=[pl.BlockSpec(memory_space=plt...  14 us
    pallas_call x1, Pallas kernels, bias_parts(): pl.pallas_call(bias_kernel, in_specs=[whole_vmem] * 3 + [in_hbm], out_spe...  13.7 us
    ppermute x4, waiting for transfers between devices, local(): moving_right = lax.ppermute(moving_right, 'row', right)  9.21 us
    ppermute x1, starting transfers between devices, local(): other_core = lax.ppermute(own_core, 'row', swap)  8.27 us
    ppermute x3, waiting for transfers between devices, local(): going_left = lax.ppermute(going_left, 'row', left)  6.97 us
    all_to_all x1, starting transfers between devices, local(): lax.all_to_all(payload(copies, jnp.transpose(walkers, (0, 2, 1)), inv_int...  6.57 us
  transfers between devices with their start and end apart: 22, of which 15 were waited for; matrix products, arithmetic and copies ran while one was open for 4% of the time, Pallas kernels for 22%

profile of v8, /device:TPU:15, one launch (start us, length us, event | category | flops | bytes accessed | tf_op | source)
XLA Modules:
  0.0 173.9 jit_solution(12860653183235190226)
XLA Ops:
  0.6 3.9 %shard_map.86 = bf16[16,17,16,128]{3,2,1,0:T(8,128)(2,1)} custom-call(s32[16]{0:T(128)} %copies.1, bf16[16,64,256]{2,1,0:T(8,128)(2,1)} %bitcast.134, bf16[16,64,64]{2,1,0:T(8,128)(2,1)} %from_inverse.1), custom_call_target="tpu_custom_call" | custom-call | flops 67108864 | bytes 1572864 | tf_op jit(solution)/shard_map/pallas_call | solution.py:322
  4.5 6.6 %all-to-all-start = ((bf16[16,17,16,128]{3,2,1,0:T(8,128)(2,1)}), bf16[16,17,16,128]{3,2,1,0:T(8,128)(2,1)S(1)}, u32[]{:S(2)}, u32[]{:S(2)}) async-start(bf16[16,17,16,128]{3,2,1,0:T(8,128)(2,1)} %shard_map.86), calls=%async_computation | async-start | bytes 2228224 | tf_op jit(solution)/shard_map/all_to_all | solution.py:428
  11.2 0.1 select_reduce_fusion.2
  11.3 22.8 %shard_map.87.chol = bf16[16,4096,256]{2,1,0:T(8,128)(2,1)} custom-call(bf16[4096,16,256]{2,1,0:T(8,128)(2,1)} %chol.1), custom_call_target="tpu_custom_call" | custom-call | flops 8589934592 | bytes 67108864 | tf_op jit(solution)/shard_map/pallas_call | solution.py:110
  34.0 3.4 %all-to-all-done.first = bf16[16,17,16,128]{3,2,1,0:T(8,128)(2,1)S(1)} async-done(((bf16[16,17,16,128]{3,2,1,0:T(8,128)(2,1)}), bf16[16,17,16,128]{3,2,1,0:T(8,128)(2,1)S(1)}, u32[]{:S(2)}, u32[]{:S(2)}) %all-to-all-start) | async-done | bytes 1114144 | tf_op jit(solution)/shard_map/all_to_all | solution.py:428
  37.5 0.1 convert_reduce_fusion
  37.6 0.1 reshape.139
  37.7 0.1 select_reduce_fusion.1
  37.8 0.1 and_convert_fusion
  37.9 13.7 %shard_map.88 = bf16[256,4096]{1,0:T(8,128)(2,1)S(1)} custom-call(bf16[256,256]{1,0:T(8,128)(2,1)S(1)} %get-tuple-element.15.pick, bf16[16,17,16,128]{3,2,1,0:T(8,128)(2,1)S(1)} %all-to-all-done.first, bf16[64,256]{1,0:T(8,128)(2,1)S(1)} %bitcast.132, bf16[16,4096,256]{2,1,0:T(8,128)(2,1)} %shard_map.87.chol), custom_call_target="tpu_custom_call" | custom-call | flops 8589934592 | bytes 33554432 | tf_op jit(solution)/shard_map/pallas_call | solution.py:160
  51.7 0.3 collective-permute-start.1
  52.0 0.4 collective-permute-start.7
  52.4 0.2 collective-permute-start
  52.6 0.7 collective-permute-done.1
  53.3 0.1 collective-permute-start.2
  53.4 1.5 collective-permute-start.6
  54.9 3.3 %collective-permute-done.2 = bf16[16,4096]{1,0:T(8,128)(2,1)S(1)} collective-permute-done((bf16[16,4096]{1,0:T(8,128)(2,1)S(1)}, bf16[16,4096]{1,0:T(8,128)(2,1)S(1)}, u32[]{:S(2)}, u32[]{:S(2)}) %collective-permute-start.2) | collective-permute-done | bytes 131104 | tf_op jit(solution)/shard_map/ppermute | solution.py:493
  58.3 0.0 collective-permute-done
  58.3 0.1 fusion.10
  58.3 0.0 copy-start
  58.3 0.4 collective-permute-start.3
  58.7 0.0 collective-permute-done.6
  58.7 0.1 fusion.3
  58.8 1.2 collective-permute-start.8
  60.0 2.2 %collective-permute-done.3 = bf16[16,4096]{1,0:T(8,128)(2,1)S(1)} collective-permute-done((bf16[16,4096]{1,0:T(8,128)(2,1)S(1)}, bf16[16,4096]{1,0:T(8,128)(2,1)S(1)}, u32[]{:S(2)}, u32[]{:S(2)}) %collective-permute-start.3) | collective-permute-done | bytes 131104 | tf_op jit(solution)/shard_map/ppermute | solution.py:493
  62.2 0.1 fusion.8
  62.3 0.9 collective-permute-start.4
  63.1 0.1 fusion.1
  63.2 0.8 collective-permute-start.9
  64.0 2.1 %collective-permute-done.4 = bf16[16,4096]{1,0:T(8,128)(2,1)S(1)} collective-permute-done((bf16[16,4096]{1,0:T(8,128)(2,1)S(1)}, bf16[16,4096]{1,0:T(8,128)(2,1)S(1)}, u32[]{:S(2)}, u32[]{:S(2)}) %collective-permute-start.4) | collective-permute-done | bytes 131104 | tf_op jit(solution)/shard_map/ppermute | solution.py:493
  66.1 0.1 fusion.6
  66.2 0.9 collective-permute-start.5
  67.1 1.6 shard_map.89.moved
  68.7 1.5 collective-permute-done.5.from_left
  70.2 0.8 shard_map.90
  70.9 0.2 collective-permute-start.11
  71.1 1.3 collective-permute-start.10
  72.4 2.3 %collective-permute-done.11 = bf16[16,4096]{1,0:T(8,128)(2,1)S(1)} collective-permute-done((bf16[16,4096]{1,0:T(8,128)(2,1)S(1)}, bf16[16,4096]{1,0:T(8,128)(2,1)S(1)}, u32[]{:S(2)}, u32[]{:S(2)}) %collective-permute-start.11) | collective-permute-done | bytes 131104 | tf_op jit(solution)/shard_map/ppermute | solution.py:510
  74.7 0.2 collective-permute-start.13
  75.0 0.4 collective-permute-done.10
  75.3 0.9 collective-permute-start.12
  76.3 2.3 %collective-permute-done.13 = bf16[16,4096]{1,0:T(8,128)(2,1)S(1)} collective-permute-done((bf16[16,4096]{1,0:T(8,128)(2,1)S(1)}, bf16[16,4096]{1,0:T(8,128)(2,1)S(1)}, u32[]{:S(2)}, u32[]{:S(2)}) %collective-permute-start.13) | collective-permute-done | bytes 131104 | tf_op jit(solution)/shard_map/ppermute | solution.py:510
  78.6 1.0 collective-permute-start.15
  79.6 0.4 collective-permute-done.12
  80.0 0.6 collective-permute-start.14
  80.6 2.3 %collective-permute-done.15 = bf16[16,4096]{1,0:T(8,128)(2,1)S(1)} collective-permute-done((bf16[16,4096]{1,0:T(8,128)(2,1)S(1)}, bf16[16,4096]{1,0:T(8,128)(2,1)S(1)}, u32[]{:S(2)}, u32[]{:S(2)}) %collective-permute-start.15) | collective-permute-done | bytes 131104 | tf_op jit(solution)/shard_map/ppermute | solution.py:510
  82.9 0.5 collective-permute-start.17
  83.4 0.7 collective-permute-done.14
  84.1 0.7 collective-permute-start.16
  84.8 1.5 collective-permute-done.17
  86.4 0.8 collective-permute-done.16
  87.2 8.3 %collective-permute-start.18 = (bf16[8,16,4096]{2,1,0:T(8,128)(2,1)S(1)}, bf16[8,16,4096]{2,1,0:T(8,128)(2,1)S(1)}, u32[]{:S(2)}, u32[]{:S(2)}) collective-permute-start(bf16[8,16,4096]{2,1,0:T(8,128)(2,1)S(1)} %fusion.12.own_core), channel_id=1, source_target_pairs={{0,1},{1,0},{4,5},{5,4},{8,9},{9,8},{12,13},{13,12},{14,15},{15,14... | collective-permute-start | bytes 3145736 | tf_op jit(solution)/shard_map/ppermute | solution.py:520
  95.5 0.1 stack.62
  95.6 6.0 %all-to-all-start.2 = ((bf16[16,8,16,128]{3,2,1,0:T(8,128)(2,1)}), bf16[16,8,16,128]{3,2,1,0:T(8,128)(2,1)S(1)}, u32[]{:S(2)}, u32[]{:S(2)}) async-start(bf16[16,8,16,128]{3,2,1,0:T(8,128)(2,1)} %shard_map.89.moved), calls=%async_computation.2 | async-start | bytes 1048576 | tf_op jit(solution)/shard_map/all_to_all | solution.py:461
  101.6 0.1 pad_add_fusion.spots
  101.7 14.0 %shard_map.91 = bf16[16,16,16,256]{3,2,1,0:T(8,128)(2,1)} custom-call(s32[16]{0:T(128)S(1)} %pad_add_fusion.spots, bf16[8,16,4096]{2,1,0:T(8,128)(2,1)S(1)} %fusion.12.own_core, bf16[8,16,4096]{2,1,0:T(8,128)(2,1)S(1)} %collective-permute-done.18.other_core, bf16[16,4096,256]{2,1,0:T(8,128)(2,1)} %shard_map.87.chol), custom_call_target="tpu_custom_call" | custom-call | flops 8589934592 | bytes 33554432 | tf_op jit(solution)/shard_map/pallas_call | solution.py:221
  115.7 0.0 copy-start.2
  115.7 0.8 copy-done.2
  116.5 6.0 %all-to-all-start.1 = ((bf16[16,16,16,256]{3,2,1,0:T(8,128)(2,1)}), bf16[16,16,16,256]{3,2,1,0:T(8,128)(2,1)S(1)}, u32[]{:S(2)}, u32[]{:S(2)}) async-start(bf16[16,16,16,256]{3,2,1,0:T(8,128)(2,1)} %shard_map.91), calls=%async_computation.1 | async-start | bytes 4194304 | tf_op jit(solution)/shard_map/all_to_all | solution.py:524
  122.5 2.4 %reshape.137 = bf16[16,8,16,2,64]{4,3,2,1,0:T(2,128)(2,1)S(1)} reshape(bf16[16,8,16,128]{3,2,1,0:T(8,128)(2,1)} %copy-done.2) | data formatting | bytes 1048576 | tf_op jit(solution)/shard_map/reshape | solution.py:463
  125.0 1.3 copy.12
  126.2 2.0 %copy.13.orbitals = bf16[16,64,256]{2,1,0:T(8,128)(2,1)S(1)} copy(bf16[16,64,256]{1,0,2:T(8,128)(2,1)} %bitcast.133) | data formatting | bytes 1048576 | tf_op jit(solution)/shard_map/reshape | solution.py:464
  128.2 41.7 %all-to-all-done.1.got = bf16[16,16,16,256]{3,2,1,0:T(8,128)(2,1)S(1)} async-done(((bf16[16,16,16,256]{3,2,1,0:T(8,128)(2,1)}), bf16[16,16,16,256]{3,2,1,0:T(8,128)(2,1)S(1)}, u32[]{:S(2)}, u32[]{:S(2)}) %all-to-all-start.1) | async-done | bytes 2097184 | tf_op jit(solution)/shard_map/all_to_all | solution.py:524
  169.9 4.0 %shard_map.92 = bf16[16,64,256]{2,1,0:T(8,128)(2,1)} custom-call(bf16[16,16,16,256]{3,2,1,0:T(8,128)(2,1)S(1)} %all-to-all-done.1.got, bf16[16,64,256]{2,1,0:T(8,128)(2,1)S(1)} %copy.13.orbitals), custom_call_target="tpu_custom_call" | custom-call | flops 536870912 | bytes 4194304 | tf_op jit(solution)/shard_map/pallas_call | solution.py:379
  (28 shorter events, 0.3 us)
Async XLA Ops:
  0.6 10.5 %copy-start.3 = (s32[16]{0:T(128)S(1)}, s32[16]{0:T(128)}, u32[]{:S(2)}) copy-start(s32[16]{0:T(128)} %param.10) | copy-start | bytes 196
  4.5 32.9 %all-to-all-start = ((bf16[16,17,16,128]{3,2,1,0:T(8,128)(2,1)}), bf16[16,17,16,128]{3,2,1,0:T(8,128)(2,1)S(1)}, u32[]{:S(2)}, u32[]{:S(2)}) async-start(bf16[16,17,16,128]{3,2,1,0:T(8,128)(2,1)} %shard_map.86), calls=%async_computation | async-start | bytes 2228224 | tf_op jit(solution)/shard_map/all_to_all | solution.py:428
  11.2 26.7 %copy-start.1 = (bf16[256,64]{0,1:T(8,128)(2,1)S(1)}, bf16[256,64]{0,1:T(8,128)(2,1)}, u32[]{:S(2)}) copy-start(bf16[256,64]{0,1:T(8,128)(2,1)} %param.11) | copy-start | bytes 98308
  51.7 1.6 collective-permute-start.1
  52.0 6.7 %collective-permute-start.7 = (bf16[2,16,4096]{2,1,0:T(8,128)(2,1)S(1)}, bf16[2,16,4096]{2,1,0:T(8,128)(2,1)S(1)}, u32[]{:S(2)}, u32[]{:S(2)}) collective-permute-start(bf16[2,16,4096]{2,1,0:T(8,128)(2,1)S(1)} %get-tuple-element.12), channel_id=1, source_target_pairs={{0,1},{1,0},{4,5},{5,4},{8,9},{9,8},{12,13},{13,12},{14,15},{15,14... | collective-permute-start | bytes 786440 | tf_op jit(solution)/shard_map/ppermute | solution.py:474
  52.4 5.9 %collective-permute-start = (bf16[4,16,4096]{2,1,0:T(8,128)(2,1)S(1)}, bf16[4,16,4096]{2,1,0:T(8,128)(2,1)S(1)}, u32[]{:S(2)}, u32[]{:S(2)}) collective-permute-start(bf16[4,16,4096]{2,1,0:T(8,128)(2,1)S(1)} %slice_bitcast_fusion), channel_id=1, source_target_pairs={{0,1},{1,0},{4,5},{5,4},{8,9},{9,8},{12,13},{13,12},{14,15},{15,14... | collective-permute-start | bytes 1572872 | tf_op jit(solution)/shard_map/ppermute | solution.py:474
  53.3 4.9 %collective-permute-start.2 = (bf16[16,4096]{1,0:T(8,128)(2,1)S(1)}, bf16[16,4096]{1,0:T(8,128)(2,1)S(1)}, u32[]{:S(2)}, u32[]{:S(2)}) collective-permute-start(bf16[16,4096]{1,0:T(8,128)(2,1)S(1)} %fusion.11), channel_id=1, source_target_pairs={{0,4},{1,5},{4,8},{5,9},{8,12},{9,13},{12,14},{13,15},{14,10},{15,... | collective-permute-start | bytes 393224 | tf_op jit(solution)/shard_map/ppermute | solution.py:493
  53.4 5.3 %collective-permute-start.6 = (bf16[2,8,4096]{2,1,0:T(8,128)(2,1)S(1)}, bf16[2,8,4096]{2,1,0:T(8,128)(2,1)S(1)}, u32[]{:S(2)}, u32[]{:S(2)}) collective-permute-start(bf16[2,8,4096]{2,1,0:T(8,128)(2,1)S(1)} %fusion.4), channel_id=1, source_target_pairs={{0,2},{1,3},{4,0},{5,1},{8,4},{9,5},{12,8},{13,9},{14,12},{15,13},... | collective-permute-start | bytes 393224 | tf_op jit(solution)/shard_map/ppermute | solution.py:495
  58.3 11.9 %copy-start = (f32[16,4096]{1,0:T(8,128)S(1)}, f32[16,4096]{1,0:T(8,128)}, u32[]{:S(2)}) copy-start(f32[16,4096]{1,0:T(8,128)} %noise.1) | copy-start | bytes 786436
  58.3 3.9 %collective-permute-start.3 = (bf16[16,4096]{1,0:T(8,128)(2,1)S(1)}, bf16[16,4096]{1,0:T(8,128)(2,1)S(1)}, u32[]{:S(2)}, u32[]{:S(2)}) collective-permute-start(bf16[16,4096]{1,0:T(8,128)(2,1)S(1)} %fusion.10), channel_id=1, source_target_pairs={{0,4},{1,5},{4,8},{5,9},{8,12},{9,13},{12,14},{13,15},{14,10},{15,... | collective-permute-start | bytes 393224 | tf_op jit(solution)/shard_map/ppermute | solution.py:493
  58.8 4.4 %collective-permute-start.8 = (bf16[2,8,4096]{2,1,0:T(8,128)(2,1)S(1)}, bf16[2,8,4096]{2,1,0:T(8,128)(2,1)S(1)}, u32[]{:S(2)}, u32[]{:S(2)}) collective-permute-start(bf16[2,8,4096]{2,1,0:T(8,128)(2,1)S(1)} %fusion.3), channel_id=1, source_target_pairs={{0,2},{1,3},{4,0},{5,1},{8,4},{9,5},{12,8},{13,9},{14,12},{15,13},... | collective-permute-start | bytes 393224 | tf_op jit(solution)/shard_map/ppermute | solution.py:495
  62.3 3.9 %collective-permute-start.4 = (bf16[16,4096]{1,0:T(8,128)(2,1)S(1)}, bf16[16,4096]{1,0:T(8,128)(2,1)S(1)}, u32[]{:S(2)}, u32[]{:S(2)}) collective-permute-start(bf16[16,4096]{1,0:T(8,128)(2,1)S(1)} %fusion.8), channel_id=1, source_target_pairs={{0,4},{1,5},{4,8},{5,9},{8,12},{9,13},{12,14},{13,15},{14,10},{15,... | collective-permute-start | bytes 393224 | tf_op jit(solution)/shard_map/ppermute | solution.py:493
  63.2 5.5 %collective-permute-start.9 = (bf16[2,8,4096]{2,1,0:T(8,128)(2,1)S(1)}, bf16[2,8,4096]{2,1,0:T(8,128)(2,1)S(1)}, u32[]{:S(2)}, u32[]{:S(2)}) collective-permute-start(bf16[2,8,4096]{2,1,0:T(8,128)(2,1)S(1)} %fusion.1), channel_id=1, source_target_pairs={{0,2},{1,3},{4,0},{5,1},{8,4},{9,5},{12,8},{13,9},{14,12},{15,13},... | collective-permute-start | bytes 393224 | tf_op jit(solution)/shard_map/ppermute | solution.py:495
  66.2 4.0 %collective-permute-start.5 = (bf16[16,4096]{1,0:T(8,128)(2,1)S(1)}, bf16[16,4096]{1,0:T(8,128)(2,1)S(1)}, u32[]{:S(2)}, u32[]{:S(2)}) collective-permute-start(bf16[16,4096]{1,0:T(8,128)(2,1)S(1)} %get-tuple-element.10), channel_id=1, source_target_pairs={{0,4},{1,5},{4,8},{5,9},{8,12},{9,13},{12,14},{13,15},{14,10},{15,... | collective-permute-start | bytes 393224 | tf_op jit(solution)/shard_map/ppermute | solution.py:493
  70.9 3.8 %collective-permute-start.11 = (bf16[16,4096]{1,0:T(8,128)(2,1)S(1)}, bf16[16,4096]{1,0:T(8,128)(2,1)S(1)}, u32[]{:S(2)}, u32[]{:S(2)}) collective-permute-start(bf16[16,4096]{1,0:T(8,128)(2,1)S(1)} %get-tuple-element.4), channel_id=1, source_target_pairs={{0,2},{1,3},{4,0},{5,1},{8,4},{9,5},{12,8},{13,9},{14,12},{15,13},... | collective-permute-start | bytes 393224 | tf_op jit(solution)/shard_map/ppermute | solution.py:510
  71.1 4.2 %collective-permute-start.10 = (bf16[16,4096]{1,0:T(8,128)(2,1)S(1)}, bf16[16,4096]{1,0:T(8,128)(2,1)S(1)}, u32[]{:S(2)}, u32[]{:S(2)}) collective-permute-start(bf16[16,4096]{1,0:T(8,128)(2,1)S(1)} %get-tuple-element.4), channel_id=1, source_target_pairs={{0,4},{1,5},{4,8},{5,9},{8,12},{9,13},{12,14},{13,15},{14,10},{15,... | collective-permute-start | bytes 393224 | tf_op jit(solution)/shard_map/ppermute | solution.py:509
  74.7 3.8 %collective-permute-start.13 = (bf16[16,4096]{1,0:T(8,128)(2,1)S(1)}, bf16[16,4096]{1,0:T(8,128)(2,1)S(1)}, u32[]{:S(2)}, u32[]{:S(2)}) collective-permute-start(bf16[16,4096]{1,0:T(8,128)(2,1)S(1)} %collective-permute-done.11), channel_id=1, source_target_pairs={{0,2},{1,3},{4,0},{5,1},{8,4},{9,5},{12,8},{13,9},{14,12},{15,13},... | collective-permute-start | bytes 393224 | tf_op jit(solution)/shard_map/ppermute | solution.py:510
  75.3 4.7 %collective-permute-start.12 = (bf16[16,4096]{1,0:T(8,128)(2,1)S(1)}, bf16[16,4096]{1,0:T(8,128)(2,1)S(1)}, u32[]{:S(2)}, u32[]{:S(2)}) collective-permute-start(bf16[16,4096]{1,0:T(8,128)(2,1)S(1)} %collective-permute-done.10), channel_id=1, source_target_pairs={{0,4},{1,5},{4,8},{5,9},{8,12},{9,13},{12,14},{13,15},{14,10},{15,... | collective-permute-start | bytes 393224 | tf_op jit(solution)/shard_map/ppermute | solution.py:509
  78.6 4.3 %collective-permute-start.15 = (bf16[16,4096]{1,0:T(8,128)(2,1)S(1)}, bf16[16,4096]{1,0:T(8,128)(2,1)S(1)}, u32[]{:S(2)}, u32[]{:S(2)}) collective-permute-start(bf16[16,4096]{1,0:T(8,128)(2,1)S(1)} %collective-permute-done.13), channel_id=1, source_target_pairs={{0,2},{1,3},{4,0},{5,1},{8,4},{9,5},{12,8},{13,9},{14,12},{15,13},... | collective-permute-start | bytes 393224 | tf_op jit(solution)/shard_map/ppermute | solution.py:510
  80.0 4.1 %collective-permute-start.14 = (bf16[16,4096]{1,0:T(8,128)(2,1)S(1)}, bf16[16,4096]{1,0:T(8,128)(2,1)S(1)}, u32[]{:S(2)}, u32[]{:S(2)}) collective-permute-start(bf16[16,4096]{1,0:T(8,128)(2,1)S(1)} %collective-permute-done.12), channel_id=1, source_target_pairs={{0,4},{1,5},{4,8},{5,9},{8,12},{9,13},{12,14},{13,15},{14,10},{15,... | collective-permute-start | bytes 393224 | tf_op jit(solution)/shard_map/ppermute | solution.py:509
  82.9 3.5 %collective-permute-start.17 = (bf16[8,4096]{1,0:T(8,128)(2,1)S(1)}, bf16[8,4096]{1,0:T(8,128)(2,1)S(1)}, u32[]{:S(2)}, u32[]{:S(2)}) collective-permute-start(bf16[8,4096]{1,0:T(8,128)(2,1)S(1)} %slice.109), channel_id=1, source_target_pairs={{0,2},{1,3},{4,0},{5,1},{8,4},{9,5},{12,8},{13,9},{14,12},{15,13},... | collective-permute-start | bytes 196616 | tf_op jit(solution)/shard_map/ppermute | solution.py:516
  84.1 3.1 %collective-permute-start.16 = (bf16[8,4096]{1,0:T(8,128)(2,1)S(1)}, bf16[8,4096]{1,0:T(8,128)(2,1)S(1)}, u32[]{:S(2)}, u32[]{:S(2)}) collective-permute-start(bf16[8,4096]{1,0:T(8,128)(2,1)S(1)} %slice.108), channel_id=1, source_target_pairs={{0,4},{1,5},{4,8},{5,9},{8,12},{9,13},{12,14},{13,15},{14,10},{15,... | collective-permute-start | bytes 196616 | tf_op jit(solution)/shard_map/ppermute | solution.py:515
  87.2 14.4 %collective-permute-start.18 = (bf16[8,16,4096]{2,1,0:T(8,128)(2,1)S(1)}, bf16[8,16,4096]{2,1,0:T(8,128)(2,1)S(1)}, u32[]{:S(2)}, u32[]{:S(2)}) collective-permute-start(bf16[8,16,4096]{2,1,0:T(8,128)(2,1)S(1)} %fusion.12.own_core), channel_id=1, source_target_pairs={{0,1},{1,0},{4,5},{5,4},{8,9},{9,8},{12,13},{13,12},{14,15},{15,14... | collective-permute-start | bytes 3145736 | tf_op jit(solution)/shard_map/ppermute | solution.py:520
  95.6 20.1 %all-to-all-start.2 = ((bf16[16,8,16,128]{3,2,1,0:T(8,128)(2,1)}), bf16[16,8,16,128]{3,2,1,0:T(8,128)(2,1)S(1)}, u32[]{:S(2)}, u32[]{:S(2)}) async-start(bf16[16,8,16,128]{3,2,1,0:T(8,128)(2,1)} %shard_map.89.moved), calls=%async_computation.2 | async-start | bytes 1048576 | tf_op jit(solution)/shard_map/all_to_all | solution.py:461
  115.7 0.8 copy-start.2
  116.5 53.4 %all-to-all-start.1 = ((bf16[16,16,16,256]{3,2,1,0:T(8,128)(2,1)}), bf16[16,16,16,256]{3,2,1,0:T(8,128)(2,1)S(1)}, u32[]{:S(2)}, u32[]{:S(2)}) async-start(bf16[16,16,16,256]{3,2,1,0:T(8,128)(2,1)} %shard_map.91), calls=%async_computation.1 | async-start | bytes 4194304 | tf_op jit(solution)/shard_map/all_to_all | solution.py:524
